TPU v7x, 32 devices: a whole 2x2x4 slice. The times are simulated.
32 devices in a mesh: groups: 2 (over y), tp: 16 (over z, x, core).
Axes of the slice: x: 2, y: 2, z: 4, core: 2. Of those that a mesh axis runs over, the one named last changes fastest.
Arguments:
- stream: bfloat16 [128, 8192], P('groups', 'tp'), parts along dimension 0, may hold values from -6 to 6
- table_rows: bfloat16 [1024, 8192], P('groups', 'tp'), parts along dimension 0, may hold values from -6 to 6
- token_ids: int32 [1, 128], P(None, 'groups'), parts along dimension 1, may hold values from 0 to 511
- norm_gain: float32 [8192], replicated, may hold values from 0.1 to 1.9
- gate_weight: bfloat16 [16, 1024, 13312], P('tp'), may hold values from -0.0625 to 0.0625
- up_weight: bfloat16 [16, 1024, 13312], P('tp'), may hold values from -0.0625 to 0.0625
- down_weight: bfloat16 [16, 13312, 1024], P('tp'), may hold values from -0.0546875 to 0.0546875
Outputs:
- states: bfloat16 [1, 128, 8192], P(None, 'groups', 'tp'), parts along dimension 1
There are 2 independent parts, one for each index of `groups`. A program takes and returns all parts, laid end to end along the dimension named above; an argument that names none is the same for every part. Nothing has to cross between parts.
All inputs are finite; a program needn't handle non-finite values.
Results may differ from a plain program's by a relative error of at most 0.006.
Values may be sent and summed in bfloat16 or wider, within the bound.
No kernel may reach another device: no remote copies, remote signals or barrier semaphores. Data moves between devices by JAX's collectives and lax.ppermute only.
A program may use at most 256 MiB of HBM per device.

v0:
```python
import jax
import jax.numpy as jnp
from jax import lax
from jax.sharding import PartitionSpec as P

D = 8192
D_WAYS = 8


def from_partner(value, axis, distance):
    mask = 2**distance
    pairs = [(source, source ^ mask) for source in range(lax.axis_size(axis))]
    return lax.ppermute(value, axis, pairs)


def bit_high(index, bit):
    return index // 2**bit % 2 == 1


def gather_block(local_rows, index, low_bits):
    piece = local_rows
    for bit in range(low_bits):
        other = from_partner(piece, "tp", bit)
        piece = jnp.where(
            bit_high(index, bit),
            jnp.concatenate([other, piece], 1),
            jnp.concatenate([piece, other], 1),
        )
    return piece


def squares_total(block_f32, low_bits, high_bits):
    total = jnp.sum(block_f32 * block_f32, axis=1)
    for level in range(high_bits):
        total = total + from_partner(total, "tp", low_bits + level)
    return total


def halve_columns(values, index, bit):
    width = values.shape[-1] // 2
    lower = values[..., :width]
    upper = values[..., width:]
    high = bit_high(index, bit)
    return (jnp.where(high, upper, lower), jnp.where(high, lower, upper))


def sum_units(pair, low_bits, high_bits):
    for level in range(high_bits):
        pair = pair + from_partner(pair, "tp", low_bits + level)
    return (jax.nn.silu(pair[0]) * pair[1]).astype(jnp.bfloat16)


def sum_blocks(partial_value, index, low_bits):
    for bit in reversed(range(low_bits)):
        kept, sent = halve_columns(partial_value, index, bit)
        partial_value = kept + from_partner(sent.astype(jnp.bfloat16), "tp", bit).astype(sent.dtype)
    return partial_value


def on_device(stream, table_rows, token_ids, norm_gain, gate_weight, up_weight, down_weight):
    f_ways = lax.axis_size("tp") // D_WAYS
    low_bits = f_ways.bit_length() - 1
    high_bits = D_WAYS.bit_length() - 1
    index = lax.axis_index("tp")
    block_pos = index // f_ways
    width = gate_weight.shape[1]
    gain_block = lax.dynamic_slice_in_dim(norm_gain, block_pos * width, width)
    gate_tile = gate_weight[0]
    up_tile = up_weight[0]
    down_tile = down_weight[0]
    current = stream
    picked = jnp.take(table_rows, token_ids[0], axis=0)
    block_in = (current.astype(jnp.float32) + picked.astype(jnp.float32)).astype(jnp.bfloat16)
    feature_block = gather_block(block_in, index, low_bits).astype(jnp.float32)
    total = squares_total(feature_block, low_bits, high_bits)
    scale_rows = lax.rsqrt(total[:, None] / D + 1e-05)
    normed = (feature_block * scale_rows * gain_block[None, :]).astype(jnp.bfloat16)
    pair = jnp.stack(
        [
            jnp.dot(normed, gate_tile, preferred_element_type=jnp.float32),
            jnp.dot(normed, up_tile, preferred_element_type=jnp.float32),
        ],
        axis=0,
    )
    hidden = sum_units(pair, low_bits, high_bits)
    partial_value = jnp.dot(hidden, down_tile, preferred_element_type=jnp.float32)
    summed = sum_blocks(partial_value, index, low_bits)
    current = (block_in.astype(jnp.float32) + summed).astype(jnp.bfloat16)
    results = [current]
    return jnp.stack(results, axis=0)


def solution(mesh):
    placed = (
        P("groups", "tp"),
        P("groups", "tp"),
        P(None, "groups"),
        P(),
        P("tp", None, None),
        P("tp", None, None),
        P("tp", None, None),
    )
    return jax.shard_map(
        on_device, mesh=mesh, in_specs=placed, out_specs=P(None, "groups", "tp"), check_vma=False
    )
```

profile of v0, /device:TPU:0, one launch (start us, length us, event | category | flops | bytes accessed | tf_op | source)
XLA Modules:
  0.0 658.4 jit_solution(9652190292628491218)
XLA Ops:
  0.0 0.7 fusion.21
  1.4 0.7 gather_fusion
  2.1 0.9 add_convert_fusion.1
  3.6 0.9 collective-permute-done
  4.6 2.9 collective-permute-start.1
  7.5 1.5 collective-permute-done.1
  9.0 2.1 collective-permute-start.2
  11.1 1.5 collective-permute-done.2
  12.6 3.0 collective-permute-start.3
  16.4 0.8 collective-permute-done.3
  17.2 11.3 %fusion.9 = f32[1,64,13312]{2,1,0:T(8,128)S(1)} fusion(bf16[1,1024,13312]{2,1,0:T(8,128)(2,1)} %param.12, f32[1024]{0:T(1024)S(1)} %dynamic_slice.3, f32[64]{0:T(128)S(1)} %add_rsqrt_fusion, bf16[64,512]{1,0:T(8,128)(2,1)S(1)} %add_convert_fusion.1, bf16[64,512]{1,0:T(8,128)(2,1)S(1)} %collective-permute-done, pred[]{:T(512)S(6)} %eq.7), kind=kOutput, calls=%fused_computation.8 | convolution fusion | flops 1745682432 | bytes 30806272 | tf_op jit(solution)/shard_map/dot_general | solution.py:81
  28.5 11.3 %fusion.6 = f32[1,64,13312]{2,1,0:T(8,128)S(1)} fusion(bf16[1,1024,13312]{2,1,0:T(8,128)(2,1)} %param.11, f32[1024]{0:T(1024)S(1)} %dynamic_slice.3, f32[64]{0:T(128)S(1)} %add_rsqrt_fusion, bf16[64,512]{1,0:T(8,128)(2,1)S(1)} %add_convert_fusion.1, bf16[64,512]{1,0:T(8,128)(2,1)S(1)} %collective-permute-done, pred[]{:T(512)S(6)} %eq.7), kind=kOutput, calls=%fused_computation.7 | convolution fusion | flops 1745682432 | bytes 30806272 | tf_op jit(solution)/shard_map/dot_general | solution.py:80
  40.5 1.9 collective-permute-start.4
  42.4 143.8 %collective-permute-done.4 = f32[2,64,13312]{2,1,0:T(8,128)S(1)} collective-permute-done((f32[2,64,13312]{2,1,0:T(8,128)S(1)}, f32[2,64,13312]{2,1,0:T(8,128)S(1)}, u32[]{:S(2)}, u32[]{:S(2)}) %collective-permute-start.4) | collective-permute-done | bytes 6815776 | tf_op jit(solution)/shard_map/ppermute | solution.py:13
  186.2 4.1 fusion.23
  190.3 0.7 copy-done.3
  191.0 1.6 collective-permute-start.5
  192.7 143.4 %collective-permute-done.5 = f32[2,64,13312]{2,1,0:T(8,128)} collective-permute-done((f32[2,64,13312]{2,1,0:T(8,128)}, f32[2,64,13312]{2,1,0:T(8,128)}, u32[]{:S(2)}, u32[]{:S(2)}) %collective-permute-start.5) | collective-permute-done | bytes 6815776 | tf_op jit(solution)/shard_map/ppermute | solution.py:13
  336.1 9.6 %fusion.24 = f32[2,64,13312]{2,1,0:T(8,128)} fusion(f32[2,64,13312]{2,1,0:T(8,128)} %collective-permute-done.5, f32[2,64,13312]{2,1,0:T(8,128)} %copy-done.3, f32[1,64,13312]{2,1,0:T(8,128)S(1)} %fusion.9, f32[1,64,13312]{2,1,0:T(8,128)} %copy-done.2), kind=kLoop, calls=%fused_computation.31 | loop fusion | flops 5111808 | bytes 27262976 | tf_op jit(solution)/shard_map/add | solution.py:49
  345.6 2.4 collective-permute-start.6
  348.0 288.6 %collective-permute-done.6 = f32[2,64,13312]{2,1,0:T(8,128)S(1)} collective-permute-done((f32[2,64,13312]{2,1,0:T(8,128)}, f32[2,64,13312]{2,1,0:T(8,128)S(1)}, u32[]{:S(2)}, u32[]{:S(2)}) %collective-permute-start.6) | collective-permute-done | bytes 6815776 | tf_op jit(solution)/shard_map/ppermute | solution.py:13
  636.6 6.7 %add.84 = f32[2,64,13312]{2,1,0:T(8,128)} add(f32[2,64,13312]{2,1,0:T(8,128)} %fusion.24, f32[2,64,13312]{2,1,0:T(8,128)S(1)} %collective-permute-done.6) | non-fusion elementwise | flops 1703936 | bytes 20447232 | tf_op jit(solution)/shard_map/add | solution.py:49
  643.3 13.0 %fusion = f32[64,1024]{1,0:T(8,128)S(1)} fusion(bf16[1,13312,1024]{2,1,0:T(8,128)(2,1)} %param.13, f32[2,64,13312]{2,1,0:T(8,128)} %add.84), kind=kOutput, calls=%fused_computation.1 | convolution fusion | flops 1749942272 | bytes 34340864 | tf_op jit(solution)/shard_map/dot_general | solution.py:86
  656.5 1.2 collective-permute-done.7
  (19 shorter events, 3.4 us)
Async XLA Ops:
  0.0 1.4 copy-start
  3.0 1.4 collective-permute-start
  4.6 4.4 collective-permute-start.1
  9.0 3.6 collective-permute-start.2
  12.6 4.6 collective-permute-start.3
  39.9 146.3 %copy-start.2 = (f32[1,64,13312]{2,1,0:T(8,128)}, f32[1,64,13312]{2,1,0:T(8,128)S(1)}, u32[]{:S(2)}) copy-start(f32[1,64,13312]{2,1,0:T(8,128)S(1)} %fusion.6) | copy-start | bytes 10223620
  40.5 145.7 %collective-permute-start.4 = (f32[2,64,13312]{2,1,0:T(8,128)S(1)}, f32[2,64,13312]{2,1,0:T(8,128)S(1)}, u32[]{:S(2)}, u32[]{:S(2)}) collective-permute-start(f32[2,64,13312]{2,1,0:T(8,128)S(1)} %pad_maximum_fusion), channel_id=1, source_target_pairs={{0,2},{1,3},{2,0},{3,1},{4,6},{5,7},{6,4},{7,5},{8,10},{9,11},{10,... | collective-permute-start | bytes 20447240 | tf_op jit(solution)/shard_map/ppermute | solution.py:13
  186.2 4.8 copy-start.3
  191.0 145.0 %collective-permute-start.5 = (f32[2,64,13312]{2,1,0:T(8,128)}, f32[2,64,13312]{2,1,0:T(8,128)}, u32[]{:S(2)}, u32[]{:S(2)}) collective-permute-start(f32[2,64,13312]{2,1,0:T(8,128)} %fusion.23), channel_id=1, source_target_pairs={{0,4},{1,5},{2,6},{3,7},{4,0},{5,1},{6,2},{7,3},{8,12},{9,13},{10,... | collective-permute-start | bytes 20447240 | tf_op jit(solution)/shard_map/ppermute | solution.py:13
  345.6 291.0 %collective-permute-start.6 = (f32[2,64,13312]{2,1,0:T(8,128)}, f32[2,64,13312]{2,1,0:T(8,128)S(1)}, u32[]{:S(2)}, u32[]{:S(2)}) collective-permute-start(f32[2,64,13312]{2,1,0:T(8,128)} %fusion.24), channel_id=1, source_target_pairs={{0,8},{1,9},{2,10},{3,11},{4,12},{5,13},{6,14},{7,15},{8,0},{9,1},... | collective-permute-start | bytes 20447240 | tf_op jit(solution)/shard_map/ppermute | solution.py:13
  643.3 15.1 %copy-start.1 = (bf16[512,512]{1,0:T(8,128)(2,1)S(1)}, bf16[512,512]{1,0:T(8,128)(2,1)}, u32[]{:S(2)}) copy-start(bf16[512,512]{1,0:T(8,128)(2,1)} %param.8) | copy-start | bytes 1572868
  656.4 1.3 collective-permute-start.7
where the time goes:
time: 659 us; the launch traced here: 658 us
  waiting for transfers between devices  582 us (88%)
  matrix products  35.7 us (5%)
  other arithmetic  24.1 us (4%)
  starting transfers between devices  14.5 us (2%)
    ppermute x8, waiting for transfers between devices, from_partner(): return lax.ppermute(value, axis, pairs)  582 us
    add x3, other arithmetic, sum_units(): pair = pair + from_partner(pair, 'tp', low_bits + level)  20.4 us
    ppermute x8, starting transfers between devices, from_partner(): return lax.ppermute(value, axis, pairs)  14.5 us
  transfers between devices with their start and end apart: 8, of which 8 were waited for; matrix products, arithmetic and copies ran while one was open for 0% of the time, Pallas kernels for 0%

commit v1 on v0

v1 whole, which is shorter than its diff:
```python
import jax
import jax.numpy as jnp
from jax import lax
from jax.experimental import pallas as pl
from jax.experimental.pallas import tpu as pltpu
from jax.sharding import PartitionSpec as P

D = 8192
D_WAYS = 8
LANES = 128
VMEM_LIMIT = 40 * 2**20


def ring_order(f_ways):
    if f_ways == 2:
        return [0, 2, 4, 6, 7, 5, 3, 1]
    return list(range(D_WAYS))


def from_partner(value, axis, distance):
    mask = 2**distance
    pairs = [(source, source ^ mask) for source in range(lax.axis_size(axis))]
    return lax.ppermute(value, axis, pairs)


def bit_high(index, bit):
    return index // 2**bit % 2 == 1


def gather_block(local_rows, index, low_bits):
    piece = local_rows
    for bit in range(low_bits):
        other = from_partner(piece, "tp", bit)
        piece = jnp.where(
            bit_high(index, bit),
            jnp.concatenate([other, piece], 1),
            jnp.concatenate([piece, other], 1),
        )
    return piece


def halve_columns(values, index, bit):
    width = values.shape[-1] // 2
    lower = values[..., :width]
    upper = values[..., width:]
    high = bit_high(index, bit)
    return (jnp.where(high, upper, lower), jnp.where(high, lower, upper))


def sum_blocks(partial_value, index, low_bits):
    for bit in reversed(range(low_bits)):
        kept, sent = halve_columns(partial_value, index, bit)
        partial_value = kept + from_partner(sent.astype(jnp.bfloat16), "tp", bit).astype(sent.dtype)
    return partial_value


def up_blocks(x, gate_tile, up_tile, blocks, after):
    depth, units = gate_tile.shape
    width = units // D_WAYS
    rows = x.shape[0]
    count = len(blocks)
    if width % LANES:
        tiles = [
            lax.dynamic_slice_in_dim(tile, block * width, width, 1)
            for block in blocks
            for tile in (gate_tile, up_tile)
        ]
        parts = [jnp.dot(x, tile, preferred_element_type=jnp.float32) for tile in tiles]
        return jnp.stack(parts).reshape(count, 2, rows, width)
    cuts = 2
    cut = depth // cuts

    def kernel(ids, x_ref, gate_ref, up_ref, *rest):
        out_ref, tiles, arrived = rest[-3:]
        copies = []
        for j in range(count):
            columns = pl.ds(pl.multiple_of(ids[j] * width, LANES), width)
            for m, tile_ref in enumerate((gate_ref, up_ref)):
                for c in range(cuts):
                    copy = pltpu.make_async_copy(
                        tile_ref.at[pl.ds(c * cut, cut), columns],
                        tiles.at[2 * j + m, pl.ds(c * cut, cut), :],
                        arrived.at[2 * j + m, c],
                    )
                    copy.start()
                    copies.append((j, m, c, copy))
        for j, m, c, copy in copies:
            copy.wait()
            product = jnp.dot(
                x_ref[:, c * cut : (c + 1) * cut],
                tiles[2 * j + m, c * cut : (c + 1) * cut, :],
                preferred_element_type=jnp.float32,
            )
            if c == 0:
                out_ref[j, m] = product
            else:
                out_ref[j, m] += product

    return pl.pallas_call(
        kernel,
        out_shape=jax.ShapeDtypeStruct((count, 2, rows, width), jnp.float32),
        grid_spec=pltpu.PrefetchScalarGridSpec(
            num_scalar_prefetch=1,
            grid=(),
            in_specs=[pl.BlockSpec(memory_space=pltpu.VMEM)]
            + [pl.BlockSpec(memory_space=pl.ANY)] * (2 + len(after)),
            out_specs=pl.BlockSpec(memory_space=pltpu.VMEM),
            scratch_shapes=[
                pltpu.VMEM((2 * count, depth, width), jnp.bfloat16),
                pltpu.SemaphoreType.DMA((2 * count, cuts)),
            ],
        ),
        compiler_params=pltpu.CompilerParams(vmem_limit_bytes=VMEM_LIMIT),
        cost_estimate=pl.CostEstimate(
            flops=4 * count * rows * depth * width,
            bytes_accessed=4 * count * depth * width,
            transcendentals=0,
        ),
        name="up_blocks",
    )(jnp.stack(blocks), x, gate_tile, up_tile, *after)


def down_blocks(total, hidden, down_tile, blocks, after):
    units, width = down_tile.shape
    depth = units // D_WAYS
    rows = total.shape[0]
    count = len(blocks)
    if depth % LANES:
        for block, value in zip(blocks, hidden):
            tile = lax.dynamic_slice_in_dim(down_tile, block * depth, depth, 0)
            total = total + jnp.dot(value, tile, preferred_element_type=jnp.float32)
        return total
    cuts = depth // LANES
    cut = LANES

    def kernel(ids, total_ref, *rest):
        hidden_refs = rest[:count]
        down_ref = rest[count]
        out_ref, tiles, arrived = rest[-3:]
        copies = []
        for j in range(count):
            for c in range(cuts):
                start = pl.multiple_of(ids[j] * depth + c * cut, LANES)
                copy = pltpu.make_async_copy(
                    down_ref.at[pl.ds(start, cut), :],
                    tiles.at[j, pl.ds(c * cut, cut), :],
                    arrived.at[j, c],
                )
                copy.start()
                copies.append((j, c, copy))
        value = total_ref[...]
        for j, c, copy in copies:
            copy.wait()
            value = value + jnp.dot(
                hidden_refs[j][:, c * cut : (c + 1) * cut],
                tiles[j, c * cut : (c + 1) * cut, :],
                preferred_element_type=jnp.float32,
            )
        out_ref[...] = value

    return pl.pallas_call(
        kernel,
        out_shape=jax.ShapeDtypeStruct((rows, width), jnp.float32),
        grid_spec=pltpu.PrefetchScalarGridSpec(
            num_scalar_prefetch=1,
            grid=(),
            in_specs=[pl.BlockSpec(memory_space=pltpu.VMEM)] * (1 + count)
            + [pl.BlockSpec(memory_space=pl.ANY)] * (1 + len(after)),
            out_specs=pl.BlockSpec(memory_space=pltpu.VMEM),
            scratch_shapes=[
                pltpu.VMEM((count, depth, width), jnp.bfloat16),
                pltpu.SemaphoreType.DMA((count, cuts)),
            ],
        ),
        compiler_params=pltpu.CompilerParams(vmem_limit_bytes=VMEM_LIMIT),
        cost_estimate=pl.CostEstimate(
            flops=2 * count * rows * depth * width,
            bytes_accessed=2 * count * depth * width,
            transcendentals=0,
        ),
        name="down_blocks",
    )(jnp.stack(blocks), total, *hidden, down_tile, *after)


def on_device(stream, table_rows, token_ids, norm_gain, gate_weight, up_weight, down_weight):
    f_ways = lax.axis_size("tp") // D_WAYS
    low_bits = f_ways.bit_length() - 1
    index = lax.axis_index("tp")
    block_pos = index // f_ways
    width = gate_weight.shape[1]
    order = ring_order(f_ways)
    place = jnp.array([order.index(d) for d in range(D_WAYS)], jnp.int32)[block_pos]

    def shift(value, step):
        pairs = [
            (order[p] * f_ways + f, order[(p + step) % D_WAYS] * f_ways + f)
            for p in range(D_WAYS)
            for f in range(f_ways)
        ]
        return lax.ppermute(value, "tp", pairs)

    def at(distance):
        return (place + distance + D_WAYS) % D_WAYS

    gate_tile = gate_weight[0]
    up_tile = up_weight[0]
    down_tile = down_weight[0]
    bf16, f32 = jnp.bfloat16, jnp.float32

    gain_block = lax.dynamic_slice_in_dim(norm_gain, block_pos * width, width)
    picked = jnp.take(table_rows, token_ids[0], axis=0)
    block_in = (stream.astype(f32) + picked.astype(f32)).astype(bf16)
    feature_block = gather_block(block_in, index, low_bits).astype(f32)
    scaled = (feature_block * gain_block[None, :]).astype(bf16)
    wide_in = block_in.astype(f32)
    squares = lax.psum(jnp.sum(wide_in * wide_in, axis=1), "tp")

    far = up_blocks(scaled, gate_tile, up_tile, [at(4)], [])
    right, left = far[0, 0].astype(bf16), far[0, 1].astype(bf16)
    for distance in (3, 2, 1, 0):
        blocks = [at(distance), at(-distance)] if distance else [at(0)]
        own = up_blocks(scaled, gate_tile, up_tile, blocks, [right, left])
        right, left = shift(right, 1), shift(left, -1)
        if distance == 3:
            right = jnp.stack([own[0, 0] + right.astype(f32), own[0, 1]]).astype(bf16)
            left = jnp.stack([own[1, 0], own[1, 1] + left.astype(f32)]).astype(bf16)
        elif distance:
            right = (own[0] + right.astype(f32)).astype(bf16)
            left = (own[1] + left.astype(f32)).astype(bf16)
        else:
            pair = own[0] + right.astype(f32) + left.astype(f32)

    scale_rows = lax.rsqrt(squares[:, None] / D + 1e-05)
    pair = pair * scale_rows
    mine = (jax.nn.silu(pair[0]) * pair[1]).astype(bf16)

    half = mine.shape[0] // 2
    total = jnp.zeros((mine.shape[0], width), f32)
    total = down_blocks(total, [mine], down_tile, [at(0)], [])
    right, left = shift(mine, 1), shift(mine, -1)
    for distance in (1, 2):
        next_right, next_left = shift(right, 1), shift(left, -1)
        total = down_blocks(total, [right, left], down_tile, [at(-distance), at(distance)], [])
        right, left = next_right, next_left
    upper, lower = shift(right[:half], 1), shift(left[half:], -1)
    total = down_blocks(total, [right, left], down_tile, [at(-3), at(3)], [])
    far_hidden = jnp.concatenate([upper, lower], 0)
    total = down_blocks(total, [far_hidden], down_tile, [at(4)], [])

    summed = sum_blocks(total, index, low_bits)
    current = (wide_in + summed).astype(bf16)
    return current[None]


def solution(mesh):
    placed = (
        P("groups", "tp"),
        P("groups", "tp"),
        P(None, "groups"),
        P(),
        P("tp", None, None),
        P("tp", None, None),
        P("tp", None, None),
    )
    return jax.shard_map(
        on_device, mesh=mesh, in_specs=placed, out_specs=P(None, "groups", "tp"), check_vma=False
    )
```

time: 659 us -> 123 us (0.19)
  waiting for transfers between devices: 582 us -> 17.6 us
  Pallas kernels: 0 us -> 41 us
  matrix products: 35.7 us -> 0 us
  blocking collectives: 0 us -> 32.1 us
  other arithmetic: 24.1 us -> 4.62 us
    ppermute x8 -> x2, waiting for transfers between devices: 582 us -> 1.24 us  [from_partner(): return lax.ppermute(value, axis, pairs)]
    pallas_call x0 -> x10, Pallas kernels: none -> 41 us  [the longest x5 25 us: up_blocks(): pl.pallas_call(kernel, out_shape=jax.ShapeDtypeStruct((count, 2, rows, wi...]
    dot_general x3 -> x0, matrix products: 35.7 us -> none  [the longest x1 13 us: on_device(): jnp.dot(hidden, down_tile, preferred_element_type=jnp.float32)]
    psum x0 -> x1, blocking collectives: none -> 32.1 us  [on_device(): squares = lax.psum(jnp.sum(wide_in * wide_in, axis=1), 'tp')]
    add x5 -> x0, other arithmetic: 20.4 us -> none  [the longest x3 20.4 us: sum_units(): pair = pair + from_partner(pair, 'tp', low_bits + level)]
    ppermute x0 -> x16, starting transfers between devices: none -> 18.3 us  [shift(): return lax.ppermute(value, 'tp', pairs)]
    ppermute x0 -> x16, waiting for transfers between devices: none -> 16.4 us  [shift(): return lax.ppermute(value, 'tp', pairs)]
    ppermute x8 -> x2, starting transfers between devices: 14.5 us -> 0.59 us  [from_partner(): return lax.ppermute(value, axis, pairs)]
  transfers between devices with their start and end apart: 8 -> 18, of which waited for: 8 -> 11; matrix products, arithmetic and copies ran while one was open for 0% -> 2% of each run, Pallas kernels for 0% -> 29%
where the time goes in v1:
time: 123 us
  Pallas kernels  41 us (33%)
  blocking collectives  32.1 us (26%)
  starting transfers between devices  18.9 us (15%)
  waiting for transfers between devices  17.6 us (14%)
  between operations  5.59 us (5%)
  other arithmetic  4.62 us (4%)
  local copies, waits for them, and re-layouts  2.74 us (2%)
    psum x1, blocking collectives, on_device(): squares = lax.psum(jnp.sum(wide_in * wide_in, axis=1), 'tp')  32.1 us
    pallas_call x5, Pallas kernels, up_blocks(): pl.pallas_call(kernel, out_shape=jax.ShapeDtypeStruct((count, 2, rows, wi...  25 us
    ppermute x16, starting transfers between devices, shift(): return lax.ppermute(value, 'tp', pairs)  18.3 us
    ppermute x16, waiting for transfers between devices, shift(): return lax.ppermute(value, 'tp', pairs)  16.4 us
    pallas_call x5, Pallas kernels, down_blocks(): pl.pallas_call(kernel, out_shape=jax.ShapeDtypeStruct((rows, width), jnp....  16 us
  transfers between devices with their start and end apart: 18, of which 11 were waited for; matrix products, arithmetic and copies ran while one was open for 2% of the time, Pallas kernels for 29%

profile of v1, /device:TPU:0, one launch (start us, length us, event | category | flops | bytes accessed | tf_op | source)
XLA Modules:
  0.0 122.6 jit_solution(15543714074742091799)
XLA Ops:
  7.7 3.5 %up_blocks.5 = f32[1,2,64,1664]{3,2,1,0:T(8,128)S(1)} custom-call(s32[1]{0:T(128)} %bitcast.4.ids, bf16[64,1024]{1,0:T(8,128)(2,1)S(1)} %multiply_convert_fusion.x_ref, bf16[1024,13312]{1,0:T(8,128)(2,1)} %bitcast.95, bf16[1024,13312]{1,0:T(8,128)(2,1)} %bitcast.100), custom_call_target="tpu_custom_call" | custom-call | flops 436207616 | bytes 6815744 | tf_op jit(solution)/shard_map/up_blocks/pallas_call | solution.py:99
  11.3 2.7 %collective-permute-start.1 = (bf16[64,1664]{1,0:T(8,128)(2,1)S(1)}, bf16[64,1664]{1,0:T(8,128)(2,1)S(1)}, u32[]{:S(2)}, u32[]{:S(2)}) collective-permute-start(bf16[64,1664]{1,0:T(8,128)(2,1)S(1)} %get-tuple-element.16.rest_0_), channel_id=1, source_target_pairs={{0,4},{1,5},{4,8},{5,9},{8,12},{9,13},{12,14},{13,15},{14,10},{15,... | collective-permute-start | bytes 638984 | tf_op jit(solution)/shard_map/ppermute | solution.py:200
  13.9 6.0 %up_blocks.6 = f32[2,2,64,1664]{3,2,1,0:T(8,128)S(1)} custom-call(s32[2]{0:T(128)S(1)} %pad_add_fusion.5.ids, bf16[64,1024]{1,0:T(8,128)(2,1)S(1)} %multiply_convert_fusion.x_ref, bf16[1024,13312]{1,0:T(8,128)(2,1)} %bitcast.96, bf16[1024,13312]{1,0:T(8,128)(2,1)} %bitcast.101, bf16[64,1664]{1,0:T(8,128)(2,1)S(1)} %get-tuple-element.16.rest_0_, ...), custom_call_target="tpu_custom_call" | custom-call | flops 872415232 | bytes 13631488 | tf_op jit(solution)/shard_map/up_blocks/pallas_call | solution.py:99
  22.3 1.3 %collective-permute-start.3 = (bf16[2,64,1664]{2,1,0:T(8,128)(2,1)S(1)}, bf16[2,64,1664]{2,1,0:T(8,128)(2,1)S(1)}, u32[]{:S(2)}, u32[]{:S(2)}) collective-permute-start(bf16[2,64,1664]{2,1,0:T(8,128)(2,1)S(1)} %pad_maximum_fusion.rest_0_), channel_id=1, source_target_pairs={{0,4},{1,5},{4,8},{5,9},{8,12},{9,13},{12,14},{13,15},{14,10},{15,... | collective-permute-start | bytes 1277960 | tf_op jit(solution)/shard_map/ppermute | solution.py:200
  25.0 6.0 %up_blocks.7 = f32[2,2,64,1664]{3,2,1,0:T(8,128)S(1)} custom-call(s32[2]{0:T(128)S(1)} %pad_add_fusion.4.ids, bf16[64,1024]{1,0:T(8,128)(2,1)S(1)} %multiply_convert_fusion.x_ref, bf16[1024,13312]{1,0:T(8,128)(2,1)} %bitcast.97, bf16[1024,13312]{1,0:T(8,128)(2,1)} %bitcast.102, bf16[2,64,1664]{2,1,0:T(8,128)(2,1)S(1)} %pad_maximum_fusion.rest_0_, ...), custom_call_target="tpu_custom_call" | custom-call | flops 872415232 | bytes 13631488 | tf_op jit(solution)/shard_map/up_blocks/pallas_call | solution.py:99
  31.0 1.6 %collective-permute-done.4 = bf16[2,64,1664]{2,1,0:T(8,128)(2,1)S(1)} collective-permute-done((bf16[2,64,1664]{2,1,0:T(8,128)(2,1)S(1)}, bf16[2,64,1664]{2,1,0:T(8,128)(2,1)S(1)}, u32[]{:S(2)}, u32[]{:S(2)}) %collective-permute-start.4) | collective-permute-done | bytes 426016 | tf_op jit(solution)/shard_map/ppermute | solution.py:200
  34.7 1.3 %collective-permute-start.6 = (bf16[2,64,1664]{2,1,0:T(8,128)(2,1)S(1)}, bf16[2,64,1664]{2,1,0:T(8,128)(2,1)S(1)}, u32[]{:S(2)}, u32[]{:S(2)}) collective-permute-start(bf16[2,64,1664]{2,1,0:T(8,128)(2,1)S(1)} %get-tuple-element.9.rest_1_), channel_id=1, source_target_pairs={{0,2},{1,3},{4,0},{5,1},{8,4},{9,5},{12,8},{13,9},{14,12},{15,13},... | collective-permute-start | bytes 1277960 | tf_op jit(solution)/shard_map/ppermute | solution.py:200
  37.4 6.1 %up_blocks.8 = f32[2,2,64,1664]{3,2,1,0:T(8,128)S(1)} custom-call(s32[2]{0:T(128)S(1)} %pad_add_fusion.3.ids, bf16[64,1024]{1,0:T(8,128)(2,1)S(1)} %multiply_convert_fusion.x_ref, bf16[1024,13312]{1,0:T(8,128)(2,1)} %bitcast.98, bf16[1024,13312]{1,0:T(8,128)(2,1)} %bitcast.103, bf16[2,64,1664]{2,1,0:T(8,128)(2,1)S(1)} %get-tuple-element.10.rest_0_, ...), custom_call_target="tpu_custom_call" | custom-call | flops 872415232 | bytes 13631488 | tf_op jit(solution)/shard_map/up_blocks/pallas_call | solution.py:99
  44.7 1.5 %collective-permute-start.7 = (bf16[2,64,1664]{2,1,0:T(8,128)(2,1)S(1)}, bf16[2,64,1664]{2,1,0:T(8,128)(2,1)S(1)}, u32[]{:S(2)}, u32[]{:S(2)}) collective-permute-start(bf16[2,64,1664]{2,1,0:T(8,128)(2,1)S(1)} %get-tuple-element.8.rest_0_), channel_id=1, source_target_pairs={{0,4},{1,5},{4,8},{5,9},{8,12},{9,13},{12,14},{13,15},{14,10},{15,... | collective-permute-start | bytes 1277960 | tf_op jit(solution)/shard_map/ppermute | solution.py:200
  47.4 32.1 %psum.7 = f32[64]{0:T(128)S(1)} all-reduce(f32[64]{0:T(128)S(1)} %get-tuple-element.5), channel_id=1, replica_groups=mesh['groups'=2,'tp'=16] {'tp'}, use_global_device_ids=true, to_apply=%region_1.2 | all-reduce | flops 64 | bytes 512 | tf_op jit(solution)/shard_map/psum | solution.py:216
  79.5 3.5 %up_blocks.9 = f32[1,2,64,1664]{3,2,1,0:T(8,128)S(1)} custom-call(s32[1]{0:T(128)} %bitcast.18.ids, bf16[64,1024]{1,0:T(8,128)(2,1)S(1)} %multiply_convert_fusion.x_ref, bf16[1024,13312]{1,0:T(8,128)(2,1)} %bitcast.99, bf16[1024,13312]{1,0:T(8,128)(2,1)} %bitcast.104, bf16[2,64,1664]{2,1,0:T(8,128)(2,1)S(1)} %get-tuple-element.8.rest_0_, ...), custom_call_target="tpu_custom_call" | custom-call | flops 436207616 | bytes 6815744 | tf_op jit(solution)/shard_map/up_blocks/pallas_call | solution.py:99
  83.4 2.0 %collective-permute-start.10 = (bf16[64,1664]{1,0:T(8,128)(2,1)S(1)}, bf16[64,1664]{1,0:T(8,128)(2,1)S(1)}, u32[]{:S(2)}, u32[]{:S(2)}) collective-permute-start(bf16[64,1664]{1,0:T(8,128)(2,1)S(1)} %fusion.11.rest_0_), channel_id=1, source_target_pairs={{0,2},{1,3},{4,0},{5,1},{8,4},{9,5},{12,8},{13,9},{14,12},{15,13},... | collective-permute-start | bytes 638984 | tf_op jit(solution)/shard_map/ppermute | solution.py:200
  85.4 4.5 %collective-permute-done.9.rest_0_ = bf16[64,1664]{1,0:T(8,128)(2,1)S(1)} collective-permute-done((bf16[64,1664]{1,0:T(8,128)(2,1)S(1)}, bf16[64,1664]{1,0:T(8,128)(2,1)S(1)}, u32[]{:S(2)}, u32[]{:S(2)}) %collective-permute-start.9) | collective-permute-done | bytes 213024 | tf_op jit(solution)/shard_map/ppermute | solution.py:200
  90.0 2.3 %collective-permute-start.12 = (bf16[64,1664]{1,0:T(8,128)(2,1)S(1)}, bf16[64,1664]{1,0:T(8,128)(2,1)S(1)}, u32[]{:S(2)}, u32[]{:S(2)}) collective-permute-start(bf16[64,1664]{1,0:T(8,128)(2,1)S(1)} %collective-permute-done.10.rest_1_), channel_id=1, source_target_pairs={{0,2},{1,3},{4,0},{5,1},{8,4},{9,5},{12,8},{13,9},{14,12},{15,13},... | collective-permute-start | bytes 638984 | tf_op jit(solution)/shard_map/ppermute | solution.py:200
  92.3 5.3 %collective-permute-done.11.rest_0_ = bf16[64,1664]{1,0:T(8,128)(2,1)S(1)} collective-permute-done((bf16[64,1664]{1,0:T(8,128)(2,1)S(1)}, bf16[64,1664]{1,0:T(8,128)(2,1)S(1)}, u32[]{:S(2)}, u32[]{:S(2)}) %collective-permute-start.11) | collective-permute-done | bytes 213024 | tf_op jit(solution)/shard_map/ppermute | solution.py:200
  97.7 2.3 %collective-permute-start.14 = (bf16[64,1664]{1,0:T(8,128)(2,1)S(1)}, bf16[64,1664]{1,0:T(8,128)(2,1)S(1)}, u32[]{:S(2)}, u32[]{:S(2)}) collective-permute-start(bf16[64,1664]{1,0:T(8,128)(2,1)S(1)} %collective-permute-done.12.rest_1_), channel_id=1, source_target_pairs={{0,2},{1,3},{4,0},{5,1},{8,4},{9,5},{12,8},{13,9},{14,12},{15,13},... | collective-permute-start | bytes 638984 | tf_op jit(solution)/shard_map/ppermute | solution.py:200
  100.1 2.2 %down_blocks.5.total_ref = f32[64,1024]{1,0:T(8,128)S(1)} custom-call(s32[1]{0:T(128)} %bitcast.18.ids, f32[64,1024]{1,0:T(8,128)S(1)} %broadcast_in_dim.21.total_ref, bf16[64,1664]{1,0:T(8,128)(2,1)S(1)} %fusion.11.rest_0_, bf16[13312,1024]{1,0:T(8,128)(2,1)} %bitcast.105), custom_call_target="tpu_custom_call" | custom-call | flops 218103808 | bytes 3407872 | tf_op jit(solution)/shard_map/down_blocks/pallas_call | solution.py:161
  102.3 1.6 %collective-permute-done.13.rest_0_ = bf16[64,1664]{1,0:T(8,128)(2,1)S(1)} collective-permute-done((bf16[64,1664]{1,0:T(8,128)(2,1)S(1)}, bf16[64,1664]{1,0:T(8,128)(2,1)S(1)}, u32[]{:S(2)}, u32[]{:S(2)}) %collective-permute-start.13) | collective-permute-done | bytes 213024 | tf_op jit(solution)/shard_map/ppermute | solution.py:200
  104.3 2.4 %collective-permute-start.16 = (bf16[32,1664]{1,0:T(8,128)(2,1)S(1)}, bf16[32,1664]{1,0:T(8,128)(2,1)S(1)}, u32[]{:S(2)}, u32[]{:S(2)}) collective-permute-start(bf16[32,1664]{1,0:T(8,128)(2,1)S(1)} %slice.83), channel_id=1, source_target_pairs={{0,2},{1,3},{4,0},{5,1},{8,4},{9,5},{12,8},{13,9},{14,12},{15,13},... | collective-permute-start | bytes 319496 | tf_op jit(solution)/shard_map/ppermute | solution.py:200
  106.7 3.9 %down_blocks.6.total_ref = f32[64,1024]{1,0:T(8,128)S(1)} custom-call(s32[2]{0:T(128)S(1)} %pad_add_fusion.2.ids, f32[64,1024]{1,0:T(8,128)S(1)} %down_blocks.5.total_ref, bf16[64,1664]{1,0:T(8,128)(2,1)S(1)} %collective-permute-done.9.rest_0_, bf16[64,1664]{1,0:T(8,128)(2,1)S(1)} %collective-permute-done.10.rest_1_, bf16[13312,1024]{1,0:T(8,128)(2,1)} %bitcast.106), custom_call_target="tpu_custom_call" | custom-call | flops 436207616 | bytes 6815744 | tf_op jit(solution)/shard_map/down_blocks/pallas_call | solution.py:161
  110.6 3.9 %down_blocks.7.total_ref = f32[64,1024]{1,0:T(8,128)S(1)} custom-call(s32[2]{0:T(128)S(1)} %pad_add_fusion.1.ids, f32[64,1024]{1,0:T(8,128)S(1)} %down_blocks.6.total_ref, bf16[64,1664]{1,0:T(8,128)(2,1)S(1)} %collective-permute-done.11.rest_0_, bf16[64,1664]{1,0:T(8,128)(2,1)S(1)} %collective-permute-done.12.rest_1_, bf16[13312,1024]{1,0:T(8,128)(2,1)} %bitcast.107), custom_call_target="tpu_custom_call" | custom-call | flops 436207616 | bytes 6815744 | tf_op jit(solution)/shard_map/down_blocks/pallas_call | solution.py:161
  114.4 3.9 %down_blocks.8.total_ref = f32[64,1024]{1,0:T(8,128)S(1)} custom-call(s32[2]{0:T(128)S(1)} %pad_add_fusion.ids, f32[64,1024]{1,0:T(8,128)S(1)} %down_blocks.7.total_ref, bf16[64,1664]{1,0:T(8,128)(2,1)S(1)} %collective-permute-done.13.rest_0_, bf16[64,1664]{1,0:T(8,128)(2,1)S(1)} %collective-permute-done.14.rest_1_, bf16[13312,1024]{1,0:T(8,128)(2,1)} %bitcast.108), custom_call_target="tpu_custom_call" | custom-call | flops 436207616 | bytes 6815744 | tf_op jit(solution)/shard_map/down_blocks/pallas_call | solution.py:161
  118.4 2.2 %down_blocks.9 = f32[64,1024]{1,0:T(8,128)S(1)} custom-call(s32[1]{0:T(128)} %bitcast.4.ids, f32[64,1024]{1,0:T(8,128)S(1)} %down_blocks.8.total_ref, bf16[64,1664]{1,0:T(8,128)(2,1)S(1)} %pad_maximum_fusion.2.rest_0_, bf16[13312,1024]{1,0:T(8,128)(2,1)} %bitcast.109), custom_call_target="tpu_custom_call" | custom-call | flops 218103808 | bytes 3407872 | tf_op jit(solution)/shard_map/down_blocks/pallas_call | solution.py:161
  120.7 1.2 %collective-permute-done.17 = bf16[64,512]{1,0:T(8,128)(2,1)S(1)} collective-permute-done((bf16[64,512]{1,0:T(8,128)(2,1)S(1)}, bf16[64,512]{1,0:T(8,128)(2,1)S(1)}, u32[]{:S(2)}, u32[]{:S(2)}) %collective-permute-start.17) | collective-permute-done | bytes 65568 | tf_op jit(solution)/shard_map/ppermute | solution.py:23
  (59 shorter events, 14.0 us)
Async XLA Ops:
  0.0 1.4 %copy-start = (bf16[512,512]{1,0:T(8,128)(2,1)S(1)}, bf16[512,512]{1,0:T(8,128)(2,1)}, u32[]{:S(2)}) copy-start(bf16[512,512]{1,0:T(8,128)(2,1)} %param.9) | copy-start | bytes 1572868
  3.1 4.5 %collective-permute-start = (bf16[64,512]{1,0:T(8,128)(2,1)S(1)}, bf16[64,512]{1,0:T(8,128)(2,1)S(1)}, u32[]{:S(2)}, u32[]{:S(2)}) collective-permute-start(bf16[64,512]{1,0:T(8,128)(2,1)S(1)} %get-tuple-element.6), channel_id=1, source_target_pairs={{0,1},{1,0},{2,3},{3,2},{4,5},{5,4},{6,7},{7,6},{8,9},{9,8},{10,11... | collective-permute-start | bytes 196616 | tf_op jit(solution)/shard_map/ppermute | solution.py:23
  11.3 8.8 %collective-permute-start.1 = (bf16[64,1664]{1,0:T(8,128)(2,1)S(1)}, bf16[64,1664]{1,0:T(8,128)(2,1)S(1)}, u32[]{:S(2)}, u32[]{:S(2)}) collective-permute-start(bf16[64,1664]{1,0:T(8,128)(2,1)S(1)} %get-tuple-element.16.rest_0_), channel_id=1, source_target_pairs={{0,4},{1,5},{4,8},{5,9},{8,12},{9,13},{12,14},{13,15},{14,10},{15,... | collective-permute-start | bytes 638984 | tf_op jit(solution)/shard_map/ppermute | solution.py:200
  13.9 7.3 %collective-permute-start.2 = (bf16[64,1664]{1,0:T(8,128)(2,1)S(1)}, bf16[64,1664]{1,0:T(8,128)(2,1)S(1)}, u32[]{:S(2)}, u32[]{:S(2)}) collective-permute-start(bf16[64,1664]{1,0:T(8,128)(2,1)S(1)} %get-tuple-element.15.rest_1_), channel_id=1, source_target_pairs={{0,2},{1,3},{4,0},{5,1},{8,4},{9,5},{12,8},{13,9},{14,12},{15,13},... | collective-permute-start | bytes 638984 | tf_op jit(solution)/shard_map/ppermute | solution.py:200
  21.4 11.1 %collective-permute-start.4 = (bf16[2,64,1664]{2,1,0:T(8,128)(2,1)S(1)}, bf16[2,64,1664]{2,1,0:T(8,128)(2,1)S(1)}, u32[]{:S(2)}, u32[]{:S(2)}) collective-permute-start(bf16[2,64,1664]{2,1,0:T(8,128)(2,1)S(1)} %pad_maximum_fusion.1.rest_1_), channel_id=1, source_target_pairs={{0,2},{1,3},{4,0},{5,1},{8,4},{9,5},{12,8},{13,9},{14,12},{15,13},... | collective-permute-start | bytes 1277960 | tf_op jit(solution)/shard_map/ppermute | solution.py:200
  22.3 11.4 %collective-permute-start.3 = (bf16[2,64,1664]{2,1,0:T(8,128)(2,1)S(1)}, bf16[2,64,1664]{2,1,0:T(8,128)(2,1)S(1)}, u32[]{:S(2)}, u32[]{:S(2)}) collective-permute-start(bf16[2,64,1664]{2,1,0:T(8,128)(2,1)S(1)} %pad_maximum_fusion.rest_0_), channel_id=1, source_target_pairs={{0,4},{1,5},{4,8},{5,9},{8,12},{9,13},{12,14},{13,15},{14,10},{15,... | collective-permute-start | bytes 1277960 | tf_op jit(solution)/shard_map/ppermute | solution.py:200
  33.9 10.5 %collective-permute-start.5 = (bf16[2,64,1664]{2,1,0:T(8,128)(2,1)S(1)}, bf16[2,64,1664]{2,1,0:T(8,128)(2,1)S(1)}, u32[]{:S(2)}, u32[]{:S(2)}) collective-permute-start(bf16[2,64,1664]{2,1,0:T(8,128)(2,1)S(1)} %get-tuple-element.10.rest_0_), channel_id=1, source_target_pairs={{0,4},{1,5},{4,8},{5,9},{8,12},{9,13},{12,14},{13,15},{14,10},{15,... | collective-permute-start | bytes 1277960 | tf_op jit(solution)/shard_map/ppermute | solution.py:200
  34.7 9.8 %collective-permute-start.6 = (bf16[2,64,1664]{2,1,0:T(8,128)(2,1)S(1)}, bf16[2,64,1664]{2,1,0:T(8,128)(2,1)S(1)}, u32[]{:S(2)}, u32[]{:S(2)}) collective-permute-start(bf16[2,64,1664]{2,1,0:T(8,128)(2,1)S(1)} %get-tuple-element.9.rest_1_), channel_id=1, source_target_pairs={{0,2},{1,3},{4,0},{5,1},{8,4},{9,5},{12,8},{13,9},{14,12},{15,13},... | collective-permute-start | bytes 1277960 | tf_op jit(solution)/shard_map/ppermute | solution.py:200
  44.7 38.4 %collective-permute-start.7 = (bf16[2,64,1664]{2,1,0:T(8,128)(2,1)S(1)}, bf16[2,64,1664]{2,1,0:T(8,128)(2,1)S(1)}, u32[]{:S(2)}, u32[]{:S(2)}) collective-permute-start(bf16[2,64,1664]{2,1,0:T(8,128)(2,1)S(1)} %get-tuple-element.8.rest_0_), channel_id=1, source_target_pairs={{0,4},{1,5},{4,8},{5,9},{8,12},{9,13},{12,14},{13,15},{14,10},{15,... | collective-permute-start | bytes 1277960 | tf_op jit(solution)/shard_map/ppermute | solution.py:200
  46.1 36.9 %collective-permute-start.8 = (bf16[2,64,1664]{2,1,0:T(8,128)(2,1)S(1)}, bf16[2,64,1664]{2,1,0:T(8,128)(2,1)S(1)}, u32[]{:S(2)}, u32[]{:S(2)}) collective-permute-start(bf16[2,64,1664]{2,1,0:T(8,128)(2,1)S(1)} %get-tuple-element.7.rest_1_), channel_id=1, source_target_pairs={{0,2},{1,3},{4,0},{5,1},{8,4},{9,5},{12,8},{13,9},{14,12},{15,13},... | collective-permute-start | bytes 1277960 | tf_op jit(solution)/shard_map/ppermute | solution.py:200
  83.3 6.6 %collective-permute-start.9 = (bf16[64,1664]{1,0:T(8,128)(2,1)S(1)}, bf16[64,1664]{1,0:T(8,128)(2,1)S(1)}, u32[]{:S(2)}, u32[]{:S(2)}) collective-permute-start(bf16[64,1664]{1,0:T(8,128)(2,1)S(1)} %fusion.11.rest_0_), channel_id=1, source_target_pairs={{0,4},{1,5},{4,8},{5,9},{8,12},{9,13},{12,14},{13,15},{14,10},{15,... | collective-permute-start | bytes 638984 | tf_op jit(solution)/shard_map/ppermute | solution.py:200
  83.4 6.6 %collective-permute-start.10 = (bf16[64,1664]{1,0:T(8,128)(2,1)S(1)}, bf16[64,1664]{1,0:T(8,128)(2,1)S(1)}, u32[]{:S(2)}, u32[]{:S(2)}) collective-permute-start(bf16[64,1664]{1,0:T(8,128)(2,1)S(1)} %fusion.11.rest_0_), channel_id=1, source_target_pairs={{0,2},{1,3},{4,0},{5,1},{8,4},{9,5},{12,8},{13,9},{14,12},{15,13},... | collective-permute-start | bytes 638984 | tf_op jit(solution)/shard_map/ppermute | solution.py:200
  89.9 7.7 %collective-permute-start.11 = (bf16[64,1664]{1,0:T(8,128)(2,1)S(1)}, bf16[64,1664]{1,0:T(8,128)(2,1)S(1)}, u32[]{:S(2)}, u32[]{:S(2)}) collective-permute-start(bf16[64,1664]{1,0:T(8,128)(2,1)S(1)} %collective-permute-done.9.rest_0_), channel_id=1, source_target_pairs={{0,4},{1,5},{4,8},{5,9},{8,12},{9,13},{12,14},{13,15},{14,10},{15,... | collective-permute-start | bytes 638984 | tf_op jit(solution)/shard_map/ppermute | solution.py:200
  90.0 7.7 %collective-permute-start.12 = (bf16[64,1664]{1,0:T(8,128)(2,1)S(1)}, bf16[64,1664]{1,0:T(8,128)(2,1)S(1)}, u32[]{:S(2)}, u32[]{:S(2)}) collective-permute-start(bf16[64,1664]{1,0:T(8,128)(2,1)S(1)} %collective-permute-done.10.rest_1_), channel_id=1, source_target_pairs={{0,2},{1,3},{4,0},{5,1},{8,4},{9,5},{12,8},{13,9},{14,12},{15,13},... | collective-permute-start | bytes 638984 | tf_op jit(solution)/shard_map/ppermute | solution.py:200
  97.6 6.3 %collective-permute-start.13 = (bf16[64,1664]{1,0:T(8,128)(2,1)S(1)}, bf16[64,1664]{1,0:T(8,128)(2,1)S(1)}, u32[]{:S(2)}, u32[]{:S(2)}) collective-permute-start(bf16[64,1664]{1,0:T(8,128)(2,1)S(1)} %collective-permute-done.11.rest_0_), channel_id=1, source_target_pairs={{0,4},{1,5},{4,8},{5,9},{8,12},{9,13},{12,14},{13,15},{14,10},{15,... | collective-permute-start | bytes 638984 | tf_op jit(solution)/shard_map/ppermute | solution.py:200
  97.7 6.6 %collective-permute-start.14 = (bf16[64,1664]{1,0:T(8,128)(2,1)S(1)}, bf16[64,1664]{1,0:T(8,128)(2,1)S(1)}, u32[]{:S(2)}, u32[]{:S(2)}) collective-permute-start(bf16[64,1664]{1,0:T(8,128)(2,1)S(1)} %collective-permute-done.12.rest_1_), channel_id=1, source_target_pairs={{0,2},{1,3},{4,0},{5,1},{8,4},{9,5},{12,8},{13,9},{14,12},{15,13},... | collective-permute-start | bytes 638984 | tf_op jit(solution)/shard_map/ppermute | solution.py:200
  103.9 14.4 %collective-permute-start.15 = (bf16[32,1664]{1,0:T(8,128)(2,1)S(1)}, bf16[32,1664]{1,0:T(8,128)(2,1)S(1)}, u32[]{:S(2)}, u32[]{:S(2)}) collective-permute-start(bf16[32,1664]{1,0:T(8,128)(2,1)S(1)} %slice.82), channel_id=1, source_target_pairs={{0,4},{1,5},{4,8},{5,9},{8,12},{9,13},{12,14},{13,15},{14,10},{15,... | collective-permute-start | bytes 319496 | tf_op jit(solution)/shard_map/ppermute | solution.py:200
  104.3 14.0 %collective-permute-start.16 = (bf16[32,1664]{1,0:T(8,128)(2,1)S(1)}, bf16[32,1664]{1,0:T(8,128)(2,1)S(1)}, u32[]{:S(2)}, u32[]{:S(2)}) collective-permute-start(bf16[32,1664]{1,0:T(8,128)(2,1)S(1)} %slice.83), channel_id=1, source_target_pairs={{0,2},{1,3},{4,0},{5,1},{8,4},{9,5},{12,8},{13,9},{14,12},{15,13},... | collective-permute-start | bytes 319496 | tf_op jit(solution)/shard_map/ppermute | solution.py:200
  118.3 4.3 %copy-start.1 = (bf16[512,512]{1,0:T(8,128)(2,1)S(1)}, bf16[512,512]{1,0:T(8,128)(2,1)}, u32[]{:S(2)}) copy-start(bf16[512,512]{1,0:T(8,128)(2,1)} %param.9) | copy-start | bytes 1572868
  120.6 1.3 %collective-permute-start.17 = (bf16[64,512]{1,0:T(8,128)(2,1)S(1)}, bf16[64,512]{1,0:T(8,128)(2,1)S(1)}, u32[]{:S(2)}, u32[]{:S(2)}) collective-permute-start(bf16[64,512]{1,0:T(8,128)(2,1)S(1)} %select_convert_fusion), channel_id=1, source_target_pairs={{0,1},{1,0},{2,3},{3,2},{4,5},{5,4},{6,7},{7,6},{8,9},{9,8},{10,11... | collective-permute-start | bytes 196616 | tf_op jit(solution)/shard_map/ppermute | solution.py:23

commit v2 on v0

v2 whole, which is shorter than its diff:
```python
import jax
import jax.numpy as jnp
from jax import lax
from jax.experimental import pallas as pl
from jax.experimental.pallas import tpu as pltpu
from jax.sharding import PartitionSpec as P

D = 8192
D_WAYS = 8
LANES = 128
CHUNK = 512
VMEM_LIMIT = 32 * 2**20
BF16 = jnp.bfloat16
F32 = jnp.float32
IN_VMEM = pl.BlockSpec(memory_space=pltpu.VMEM)
IN_PLACE = pl.BlockSpec(memory_space=pl.ANY)


def from_partner(value, axis, distance):
    mask = 2**distance
    pairs = [(source, source ^ mask) for source in range(lax.axis_size(axis))]
    return lax.ppermute(value, axis, pairs)


def bit_high(index, bit):
    return index // 2**bit % 2 == 1


def gather_block(local_rows, index, low_bits):
    piece = local_rows
    for bit in range(low_bits):
        other = from_partner(piece, "tp", bit)
        piece = jnp.where(
            bit_high(index, bit),
            jnp.concatenate([other, piece], 1),
            jnp.concatenate([piece, other], 1),
        )
    return piece


def halve_columns(values, index, bit):
    width = values.shape[-1] // 2
    lower = values[..., :width]
    upper = values[..., width:]
    high = bit_high(index, bit)
    return (jnp.where(high, upper, lower), jnp.where(high, lower, upper))


def sum_blocks(partial_value, index, low_bits):
    for bit in reversed(range(low_bits)):
        kept, sent = halve_columns(partial_value, index, bit)
        partial_value = kept + from_partner(sent.astype(BF16), "tp", bit).astype(sent.dtype)
    return partial_value


def general(stream, table_rows, token_ids, norm_gain, gate_tile, up_tile, down_tile):
    f_ways = lax.axis_size("tp") // D_WAYS
    low_bits = f_ways.bit_length() - 1
    high_bits = D_WAYS.bit_length() - 1
    index = lax.axis_index("tp")
    block_pos = index // f_ways
    width = gate_tile.shape[0]
    gain_block = lax.dynamic_slice_in_dim(norm_gain, block_pos * width, width)
    picked = jnp.take(table_rows, token_ids[0], axis=0)
    block_in = (stream.astype(F32) + picked.astype(F32)).astype(BF16)
    feature_block = gather_block(block_in, index, low_bits).astype(F32)
    total = jnp.sum(feature_block * feature_block, axis=1)
    for level in range(high_bits):
        total = total + from_partner(total, "tp", low_bits + level)
    scale_rows = lax.rsqrt(total[:, None] / D + 1e-05)
    normed = (feature_block * scale_rows * gain_block[None, :]).astype(BF16)
    pair = jnp.stack(
        [
            jnp.dot(normed, gate_tile, preferred_element_type=F32),
            jnp.dot(normed, up_tile, preferred_element_type=F32),
        ],
        axis=0,
    )
    for level in range(high_bits):
        pair = pair + from_partner(pair, "tp", low_bits + level)
    hidden = (jax.nn.silu(pair[0]) * pair[1]).astype(BF16)
    partial_value = jnp.dot(hidden, down_tile, preferred_element_type=F32)
    summed = sum_blocks(partial_value, index, low_bits)
    return (block_in.astype(F32) + summed).astype(BF16)


def chunks_of(size):
    return [(start, min(CHUNK, size - start)) for start in range(0, size, CHUNK)]


def params():
    return pltpu.CompilerParams(vmem_limit_bytes=VMEM_LIMIT)


def add_rows(token_ids, stream, table_rows):
    entries = table_rows.shape[0]

    def kernel(ids_ref, stream_ref, table_ref, out_ref):
        rows = lax.broadcasted_iota(jnp.int32, (entries, ids_ref.shape[1]), 0)
        chosen = jnp.where(rows == ids_ref[...], 1.0, 0.0).astype(BF16)
        picked = lax.dot_general(
            chosen, table_ref[...], (((0,), (0,)), ((), ())), preferred_element_type=F32
        )
        out_ref[...] = (stream_ref[...].astype(F32) + picked).astype(BF16)

    return pl.pallas_call(
        kernel,
        out_shape=jax.ShapeDtypeStruct(stream.shape, BF16),
        in_specs=[IN_VMEM] * 3,
        out_specs=IN_VMEM,
        name="add_rows",
    )(token_ids, stream, table_rows)


def start_up_copies(block, gate_ref, up_ref, tiles, arrived):
    width = gate_ref.shape[1] // D_WAYS
    depth = gate_ref.shape[0]
    copies = []
    for c, (start, size) in enumerate(chunks_of(2 * width)):
        pieces = []
        for m, ref in enumerate((gate_ref, up_ref)):
            low = max(start, m * width)
            high = min(start + size, (m + 1) * width)
            if low < high:
                column = pl.multiple_of(block * width + (low - m * width), LANES)
                pieces.append(
                    pltpu.make_async_copy(
                        ref.at[:, pl.ds(column, high - low)],
                        tiles.at[:, pl.ds(low, high - low)],
                        arrived.at[c, m],
                    )
                )
        for piece in pieces:
            piece.start()
        copies.append((start, size, pieces))
    return copies


def up_products(x, copies, tiles):
    for start, size, pieces in copies:
        for piece in pieces:
            piece.wait()
        yield start, size, jnp.dot(x, tiles[:, start : start + size], preferred_element_type=F32)


def first_up_block(scalars, own, other, gain, gate_tile, up_tile):
    depth, units = gate_tile.shape
    width = units // D_WAYS
    rows, share = own.shape
    count = len(chunks_of(2 * width))

    def kernel(
        scalars, own_ref, other_ref, gain_ref, gate_ref, up_ref, gate_out, up_out, x_ref, squares_ref, tiles, arrived
    ):
        copies = start_up_copies(scalars[0], gate_ref, up_ref, tiles, arrived)
        squares = jnp.zeros((rows, LANES), F32)
        for side, ref in ((scalars[2], own_ref), (1 - scalars[2], other_ref)):
            place = pl.ds(pl.multiple_of(side * share, LANES), share)
            value = ref[...].astype(F32)
            for lane in range(0, share, LANES):
                squares += value[:, lane : lane + LANES] * value[:, lane : lane + LANES]
            x_ref[:, place] = (value * gain_ref[:, place]).astype(BF16)
        squares_ref[...] = squares
        gate_out[:, :LANES] = squares.astype(BF16)
        for start, size, product in up_products(x_ref[...], copies, tiles):
            product = product.astype(BF16)
            split = min(max(width - start, 0), size)
            if split > 0:
                gate_out[:, LANES + start : LANES + start + split] = product[:, :split]
            if split < size:
                up_out[:, start + split - width : start + size - width] = product[:, split:]

    return pl.pallas_call(
        kernel,
        out_shape=[
            jax.ShapeDtypeStruct((rows, LANES + width), BF16),
            jax.ShapeDtypeStruct((rows, width), BF16),
            jax.ShapeDtypeStruct((rows, depth), BF16),
            jax.ShapeDtypeStruct((rows, LANES), F32),
        ],
        grid_spec=pltpu.PrefetchScalarGridSpec(
            num_scalar_prefetch=1,
            grid=(1,),
            in_specs=[
                IN_VMEM,
                IN_VMEM,
                pl.BlockSpec((1, depth), lambda i, scalars: (0, scalars[1])),
                IN_PLACE,
                IN_PLACE,
            ],
            out_specs=[IN_VMEM] * 4,
            scratch_shapes=[
                pltpu.VMEM((depth, 2 * width), BF16),
                pltpu.SemaphoreType.DMA((count, 2)),
            ],
        ),
        compiler_params=params(),
        cost_estimate=pl.CostEstimate(
            flops=4 * rows * depth * width, bytes_accessed=4 * depth * width, transcendentals=0
        ),
        name="first_up_block",
    )(scalars, own, other, gain, gate_tile, up_tile)


def up_blocks(x, squares, gate_tile, up_tile, blocks, after):
    depth, units = gate_tile.shape
    width = units // D_WAYS
    rows = x.shape[0]
    blocks_n = len(blocks)
    count = len(chunks_of(2 * width))

    def kernel(ids, x_ref, squares_ref, gate_ref, up_ref, *rest):
        out_refs = rest[len(after) : len(after) + blocks_n]
        tiles, arrived = rest[-2:]
        copies = [
            start_up_copies(ids[j], gate_ref, up_ref, tiles.at[j], arrived.at[j]) for j in range(blocks_n)
        ]
        for j in range(blocks_n):
            out_refs[j][:, :LANES] = squares_ref[...]
            for start, size, product in up_products(x_ref[...], copies[j], tiles.at[j]):
                out_refs[j][:, LANES + start : LANES + start + size] = product

    return pl.pallas_call(
        kernel,
        out_shape=[jax.ShapeDtypeStruct((rows, LANES + 2 * width), F32)] * blocks_n,
        grid_spec=pltpu.PrefetchScalarGridSpec(
            num_scalar_prefetch=1,
            grid=(),
            in_specs=[IN_VMEM] * 2 + [IN_PLACE] * (2 + len(after)),
            out_specs=[IN_VMEM] * blocks_n,
            scratch_shapes=[
                pltpu.VMEM((blocks_n, depth, 2 * width), BF16),
                pltpu.SemaphoreType.DMA((blocks_n, count, 2)),
            ],
        ),
        compiler_params=params(),
        cost_estimate=pl.CostEstimate(
            flops=4 * blocks_n * rows * depth * width,
            bytes_accessed=4 * blocks_n * depth * width,
            transcendentals=0,
        ),
        name="up_blocks",
    )(jnp.stack(blocks), x, squares, gate_tile, up_tile, *after)


def start_down_copies(block, down_ref, tiles, arrived):
    depth = down_ref.shape[0] // D_WAYS
    copies = []
    for c, (start, size) in enumerate(chunks_of(depth)):
        copy = pltpu.make_async_copy(
            down_ref.at[pl.ds(pl.multiple_of(block * depth + start, LANES), size), :],
            tiles.at[pl.ds(start, size), :],
            arrived.at[c],
        )
        copy.start()
        copies.append((start, size, copy))
    return copies


def down_products(value, hidden_ref, copies, tiles):
    for start, size, copy in copies:
        copy.wait()
        value = value + jnp.dot(
            hidden_ref[:, start : start + size],
            tiles[start : start + size, :],
            preferred_element_type=F32,
        )
    return value


def down_cost(count, rows, depth, width):
    return pl.CostEstimate(
        flops=2 * count * rows * depth * width,
        bytes_accessed=2 * count * depth * width,
        transcendentals=0,
    )


def down_blocks(total, hidden, down_tile, blocks):
    units, width = down_tile.shape
    depth = units // D_WAYS
    rows = hidden[0].shape[0]
    blocks_n = len(blocks)
    totals = [] if total is None else [total]

    def kernel(ids, *rest):
        hidden_refs = rest[len(totals) : len(totals) + blocks_n]
        down_ref, out_ref, tiles, arrived = rest[len(totals) + blocks_n :]
        copies = [start_down_copies(ids[j], down_ref, tiles.at[j], arrived.at[j]) for j in range(blocks_n)]
        value = rest[0][...] if totals else jnp.zeros((rows, width), F32)
        for j in range(blocks_n):
            value = down_products(value, hidden_refs[j], copies[j], tiles.at[j])
        out_ref[...] = value

    return pl.pallas_call(
        kernel,
        out_shape=jax.ShapeDtypeStruct((rows, width), F32),
        grid_spec=pltpu.PrefetchScalarGridSpec(
            num_scalar_prefetch=1,
            grid=(),
            in_specs=[IN_VMEM] * (len(totals) + blocks_n) + [IN_PLACE],
            out_specs=IN_VMEM,
            scratch_shapes=[
                pltpu.VMEM((blocks_n, depth, width), BF16),
                pltpu.SemaphoreType.DMA((blocks_n, len(chunks_of(depth)))),
            ],
        ),
        compiler_params=params(),
        cost_estimate=down_cost(blocks_n, rows, depth, width),
        name="down_blocks",
    )(jnp.stack(blocks), *totals, *hidden, down_tile)


def last_down_block(scalars, total, upper, lower, down_tile):
    units, width = down_tile.shape
    depth = units // D_WAYS
    rows = total.shape[0]
    half = width // 2

    def kernel(scalars, total_ref, upper_ref, lower_ref, down_ref, kept_ref, sent_ref, hidden, tiles, arrived):
        copies = start_down_copies(scalars[0], down_ref, tiles, arrived)
        hidden[: rows // 2] = upper_ref[...]
        hidden[rows // 2 :] = lower_ref[...]
        value = down_products(total_ref[...], hidden, copies, tiles)
        high = scalars[1] == 1
        kept_ref[...] = jnp.where(high, value[:, half:], value[:, :half])
        sent_ref[...] = jnp.where(high, value[:, :half], value[:, half:]).astype(BF16)

    return pl.pallas_call(
        kernel,
        out_shape=[
            jax.ShapeDtypeStruct((rows, half), F32),
            jax.ShapeDtypeStruct((rows, half), BF16),
        ],
        grid_spec=pltpu.PrefetchScalarGridSpec(
            num_scalar_prefetch=1,
            grid=(),
            in_specs=[IN_VMEM] * 3 + [IN_PLACE],
            out_specs=[IN_VMEM] * 2,
            scratch_shapes=[
                pltpu.VMEM((rows, depth), BF16),
                pltpu.VMEM((depth, width), BF16),
                pltpu.SemaphoreType.DMA((len(chunks_of(depth)),)),
            ],
        ),
        compiler_params=params(),
        cost_estimate=down_cost(1, rows, depth, width),
        name="last_down_block",
    )(scalars, total, upper, lower, down_tile)


def ring(stream, table_rows, token_ids, norm_gain, gate_tile, up_tile, down_tile):
    f_ways = lax.axis_size("tp") // D_WAYS
    low_bits = f_ways.bit_length() - 1
    index = lax.axis_index("tp")
    block_pos = index // f_ways
    side = index % f_ways
    width = gate_tile.shape[1] // D_WAYS
    rows = stream.shape[0]
    order = [0, 2, 4, 6, 7, 5, 3, 1]
    place = jnp.where(block_pos % 2 == 0, block_pos // 2, D_WAYS - 1 - block_pos // 2)

    def shift(value, step):
        pairs = [
            (order[p] * f_ways + f, order[(p + step) % D_WAYS] * f_ways + f)
            for p in range(D_WAYS)
            for f in range(f_ways)
        ]
        return lax.ppermute(value, "tp", pairs)

    def at(distance):
        return (place + distance + D_WAYS) % D_WAYS

    own_in = add_rows(token_ids, stream, table_rows)
    other_in = from_partner(own_in, "tp", 0)

    right, left, scaled, squares = first_up_block(
        jnp.stack([at(4), block_pos, side]), own_in, other_in, norm_gain[None], gate_tile, up_tile
    )
    split = LANES + width
    for distance in (3, 2, 1, 0):
        blocks = [at(distance), at(-distance)] if distance else [at(0)]
        own = up_blocks(scaled, squares, gate_tile, up_tile, blocks, [right, left])
        right, left = shift(right, 1), shift(left, -1)
        if distance == 3:
            right = jnp.concatenate([own[0][:, :split] + right.astype(F32), own[0][:, split:]], 1)
            left = jnp.concatenate([own[1][:, :split], own[1][:, split:] + left.astype(F32)], 1)
            right, left = right.astype(BF16), left.astype(BF16)
        elif distance:
            right = (own[0] + right.astype(F32)).astype(BF16)
            left = (own[1] + left.astype(F32)).astype(BF16)
        else:
            both = own[0] + right.astype(F32) + left.astype(F32)

    both, total_squares = both[:, LANES:], jnp.sum(both[:, :LANES], axis=1, keepdims=True)
    both = both * lax.rsqrt(total_squares / D + 1e-05)
    mine = (jax.nn.silu(both[:, :width]) * both[:, width:]).astype(BF16)

    half = rows // 2
    total = None
    right, left = mine, mine
    for distance in (0, 1, 2, 3):
        if distance == 3:
            next_right, next_left = shift(right[:half], 1), shift(left[half:], -1)
        else:
            next_right, next_left = shift(right, 1), shift(left, -1)
        if distance:
            total = down_blocks(total, [right, left], down_tile, [at(-distance), at(distance)])
        else:
            total = down_blocks(None, [mine], down_tile, [at(0)])
        right, left, total = lax.optimization_barrier((next_right, next_left, total))
    kept, sent = last_down_block(jnp.stack([at(4), side]), total, right, left, down_tile)
    summed = kept + from_partner(sent, "tp", 0).astype(F32)
    return (own_in.astype(F32) + summed).astype(BF16)


def on_device(stream, table_rows, token_ids, norm_gain, gate_weight, up_weight, down_weight):
    units = gate_weight.shape[2]
    fits = lax.axis_size("tp") == 2 * D_WAYS and units % (D_WAYS * LANES) == 0
    body = ring if fits else general
    current = body(
        stream, table_rows, token_ids, norm_gain, gate_weight[0], up_weight[0], down_weight[0]
    )
    return current[None]


def solution(mesh):
    placed = (
        P("groups", "tp"),
        P("groups", "tp"),
        P(None, "groups"),
        P(),
        P("tp", None, None),
        P("tp", None, None),
        P("tp", None, None),
    )
    return jax.shard_map(
        on_device, mesh=mesh, in_specs=placed, out_specs=P(None, "groups", "tp"), check_vma=False
    )
```

time: 659 us -> 88.7 us (0.13)
  waiting for transfers between devices: 582 us -> 20.9 us
  Pallas kernels: 0 us -> 45.2 us
  matrix products: 35.7 us -> 0 us
  other arithmetic: 24.1 us -> 2.18 us
    ppermute x8 -> x2, waiting for transfers between devices: 582 us -> 2.2 us  [from_partner(): return lax.ppermute(value, axis, pairs)]
    pallas_call x0 -> x11, Pallas kernels: none -> 45.2 us  [the longest x4 22.4 us: up_blocks(): pl.pallas_call(kernel, out_shape=[jax.ShapeDtypeStruct((rows, LANES + 2 *...]
    dot_general x3 -> x0, matrix products: 35.7 us -> none  [the longest x1 13 us: on_device(): jnp.dot(hidden, down_tile, preferred_element_type=jnp.float32)]
    add x5 -> x1, other arithmetic: 20.4 us -> 0.12 us  [ring(): both = own[0] + right.astype(F32) + left.astype(F32)]
    ppermute x0 -> x16, waiting for transfers between devices: none -> 18.7 us  [shift(): return lax.ppermute(value, 'tp', pairs)]
    ppermute x0 -> x16, starting transfers between devices: none -> 17.7 us  [shift(): return lax.ppermute(value, 'tp', pairs)]
    ppermute x8 -> x2, starting transfers between devices: 14.5 us -> 0.52 us  [from_partner(): return lax.ppermute(value, axis, pairs)]
  transfers between devices with their start and end apart: 8 -> 18, of which waited for: 8 -> 11; matrix products, arithmetic and copies ran while one was open for 0% -> 1% of each run, Pallas kernels for 0% -> 41%
where the time goes in v2:
time: 88.7 us; the launch traced here: 88.4 us
  Pallas kernels  45.2 us (51%)
  waiting for transfers between devices  20.9 us (24%)
  starting transfers between devices  18.2 us (21%)
  other arithmetic  2.18 us (2%)
  local copies, waits for them, and re-layouts  1.67 us (2%)
    pallas_call x4, Pallas kernels, up_blocks(): pl.pallas_call(kernel, out_shape=[jax.ShapeDtypeStruct((rows, LANES + 2 *...  22.4 us
    ppermute x16, waiting for transfers between devices, shift(): return lax.ppermute(value, 'tp', pairs)  18.7 us
    ppermute x16, starting transfers between devices, shift(): return lax.ppermute(value, 'tp', pairs)  17.7 us
    pallas_call x4, Pallas kernels, down_blocks(): pl.pallas_call(kernel, out_shape=jax.ShapeDtypeStruct((rows, width), F32)...  13.9 us
    pallas_call x1, Pallas kernels, first_up_block(): pl.pallas_call(kernel, out_shape=[jax.ShapeDtypeStruct((rows, LANES + wid...  4.09 us
    pallas_call x1, Pallas kernels, last_down_block(): pl.pallas_call(kernel, out_shape=[jax.ShapeDtypeStruct((rows, half), F32)...  2.81 us
    ppermute x2, waiting for transfers between devices, from_partner(): return lax.ppermute(value, axis, pairs)  2.2 us
    pallas_call x1, Pallas kernels, add_rows(): pl.pallas_call(kernel, out_shape=jax.ShapeDtypeStruct(stream.shape, BF16)...  1.96 us
  transfers between devices with their start and end apart: 18, of which 11 were waited for; matrix products, arithmetic and copies ran while one was open for 1% of the time, Pallas kernels for 41%

profile of v2, /device:TPU:0, one launch (start us, length us, event | category | flops | bytes accessed | tf_op | source)
XLA Modules:
  0.0 88.4 jit_solution(1074754187703646153)
XLA Ops:
  0.0 2.0 %add_rows.1.own_ref = bf16[64,512]{1,0:T(8,128)(2,1)} custom-call(s32[1,64]{1,0:T(1,128)} %ids_ref.1, bf16[64,512]{1,0:T(8,128)(2,1)} %stream_ref.1, bf16[512,512]{1,0:T(8,128)(2,1)} %table_ref.1), custom_call_target="tpu_custom_call" | custom-call | tf_op jit(solution)/shard_map/add_rows/pallas_call | solution.py:106
  5.1 4.1 %first_up_block.1 = (bf16[64,1792]{1,0:T(8,128)(2,1)S(1)}, bf16[64,1664]{1,0:T(8,128)(2,1)S(1)}, bf16[64,1024]{1,0:T(8,128)(2,1)S(1)}, f32[64,128]{1,0:T(8,128)S(1)}) custom-call(s32[3]{0:T(128)S(1)} %pad_add_fusion.1.scalars, bf16[64,512]{1,0:T(8,128)(2,1)S(1)} %copy-done, bf16[64,512]{1,0:T(8,128)(2,1)S(1)} %collective-permute-done.other_ref, ...), custom_call_target="tpu_custom_call" | custom-call | flops 436207616 | bytes 6815744 | tf_op jit(solution)/shard_map/first_up_block/pallas_call | solution.py:173
  9.2 2.9 %collective-permute-start.2 = (bf16[64,1664]{1,0:T(8,128)(2,1)S(1)}, bf16[64,1664]{1,0:T(8,128)(2,1)S(1)}, u32[]{:S(2)}, u32[]{:S(2)}) collective-permute-start(bf16[64,1664]{1,0:T(8,128)(2,1)S(1)} %get-tuple-element.32.rest_1_), channel_id=1, source_target_pairs={{0,2},{1,3},{4,0},{5,1},{8,4},{9,5},{12,8},{13,9},{14,12},{15,13},... | collective-permute-start | bytes 638984 | tf_op jit(solution)/shard_map/ppermute | solution.py:369
  12.4 6.3 %up_blocks.4 = (f32[64,3456]{1,0:T(8,128)S(1)}, f32[64,3456]{1,0:T(8,128)S(1)}) custom-call(s32[2]{0:T(128)S(1)} %pad_add_fusion.4.ids, bf16[64,1024]{1,0:T(8,128)(2,1)S(1)} %get-tuple-element.29.x_ref, f32[64,128]{1,0:T(8,128)S(1)} %get-tuple-element.30.squares_ref, bf16[1024,13312]{1,0:T(8,128)(2,1)} %bitcast.18, bf16[1024,13312]{1,0:T(8,128)(2,1)} %bitcast.23, ...), custom_call_target="tpu_custom_call" | custom-call | flops 872415232 | bytes 13631488 | tf_op jit(solution)/shard_map/up_blocks/pallas_call | solution.py:223
  18.8 2.0 %collective-permute-start.4 = (bf16[64,3456]{1,0:T(8,128)(2,1)S(1)}, bf16[64,3456]{1,0:T(8,128)(2,1)S(1)}, u32[]{:S(2)}, u32[]{:S(2)}) collective-permute-start(bf16[64,3456]{1,0:T(8,128)(2,1)S(1)} %pad_maximum_fusion.1.rest_1_), channel_id=1, source_target_pairs={{0,2},{1,3},{4,0},{5,1},{8,4},{9,5},{12,8},{13,9},{14,12},{15,13},... | collective-permute-start | bytes 1327112 | tf_op jit(solution)/shard_map/ppermute | solution.py:369
  21.1 6.3 %up_blocks.5 = (f32[64,3456]{1,0:T(8,128)S(1)}, f32[64,3456]{1,0:T(8,128)S(1)}) custom-call(s32[2]{0:T(128)S(1)} %pad_add_fusion.3.ids, bf16[64,1024]{1,0:T(8,128)(2,1)S(1)} %get-tuple-element.29.x_ref, f32[64,128]{1,0:T(8,128)S(1)} %get-tuple-element.30.squares_ref, bf16[1024,13312]{1,0:T(8,128)(2,1)} %bitcast.19, bf16[1024,13312]{1,0:T(8,128)(2,1)} %bitcast.24, ...), custom_call_target="tpu_custom_call" | custom-call | flops 872415232 | bytes 13631488 | tf_op jit(solution)/shard_map/up_blocks/pallas_call | solution.py:223
  27.4 3.5 %collective-permute-done.4 = bf16[64,3456]{1,0:T(8,128)(2,1)S(1)} collective-permute-done((bf16[64,3456]{1,0:T(8,128)(2,1)S(1)}, bf16[64,3456]{1,0:T(8,128)(2,1)S(1)}, u32[]{:S(2)}, u32[]{:S(2)}) %collective-permute-start.4) | collective-permute-done | bytes 442400 | tf_op jit(solution)/shard_map/ppermute | solution.py:369
  30.9 1.7 %collective-permute-start.6 = (bf16[64,3456]{1,0:T(8,128)(2,1)S(1)}, bf16[64,3456]{1,0:T(8,128)(2,1)S(1)}, u32[]{:S(2)}, u32[]{:S(2)}) collective-permute-start(bf16[64,3456]{1,0:T(8,128)(2,1)S(1)} %add_convert_fusion.2.rest_1_), channel_id=1, source_target_pairs={{0,2},{1,3},{4,0},{5,1},{8,4},{9,5},{12,8},{13,9},{14,12},{15,13},... | collective-permute-start | bytes 1327112 | tf_op jit(solution)/shard_map/ppermute | solution.py:369
  33.1 6.3 %up_blocks.6 = (f32[64,3456]{1,0:T(8,128)S(1)}, f32[64,3456]{1,0:T(8,128)S(1)}) custom-call(s32[2]{0:T(128)S(1)} %pad_add_fusion.2.ids, bf16[64,1024]{1,0:T(8,128)(2,1)S(1)} %get-tuple-element.29.x_ref, f32[64,128]{1,0:T(8,128)S(1)} %get-tuple-element.30.squares_ref, bf16[1024,13312]{1,0:T(8,128)(2,1)} %bitcast.20, bf16[1024,13312]{1,0:T(8,128)(2,1)} %bitcast.25, ...), custom_call_target="tpu_custom_call" | custom-call | flops 872415232 | bytes 13631488 | tf_op jit(solution)/shard_map/up_blocks/pallas_call | solution.py:223
  39.5 2.6 %collective-permute-done.6 = bf16[64,3456]{1,0:T(8,128)(2,1)S(1)} collective-permute-done((bf16[64,3456]{1,0:T(8,128)(2,1)S(1)}, bf16[64,3456]{1,0:T(8,128)(2,1)S(1)}, u32[]{:S(2)}, u32[]{:S(2)}) %collective-permute-start.6) | collective-permute-done | bytes 442400 | tf_op jit(solution)/shard_map/ppermute | solution.py:369
  42.1 1.4 %collective-permute-start.8 = (bf16[64,3456]{1,0:T(8,128)(2,1)S(1)}, bf16[64,3456]{1,0:T(8,128)(2,1)S(1)}, u32[]{:S(2)}, u32[]{:S(2)}) collective-permute-start(bf16[64,3456]{1,0:T(8,128)(2,1)S(1)} %add_convert_fusion.rest_1_), channel_id=1, source_target_pairs={{0,2},{1,3},{4,0},{5,1},{8,4},{9,5},{12,8},{13,9},{14,12},{15,13},... | collective-permute-start | bytes 1327112 | tf_op jit(solution)/shard_map/ppermute | solution.py:369
  44.4 3.5 %up_blocks.7 = f32[64,3456]{1,0:T(8,128)S(1)} custom-call(s32[1]{0:T(128)} %bitcast.2.ids, bf16[64,1024]{1,0:T(8,128)(2,1)S(1)} %get-tuple-element.29.x_ref, f32[64,128]{1,0:T(8,128)S(1)} %get-tuple-element.30.squares_ref, bf16[1024,13312]{1,0:T(8,128)(2,1)} %bitcast.21, bf16[1024,13312]{1,0:T(8,128)(2,1)} %bitcast.26, ...), custom_call_target="tpu_custom_call" | custom-call | flops 436207616 | bytes 6815744 | tf_op jit(solution)/shard_map/up_blocks/pallas_call | solution.py:223
  47.9 4.4 %collective-permute-done.8 = bf16[64,3456]{1,0:T(8,128)(2,1)S(1)} collective-permute-done((bf16[64,3456]{1,0:T(8,128)(2,1)S(1)}, bf16[64,3456]{1,0:T(8,128)(2,1)S(1)}, u32[]{:S(2)}, u32[]{:S(2)}) %collective-permute-start.8) | collective-permute-done | bytes 442400 | tf_op jit(solution)/shard_map/ppermute | solution.py:369
  53.7 1.6 %collective-permute-start.10 = (bf16[64,1664]{1,0:T(8,128)(2,1)S(1)}, bf16[64,1664]{1,0:T(8,128)(2,1)S(1)}, u32[]{:S(2)}, u32[]{:S(2)}) collective-permute-start(bf16[64,1664]{1,0:T(8,128)(2,1)S(1)} %fusion.rest_0_), channel_id=1, source_target_pairs={{0,2},{1,3},{4,0},{5,1},{8,4},{9,5},{12,8},{13,9},{14,12},{15,13},... | collective-permute-start | bytes 638984 | tf_op jit(solution)/shard_map/ppermute | solution.py:369
  55.8 2.3 %down_blocks.4.rest_0_ = f32[64,1024]{1,0:T(8,128)S(1)} custom-call(s32[1]{0:T(128)} %bitcast.2.ids, bf16[64,1664]{1,0:T(8,128)(2,1)S(1)} %fusion.rest_0_, bf16[13312,1024]{1,0:T(8,128)(2,1)} %bitcast.27), custom_call_target="tpu_custom_call" | custom-call | flops 218103808 | bytes 3407872 | tf_op jit(solution)/shard_map/down_blocks/pallas_call | solution.py:295
  58.1 1.9 %collective-permute-done.10.rest_2_ = bf16[64,1664]{1,0:T(8,128)(2,1)S(1)} collective-permute-done((bf16[64,1664]{1,0:T(8,128)(2,1)S(1)}, bf16[64,1664]{1,0:T(8,128)(2,1)S(1)}, u32[]{:S(2)}, u32[]{:S(2)}) %collective-permute-start.10) | collective-permute-done | bytes 213024 | tf_op jit(solution)/shard_map/ppermute | solution.py:369
  60.1 3.4 %collective-permute-done.9.rest_1_ = bf16[64,1664]{1,0:T(8,128)(2,1)S(1)} collective-permute-done((bf16[64,1664]{1,0:T(8,128)(2,1)S(1)}, bf16[64,1664]{1,0:T(8,128)(2,1)S(1)}, u32[]{:S(2)}, u32[]{:S(2)}) %collective-permute-start.9) | collective-permute-done | bytes 213024 | tf_op jit(solution)/shard_map/ppermute | solution.py:369
  63.9 1.6 %collective-permute-start.12 = (bf16[64,1664]{1,0:T(8,128)(2,1)S(1)}, bf16[64,1664]{1,0:T(8,128)(2,1)S(1)}, u32[]{:S(2)}, u32[]{:S(2)}) collective-permute-start(bf16[64,1664]{1,0:T(8,128)(2,1)S(1)} %collective-permute-done.10.rest_2_), channel_id=1, source_target_pairs={{0,2},{1,3},{4,0},{5,1},{8,4},{9,5},{12,8},{13,9},{14,12},{15,13},... | collective-permute-start | bytes 638984 | tf_op jit(solution)/shard_map/ppermute | solution.py:369
  65.6 3.9 %down_blocks.5.rest_0_ = f32[64,1024]{1,0:T(8,128)S(1)} custom-call(s32[2]{0:T(128)S(1)} %pad_add_fusion.5.ids, f32[64,1024]{1,0:T(8,128)S(1)} %down_blocks.4.rest_0_, bf16[64,1664]{1,0:T(8,128)(2,1)S(1)} %collective-permute-done.9.rest_1_, bf16[64,1664]{1,0:T(8,128)(2,1)S(1)} %collective-permute-done.10.rest_2_, bf16[13312,1024]{1,0:T(8,128)(2,1)} %bitcast.28), custom_call_target="tpu_custom_call" | custom-call | flops 436207616 | bytes 6815744 | tf_op jit(solution)/shard_map/down_blocks/pallas_call | solution.py:295
  69.4 1.3 %collective-permute-done.11.rest_1_ = bf16[64,1664]{1,0:T(8,128)(2,1)S(1)} collective-permute-done((bf16[64,1664]{1,0:T(8,128)(2,1)S(1)}, bf16[64,1664]{1,0:T(8,128)(2,1)S(1)}, u32[]{:S(2)}, u32[]{:S(2)}) %collective-permute-start.11) | collective-permute-done | bytes 213024 | tf_op jit(solution)/shard_map/ppermute | solution.py:369
  73.1 3.9 %down_blocks.6.rest_0_ = f32[64,1024]{1,0:T(8,128)S(1)} custom-call(s32[2]{0:T(128)S(1)} %pad_add_fusion.6.ids, f32[64,1024]{1,0:T(8,128)S(1)} %down_blocks.5.rest_0_, bf16[64,1664]{1,0:T(8,128)(2,1)S(1)} %collective-permute-done.11.rest_1_, bf16[64,1664]{1,0:T(8,128)(2,1)S(1)} %collective-permute-done.12.rest_2_, bf16[13312,1024]{1,0:T(8,128)(2,1)} %bitcast.29), custom_call_target="tpu_custom_call" | custom-call | flops 436207616 | bytes 6815744 | tf_op jit(solution)/shard_map/down_blocks/pallas_call | solution.py:295
  77.5 1.4 %collective-permute-start.15 = (bf16[32,1664]{1,0:T(8,128)(2,1)S(1)}, bf16[32,1664]{1,0:T(8,128)(2,1)S(1)}, u32[]{:S(2)}, u32[]{:S(2)}) collective-permute-start(bf16[32,1664]{1,0:T(8,128)(2,1)S(1)} %slice.40), channel_id=1, source_target_pairs={{0,4},{1,5},{4,8},{5,9},{8,12},{9,13},{12,14},{13,15},{14,10},{15,... | collective-permute-start | bytes 319496 | tf_op jit(solution)/shard_map/ppermute | solution.py:369
  79.7 3.9 %down_blocks.7.total_ref = f32[64,1024]{1,0:T(8,128)S(1)} custom-call(s32[2]{0:T(128)S(1)} %pad_add_fusion.7.ids, f32[64,1024]{1,0:T(8,128)S(1)} %down_blocks.6.rest_0_, bf16[64,1664]{1,0:T(8,128)(2,1)S(1)} %collective-permute-done.13.rest_1_, bf16[64,1664]{1,0:T(8,128)(2,1)S(1)} %collective-permute-done.14.rest_2_, bf16[13312,1024]{1,0:T(8,128)(2,1)} %bitcast.30), custom_call_target="tpu_custom_call" | custom-call | flops 436207616 | bytes 6815744 | tf_op jit(solution)/shard_map/down_blocks/pallas_call | solution.py:295
  83.6 2.8 %last_down_block.1 = (f32[64,512]{1,0:T(8,128)S(1)}, bf16[64,512]{1,0:T(8,128)(2,1)S(1)}) custom-call(s32[2]{0:T(128)S(1)} %pad_add_fusion.scalars, f32[64,1024]{1,0:T(8,128)S(1)} %down_blocks.7.total_ref, bf16[32,1664]{1,0:T(8,128)(2,1)S(1)} %collective-permute-done.15.upper_ref, bf16[32,1664]{1,0:T(8,128)(2,1)S(1)} %collective-permute-done.16.lower_ref, ...), custom_call_target="tpu_custom_call" | custom-call | flops 218103808 | bytes 3407872 | tf_op jit(solution)/shard_map/last_down_block/pallas_call | solution.py:329
  (55 shorter events, 13.3 us)
Async XLA Ops:
  2.0 1.6 %collective-permute-start = (bf16[64,512]{1,0:T(8,128)(2,1)}, bf16[64,512]{1,0:T(8,128)(2,1)S(1)}, u32[]{:S(2)}, u32[]{:S(2)}) collective-permute-start(bf16[64,512]{1,0:T(8,128)(2,1)} %add_rows.1.own_ref), channel_id=1, source_target_pairs={{0,1},{1,0},{2,3},{3,2},{4,5},{5,4},{6,7},{7,6},{8,9},{9,8},{10,11... | collective-permute-start | bytes 196616 | tf_op jit(solution)/shard_map/ppermute | solution.py:22
  3.5 0.8 copy-start
  4.4 0.8 copy-start.2
  9.2 9.5 %collective-permute-start.2 = (bf16[64,1664]{1,0:T(8,128)(2,1)S(1)}, bf16[64,1664]{1,0:T(8,128)(2,1)S(1)}, u32[]{:S(2)}, u32[]{:S(2)}) collective-permute-start(bf16[64,1664]{1,0:T(8,128)(2,1)S(1)} %get-tuple-element.32.rest_1_), channel_id=1, source_target_pairs={{0,2},{1,3},{4,0},{5,1},{8,4},{9,5},{12,8},{13,9},{14,12},{15,13},... | collective-permute-start | bytes 638984 | tf_op jit(solution)/shard_map/ppermute | solution.py:369
  12.3 8.6 %collective-permute-start.1 = (bf16[64,1792]{1,0:T(8,128)(2,1)S(1)}, bf16[64,1792]{1,0:T(8,128)(2,1)S(1)}, u32[]{:S(2)}, u32[]{:S(2)}) collective-permute-start(bf16[64,1792]{1,0:T(8,128)(2,1)S(1)} %get-tuple-element.31.rest_0_), channel_id=1, source_target_pairs={{0,4},{1,5},{4,8},{5,9},{8,12},{9,13},{12,14},{13,15},{14,10},{15,... | collective-permute-start | bytes 688136 | tf_op jit(solution)/shard_map/ppermute | solution.py:369
  18.8 12.0 %collective-permute-start.4 = (bf16[64,3456]{1,0:T(8,128)(2,1)S(1)}, bf16[64,3456]{1,0:T(8,128)(2,1)S(1)}, u32[]{:S(2)}, u32[]{:S(2)}) collective-permute-start(bf16[64,3456]{1,0:T(8,128)(2,1)S(1)} %pad_maximum_fusion.1.rest_1_), channel_id=1, source_target_pairs={{0,2},{1,3},{4,0},{5,1},{8,4},{9,5},{12,8},{13,9},{14,12},{15,13},... | collective-permute-start | bytes 1327112 | tf_op jit(solution)/shard_map/ppermute | solution.py:369
  20.9 11.7 %collective-permute-start.3 = (bf16[64,3456]{1,0:T(8,128)(2,1)S(1)}, bf16[64,3456]{1,0:T(8,128)(2,1)S(1)}, u32[]{:S(2)}, u32[]{:S(2)}) collective-permute-start(bf16[64,3456]{1,0:T(8,128)(2,1)S(1)} %pad_maximum_fusion.rest_0_), channel_id=1, source_target_pairs={{0,4},{1,5},{4,8},{5,9},{8,12},{9,13},{12,14},{13,15},{14,10},{15,... | collective-permute-start | bytes 1327112 | tf_op jit(solution)/shard_map/ppermute | solution.py:369
  30.9 11.1 %collective-permute-start.6 = (bf16[64,3456]{1,0:T(8,128)(2,1)S(1)}, bf16[64,3456]{1,0:T(8,128)(2,1)S(1)}, u32[]{:S(2)}, u32[]{:S(2)}) collective-permute-start(bf16[64,3456]{1,0:T(8,128)(2,1)S(1)} %add_convert_fusion.2.rest_1_), channel_id=1, source_target_pairs={{0,2},{1,3},{4,0},{5,1},{8,4},{9,5},{12,8},{13,9},{14,12},{15,13},... | collective-permute-start | bytes 1327112 | tf_op jit(solution)/shard_map/ppermute | solution.py:369
  32.7 10.8 %collective-permute-start.5 = (bf16[64,3456]{1,0:T(8,128)(2,1)S(1)}, bf16[64,3456]{1,0:T(8,128)(2,1)S(1)}, u32[]{:S(2)}, u32[]{:S(2)}) collective-permute-start(bf16[64,3456]{1,0:T(8,128)(2,1)S(1)} %add_convert_fusion.3.rest_0_), channel_id=1, source_target_pairs={{0,4},{1,5},{4,8},{5,9},{8,12},{9,13},{12,14},{13,15},{14,10},{15,... | collective-permute-start | bytes 1327112 | tf_op jit(solution)/shard_map/ppermute | solution.py:369
  42.1 10.2 %collective-permute-start.8 = (bf16[64,3456]{1,0:T(8,128)(2,1)S(1)}, bf16[64,3456]{1,0:T(8,128)(2,1)S(1)}, u32[]{:S(2)}, u32[]{:S(2)}) collective-permute-start(bf16[64,3456]{1,0:T(8,128)(2,1)S(1)} %add_convert_fusion.rest_1_), channel_id=1, source_target_pairs={{0,2},{1,3},{4,0},{5,1},{8,4},{9,5},{12,8},{13,9},{14,12},{15,13},... | collective-permute-start | bytes 1327112 | tf_op jit(solution)/shard_map/ppermute | solution.py:369
  43.6 9.6 %collective-permute-start.7 = (bf16[64,3456]{1,0:T(8,128)(2,1)S(1)}, bf16[64,3456]{1,0:T(8,128)(2,1)S(1)}, u32[]{:S(2)}, u32[]{:S(2)}) collective-permute-start(bf16[64,3456]{1,0:T(8,128)(2,1)S(1)} %add_convert_fusion.1.rest_0_), channel_id=1, source_target_pairs={{0,4},{1,5},{4,8},{5,9},{8,12},{9,13},{12,14},{13,15},{14,10},{15,... | collective-permute-start | bytes 1327112 | tf_op jit(solution)/shard_map/ppermute | solution.py:369
  53.7 6.4 %collective-permute-start.10 = (bf16[64,1664]{1,0:T(8,128)(2,1)S(1)}, bf16[64,1664]{1,0:T(8,128)(2,1)S(1)}, u32[]{:S(2)}, u32[]{:S(2)}) collective-permute-start(bf16[64,1664]{1,0:T(8,128)(2,1)S(1)} %fusion.rest_0_), channel_id=1, source_target_pairs={{0,2},{1,3},{4,0},{5,1},{8,4},{9,5},{12,8},{13,9},{14,12},{15,13},... | collective-permute-start | bytes 638984 | tf_op jit(solution)/shard_map/ppermute | solution.py:369
  55.4 8.1 %collective-permute-start.9 = (bf16[64,1664]{1,0:T(8,128)(2,1)S(1)}, bf16[64,1664]{1,0:T(8,128)(2,1)S(1)}, u32[]{:S(2)}, u32[]{:S(2)}) collective-permute-start(bf16[64,1664]{1,0:T(8,128)(2,1)S(1)} %fusion.rest_0_), channel_id=1, source_target_pairs={{0,4},{1,5},{4,8},{5,9},{8,12},{9,13},{12,14},{13,15},{14,10},{15,... | collective-permute-start | bytes 638984 | tf_op jit(solution)/shard_map/ppermute | solution.py:369
  63.5 7.3 %collective-permute-start.11 = (bf16[64,1664]{1,0:T(8,128)(2,1)S(1)}, bf16[64,1664]{1,0:T(8,128)(2,1)S(1)}, u32[]{:S(2)}, u32[]{:S(2)}) collective-permute-start(bf16[64,1664]{1,0:T(8,128)(2,1)S(1)} %collective-permute-done.9.rest_1_), channel_id=1, source_target_pairs={{0,4},{1,5},{4,8},{5,9},{8,12},{9,13},{12,14},{13,15},{14,10},{15,... | collective-permute-start | bytes 638984 | tf_op jit(solution)/shard_map/ppermute | solution.py:369
  63.9 7.0 %collective-permute-start.12 = (bf16[64,1664]{1,0:T(8,128)(2,1)S(1)}, bf16[64,1664]{1,0:T(8,128)(2,1)S(1)}, u32[]{:S(2)}, u32[]{:S(2)}) collective-permute-start(bf16[64,1664]{1,0:T(8,128)(2,1)S(1)} %collective-permute-done.10.rest_2_), channel_id=1, source_target_pairs={{0,2},{1,3},{4,0},{5,1},{8,4},{9,5},{12,8},{13,9},{14,12},{15,13},... | collective-permute-start | bytes 638984 | tf_op jit(solution)/shard_map/ppermute | solution.py:369
  70.9 6.1 %collective-permute-start.13 = (bf16[64,1664]{1,0:T(8,128)(2,1)S(1)}, bf16[64,1664]{1,0:T(8,128)(2,1)S(1)}, u32[]{:S(2)}, u32[]{:S(2)}) collective-permute-start(bf16[64,1664]{1,0:T(8,128)(2,1)S(1)} %collective-permute-done.11.rest_1_), channel_id=1, source_target_pairs={{0,4},{1,5},{4,8},{5,9},{8,12},{9,13},{12,14},{13,15},{14,10},{15,... | collective-permute-start | bytes 638984 | tf_op jit(solution)/shard_map/ppermute | solution.py:369
  71.7 5.8 %collective-permute-start.14 = (bf16[64,1664]{1,0:T(8,128)(2,1)S(1)}, bf16[64,1664]{1,0:T(8,128)(2,1)S(1)}, u32[]{:S(2)}, u32[]{:S(2)}) collective-permute-start(bf16[64,1664]{1,0:T(8,128)(2,1)S(1)} %collective-permute-done.12.rest_2_), channel_id=1, source_target_pairs={{0,2},{1,3},{4,0},{5,1},{8,4},{9,5},{12,8},{13,9},{14,12},{15,13},... | collective-permute-start | bytes 638984 | tf_op jit(solution)/shard_map/ppermute | solution.py:369
  77.5 6.1 %collective-permute-start.15 = (bf16[32,1664]{1,0:T(8,128)(2,1)S(1)}, bf16[32,1664]{1,0:T(8,128)(2,1)S(1)}, u32[]{:S(2)}, u32[]{:S(2)}) collective-permute-start(bf16[32,1664]{1,0:T(8,128)(2,1)S(1)} %slice.40), channel_id=1, source_target_pairs={{0,4},{1,5},{4,8},{5,9},{8,12},{9,13},{12,14},{13,15},{14,10},{15,... | collective-permute-start | bytes 319496 | tf_op jit(solution)/shard_map/ppermute | solution.py:369
  78.9 4.8 %collective-permute-start.16 = (bf16[32,1664]{1,0:T(8,128)(2,1)S(1)}, bf16[32,1664]{1,0:T(8,128)(2,1)S(1)}, u32[]{:S(2)}, u32[]{:S(2)}) collective-permute-start(bf16[32,1664]{1,0:T(8,128)(2,1)S(1)} %slice.41), channel_id=1, source_target_pairs={{0,2},{1,3},{4,0},{5,1},{8,4},{9,5},{12,8},{13,9},{14,12},{15,13},... | collective-permute-start | bytes 319496 | tf_op jit(solution)/shard_map/ppermute | solution.py:369
  79.7 8.0 %copy-start.1 = (bf16[64,512]{1,0:T(8,128)(2,1)S(1)}, bf16[64,512]{1,0:T(8,128)(2,1)}, u32[]{:S(2)}) copy-start(bf16[64,512]{1,0:T(8,128)(2,1)} %add_rows.1.own_ref) | copy-start | bytes 196612
  86.5 1.3 %collective-permute-start.17 = (bf16[64,512]{1,0:T(8,128)(2,1)S(1)}, bf16[64,512]{1,0:T(8,128)(2,1)S(1)}, u32[]{:S(2)}, u32[]{:S(2)}) collective-permute-start(bf16[64,512]{1,0:T(8,128)(2,1)S(1)} %get-tuple-element.52), channel_id=1, source_target_pairs={{0,1},{1,0},{2,3},{3,2},{4,5},{5,4},{6,7},{7,6},{8,9},{9,8},{10,11... | collective-permute-start | bytes 196616 | tf_op jit(solution)/shard_map/ppermute | solution.py:22

commit v3 on v2

v3 whole, which is shorter than its diff:
```python
import jax
import jax.numpy as jnp
from jax import lax
from jax.experimental import pallas as pl
from jax.experimental.pallas import tpu as pltpu
from jax.sharding import PartitionSpec as P

D = 8192
D_WAYS = 8
LANES = 128
DOWN_CHUNK = 896
VMEM_LIMIT = 32 * 2**20
BF16 = jnp.bfloat16
F32 = jnp.float32
IN_VMEM = pl.BlockSpec(memory_space=pltpu.VMEM)
IN_PLACE = pl.BlockSpec(memory_space=pl.ANY)


def from_partner(value, axis, distance):
    mask = 2**distance
    pairs = [(source, source ^ mask) for source in range(lax.axis_size(axis))]
    return lax.ppermute(value, axis, pairs)


def bit_high(index, bit):
    return index // 2**bit % 2 == 1


def gather_block(local_rows, index, low_bits):
    piece = local_rows
    for bit in range(low_bits):
        other = from_partner(piece, "tp", bit)
        piece = jnp.where(
            bit_high(index, bit),
            jnp.concatenate([other, piece], 1),
            jnp.concatenate([piece, other], 1),
        )
    return piece


def halve_columns(values, index, bit):
    width = values.shape[-1] // 2
    lower = values[..., :width]
    upper = values[..., width:]
    high = bit_high(index, bit)
    return (jnp.where(high, upper, lower), jnp.where(high, lower, upper))


def sum_blocks(partial_value, index, low_bits):
    for bit in reversed(range(low_bits)):
        kept, sent = halve_columns(partial_value, index, bit)
        partial_value = kept + from_partner(sent.astype(BF16), "tp", bit).astype(sent.dtype)
    return partial_value


def general(stream, table_rows, token_ids, norm_gain, gate_tile, up_tile, down_tile):
    f_ways = lax.axis_size("tp") // D_WAYS
    low_bits = f_ways.bit_length() - 1
    high_bits = D_WAYS.bit_length() - 1
    index = lax.axis_index("tp")
    block_pos = index // f_ways
    width = gate_tile.shape[0]
    gain_block = lax.dynamic_slice_in_dim(norm_gain, block_pos * width, width)
    picked = jnp.take(table_rows, token_ids[0], axis=0)
    block_in = (stream.astype(F32) + picked.astype(F32)).astype(BF16)
    feature_block = gather_block(block_in, index, low_bits).astype(F32)
    total = jnp.sum(feature_block * feature_block, axis=1)
    for level in range(high_bits):
        total = total + from_partner(total, "tp", low_bits + level)
    scale_rows = lax.rsqrt(total[:, None] / D + 1e-05)
    normed = (feature_block * scale_rows * gain_block[None, :]).astype(BF16)
    pair = jnp.stack(
        [
            jnp.dot(normed, gate_tile, preferred_element_type=F32),
            jnp.dot(normed, up_tile, preferred_element_type=F32),
        ],
        axis=0,
    )
    for level in range(high_bits):
        pair = pair + from_partner(pair, "tp", low_bits + level)
    hidden = (jax.nn.silu(pair[0]) * pair[1]).astype(BF16)
    partial_value = jnp.dot(hidden, down_tile, preferred_element_type=F32)
    summed = sum_blocks(partial_value, index, low_bits)
    return (block_in.astype(F32) + summed).astype(BF16)


def params():
    return pltpu.CompilerParams(vmem_limit_bytes=VMEM_LIMIT)


def position():
    index = lax.axis_index("tp")
    block = lax.shift_right_logical(index, 1)
    half = lax.shift_right_logical(block, 1)
    place = jnp.where((block & 1) == 0, half, D_WAYS - 1 - half)
    return block, index & 1, place


def at(place, distance):
    return (place + distance + D_WAYS) & (D_WAYS - 1)


def add_rows(token_ids, stream, table_rows, gain):
    entries = table_rows.shape[0]
    rows, share = stream.shape

    def kernel(ids_ref, stream_ref, table_ref, gain_ref, out_ref, message_ref, gains, arrived):
        place = pl.multiple_of(lax.axis_index("tp") * share, LANES)
        copy = pltpu.make_async_copy(gain_ref.at[:, pl.ds(place, share)], gains, arrived)
        copy.start()
        row = lax.broadcasted_iota(jnp.int32, (rows, rows), 0)
        column = lax.broadcasted_iota(jnp.int32, (rows, rows), 1)
        across = jnp.broadcast_to(ids_ref[...].astype(F32), (rows, rows))
        ids = jnp.sum(jnp.where(row == column, across, 0.0), axis=1, keepdims=True).astype(jnp.int32)
        entry = lax.broadcasted_iota(jnp.int32, (rows, entries), 1)
        chosen = jnp.where(entry == ids, 1.0, 0.0).astype(BF16)
        picked = jnp.dot(chosen, table_ref[...], preferred_element_type=F32)
        value = (stream_ref[...].astype(F32) + picked).astype(BF16)
        out_ref[...] = value
        value = value.astype(F32)
        squares = jnp.zeros((rows, LANES), F32)
        for lane in range(0, share, LANES):
            squares += value[:, lane : lane + LANES] * value[:, lane : lane + LANES]
        message_ref[:, share:] = squares.astype(BF16)
        copy.wait()
        message_ref[:, :share] = (value * gains[...]).astype(BF16)

    return pl.pallas_call(
        kernel,
        out_shape=[
            jax.ShapeDtypeStruct((rows, share), BF16),
            jax.ShapeDtypeStruct((rows, share + LANES), BF16),
        ],
        in_specs=[IN_VMEM] * 3 + [IN_PLACE],
        out_specs=[IN_VMEM] * 2,
        scratch_shapes=[pltpu.VMEM((1, share), F32), pltpu.SemaphoreType.DMA],
        name="add_rows",
    )(token_ids, stream, table_rows, gain)


def start_up_copies(block, gate_ref, up_ref, tiles, arrived):
    cuts = arrived.shape[1]
    cut = gate_ref.shape[0] // cuts
    width = gate_ref.shape[1] // D_WAYS
    columns = pl.ds(pl.multiple_of(block * width, LANES), width)
    copies = []
    for m, ref in enumerate((gate_ref, up_ref)):
        for c in range(cuts):
            features = slice(c * cut, (c + 1) * cut)
            copy = pltpu.make_async_copy(
                ref.at[pl.ds(c * cut, cut), columns], tiles.at[m, pl.ds(c * cut, cut), :], arrived.at[m, c]
            )
            copy.start()
            copies.append((m, features, copy))
    return copies


def up_products(x_ref, copies, tiles, out_refs):
    for m, features, copy in copies:
        copy.wait()
        product = jnp.dot(x_ref[:, features], tiles[m, features, :], preferred_element_type=F32)
        if features.start == 0:
            out_refs[m][...] = product
        else:
            out_refs[m][...] += product


def up_scratch(count, depth, width):
    cuts = 2
    return [
        pltpu.VMEM((count, 2, depth, width), BF16),
        pltpu.SemaphoreType.DMA((count, 2, cuts)),
    ]


def up_cost(count, rows, depth, width):
    return pl.CostEstimate(
        flops=4 * count * rows * depth * width,
        bytes_accessed=4 * count * depth * width,
        transcendentals=0,
    )


def first_up_block(own, other, gate_tile, up_tile):
    depth, units = gate_tile.shape
    width = units // D_WAYS
    rows = own.shape[0]
    share = own.shape[1] - LANES

    def kernel(own_ref, other_ref, gate_ref, up_ref, gate_out, up_out, x_ref, squares_ref, products, tiles, arrived):
        _, side, place = position()
        copies = start_up_copies(at(place, 4), gate_ref, up_ref, tiles.at[0], arrived.at[0])
        high = side == 1
        own_x, other_x = own_ref[:, :share], other_ref[:, :share]
        x_ref[:, :share] = jnp.where(high, other_x, own_x)
        x_ref[:, share:] = jnp.where(high, own_x, other_x)
        squares = own_ref[:, share:].astype(F32) + other_ref[:, share:].astype(F32)
        squares_ref[...] = squares
        gate_out[:, :LANES] = squares.astype(BF16)
        up_products(x_ref, copies, tiles.at[0], [products.at[0], products.at[1]])
        gate_out[:, LANES:] = products[0].astype(BF16)
        up_out[...] = products[1].astype(BF16)

    return pl.pallas_call(
        kernel,
        out_shape=[
            jax.ShapeDtypeStruct((rows, LANES + width), BF16),
            jax.ShapeDtypeStruct((rows, width), BF16),
            jax.ShapeDtypeStruct((rows, depth), BF16),
            jax.ShapeDtypeStruct((rows, LANES), F32),
        ],
        in_specs=[IN_VMEM] * 2 + [IN_PLACE] * 2,
        out_specs=[IN_VMEM] * 4,
        scratch_shapes=[pltpu.VMEM((2, rows, width), F32)] + up_scratch(1, depth, width),
        compiler_params=params(),
        cost_estimate=up_cost(1, rows, depth, width),
        name="first_up_block",
    )(own, other, gate_tile, up_tile)


def up_blocks(x, squares, gate_tile, up_tile, distances, after):
    depth, units = gate_tile.shape
    width = units // D_WAYS
    rows = x.shape[0]
    count = len(distances)

    def kernel(x_ref, squares_ref, gate_ref, up_ref, *rest):
        out_refs = rest[len(after) : len(after) + count]
        tiles, arrived = rest[-2:]
        _, _, place = position()
        copies = [
            start_up_copies(at(place, distance), gate_ref, up_ref, tiles.at[j], arrived.at[j])
            for j, distance in enumerate(distances)
        ]
        for j, out_ref in enumerate(out_refs):
            out_ref[:, :LANES] = squares_ref[...]
            pair = [out_ref.at[:, pl.ds(LANES, width)], out_ref.at[:, pl.ds(LANES + width, width)]]
            up_products(x_ref, copies[j], tiles.at[j], pair)

    return pl.pallas_call(
        kernel,
        out_shape=[jax.ShapeDtypeStruct((rows, LANES + 2 * width), F32)] * count,
        in_specs=[IN_VMEM] * 2 + [IN_PLACE] * (2 + len(after)),
        out_specs=[IN_VMEM] * count,
        scratch_shapes=up_scratch(count, depth, width),
        compiler_params=params(),
        cost_estimate=up_cost(count, rows, depth, width),
        name="up_blocks",
    )(x, squares, gate_tile, up_tile, *after)


def down_chunks(depth):
    return [(start, min(DOWN_CHUNK, depth - start)) for start in range(0, depth, DOWN_CHUNK)]


def start_down_copies(block, down_ref, tiles, arrived):
    depth = down_ref.shape[0] // D_WAYS
    copies = []
    for c, (start, size) in enumerate(down_chunks(depth)):
        copy = pltpu.make_async_copy(
            down_ref.at[pl.ds(pl.multiple_of(block * depth + start, LANES), size), :],
            tiles.at[pl.ds(start, size), :],
            arrived.at[c],
        )
        copy.start()
        copies.append((start, size, copy))
    return copies


def down_products(value, hidden_ref, copies, tiles):
    for start, size, copy in copies:
        copy.wait()
        value = value + jnp.dot(
            hidden_ref[:, start : start + size],
            tiles[start : start + size, :],
            preferred_element_type=F32,
        )
    return value


def down_cost(count, rows, depth, width):
    return pl.CostEstimate(
        flops=2 * count * rows * depth * width,
        bytes_accessed=2 * count * depth * width,
        transcendentals=0,
    )


def down_blocks(total, hidden, down_tile, distances, fetch=None):
    units, width = down_tile.shape
    depth = units // D_WAYS
    rows = hidden[0].shape[0]
    count = len(distances)
    totals = [] if total is None else [total]
    fetches = 0 if fetch is None else 1

    def kernel(*rest):
        hidden_refs = rest[len(totals) : len(totals) + count]
        down_ref, out_ref, *fetched, tiles, arrived = rest[len(totals) + count :]
        _, _, place = position()
        copies = [
            start_down_copies(at(place, distance), down_ref, tiles.at[j], arrived.at[j])
            for j, distance in enumerate(distances)
        ]
        ahead = [start_down_copies(at(place, fetch), down_ref, ref, arrived.at[count]) for ref in fetched]
        value = rest[0][...] if totals else jnp.zeros((rows, width), F32)
        for j in range(count):
            value = down_products(value, hidden_refs[j], copies[j], tiles.at[j])
        out_ref[...] = value
        for pieces in ahead:
            for _, _, copy in pieces:
                copy.wait()

    return pl.pallas_call(
        kernel,
        out_shape=[jax.ShapeDtypeStruct((rows, width), F32)]
        + [jax.ShapeDtypeStruct((depth, width), BF16)] * fetches,
        in_specs=[IN_VMEM] * (len(totals) + count) + [IN_PLACE],
        out_specs=[IN_VMEM] * (1 + fetches),
        scratch_shapes=[
            pltpu.VMEM((count, depth, width), BF16),
            pltpu.SemaphoreType.DMA((count + fetches, len(down_chunks(depth)))),
        ],
        compiler_params=params(),
        cost_estimate=down_cost(count + fetches, rows, depth, width),
        name="down_blocks",
    )(*totals, *hidden, down_tile)


def last_down_block(total, upper, lower, tile):
    depth, width = tile.shape
    rows = total.shape[0]
    half = width // 2

    def kernel(total_ref, upper_ref, lower_ref, tile_ref, kept_ref, sent_ref, hidden):
        _, side, _ = position()
        hidden[: rows // 2] = upper_ref[...]
        hidden[rows // 2 :] = lower_ref[...]
        value = total_ref[...] + jnp.dot(hidden[...], tile_ref[...], preferred_element_type=F32)
        high = side == 1
        kept_ref[...] = jnp.where(high, value[:, half:], value[:, :half])
        sent_ref[...] = jnp.where(high, value[:, :half], value[:, half:]).astype(BF16)

    return pl.pallas_call(
        kernel,
        out_shape=[
            jax.ShapeDtypeStruct((rows, half), F32),
            jax.ShapeDtypeStruct((rows, half), BF16),
        ],
        in_specs=[IN_VMEM] * 4,
        out_specs=[IN_VMEM] * 2,
        scratch_shapes=[pltpu.VMEM((rows, depth), BF16)],
        compiler_params=params(),
        cost_estimate=down_cost(1, rows, depth, width),
        name="last_down_block",
    )(total, upper, lower, tile)


def ring(stream, table_rows, token_ids, norm_gain, gate_tile, up_tile, down_tile):
    f_ways = lax.axis_size("tp") // D_WAYS
    width = gate_tile.shape[1] // D_WAYS
    rows = stream.shape[0]
    order = [0, 2, 4, 6, 7, 5, 3, 1]

    def shift(value, step):
        pairs = [
            (order[p] * f_ways + f, order[(p + step) % D_WAYS] * f_ways + f)
            for p in range(D_WAYS)
            for f in range(f_ways)
        ]
        return lax.ppermute(value, "tp", pairs)

    block_in, own = add_rows(token_ids, stream, table_rows, norm_gain[None])
    other = from_partner(own, "tp", 0)

    right, left, scaled, squares = first_up_block(own, other, gate_tile, up_tile)
    split = LANES + width
    for distance in (3, 2, 1, 0):
        distances = [distance, -distance] if distance else [0]
        own = up_blocks(scaled, squares, gate_tile, up_tile, distances, [right, left])
        right, left = shift(right, 1), shift(left, -1)
        if distance == 3:
            right = jnp.concatenate([own[0][:, :split] + right.astype(F32), own[0][:, split:]], 1)
            left = jnp.concatenate([own[1][:, :split], own[1][:, split:] + left.astype(F32)], 1)
            right, left = right.astype(BF16), left.astype(BF16)
        elif distance:
            right = (own[0] + right.astype(F32)).astype(BF16)
            left = (own[1] + left.astype(F32)).astype(BF16)
        else:
            both = own[0] + right.astype(F32) + left.astype(F32)

    both, total_squares = both[:, LANES:], jnp.sum(both[:, :LANES], axis=1, keepdims=True)
    both = both * lax.rsqrt(total_squares / D + 1e-05)
    mine = (jax.nn.silu(both[:, :width]) * both[:, width:]).astype(BF16)

    half = rows // 2
    total = None
    right, left = mine, mine
    for distance in (0, 1, 2, 3):
        if distance == 3:
            next_right, next_left = shift(right[:half], 1), shift(left[half:], -1)
        else:
            next_right, next_left = shift(right, 1), shift(left, -1)
        if distance == 3:
            total, far_tile = down_blocks(total, [right, left], down_tile, [-3, 3], fetch=4)
        elif distance:
            (total,) = down_blocks(total, [right, left], down_tile, [-distance, distance])
        else:
            (total,) = down_blocks(None, [mine], down_tile, [0])
        right, left, total = lax.optimization_barrier((next_right, next_left, total))
    kept, sent = last_down_block(total, right, left, far_tile)
    summed = kept + from_partner(sent, "tp", 0).astype(F32)
    return (block_in.astype(F32) + summed).astype(BF16)


def on_device(stream, table_rows, token_ids, norm_gain, gate_weight, up_weight, down_weight):
    units = gate_weight.shape[2]
    fits = lax.axis_size("tp") == 2 * D_WAYS and units % (D_WAYS * LANES) == 0
    body = ring if fits else general
    current = body(
        stream, table_rows, token_ids, norm_gain, gate_weight[0], up_weight[0], down_weight[0]
    )
    return current[None]


def solution(mesh):
    placed = (
        P("groups", "tp"),
        P("groups", "tp"),
        P(None, "groups"),
        P(),
        P("tp", None, None),
        P("tp", None, None),
        P("tp", None, None),
    )
    return jax.shard_map(
        on_device, mesh=mesh, in_specs=placed, out_specs=P(None, "groups", "tp"), check_vma=False
    )
```

time: 88.7 us -> 85 us (0.958)
  Pallas kernels: 45.2 us -> 40.1 us
  waiting for transfers between devices: 20.9 us -> 23.6 us
    pallas_call x4, Pallas kernels: 22.4 us -> 19.9 us  [up_blocks(): pl.pallas_call(kernel, out_shape=[jax.ShapeDtypeStruct((rows, LANES + 2 *...]
    ppermute x16, waiting for transfers between devices: 18.7 us -> 21.2 us  [shift(): return lax.ppermute(value, 'tp', pairs)]
    pallas_call x1, Pallas kernels: 2.81 us -> 0.72 us  [last_down_block(): pl.pallas_call(kernel, out_shape=[jax.ShapeDtypeStruct((rows, half), F32)...]
  transfers between devices with their start and end apart: 18 -> 18, of which waited for: 11 -> 12; matrix products, arithmetic and copies ran while one was open for 1% -> 1% of each run, Pallas kernels for 41% -> 39%
where the time goes in v3:
time: 85 us; the launch traced here: 84.8 us
  Pallas kernels  40.1 us (47%)
  waiting for transfers between devices  23.6 us (28%)
  starting transfers between devices  18.4 us (22%)
  other arithmetic  1.58 us (2%)
  local copies, waits for them, and re-layouts  0.96 us (1%)
    ppermute x16, waiting for transfers between devices, shift(): return lax.ppermute(value, 'tp', pairs)  21.2 us
    pallas_call x4, Pallas kernels, up_blocks(): pl.pallas_call(kernel, out_shape=[jax.ShapeDtypeStruct((rows, LANES + 2 *...  19.9 us
    ppermute x16, starting transfers between devices, shift(): return lax.ppermute(value, 'tp', pairs)  17.8 us
    pallas_call x4, Pallas kernels, down_blocks(): pl.pallas_call(kernel, out_shape=[jax.ShapeDtypeStruct((rows, width), F32...  13.5 us
    pallas_call x1, Pallas kernels, first_up_block(): pl.pallas_call(kernel, out_shape=[jax.ShapeDtypeStruct((rows, LANES + wid...  3.48 us
    pallas_call x1, Pallas kernels, add_rows(): pl.pallas_call(kernel, out_shape=[jax.ShapeDtypeStruct((rows, share), BF1...  2.45 us
    ppermute x2, waiting for transfers between devices, from_partner(): return lax.ppermute(value, axis, pairs)  2.37 us
  transfers between devices with their start and end apart: 18, of which 12 were waited for; matrix products, arithmetic and copies ran while one was open for 1% of the time, Pallas kernels for 39%

profile of v3, /device:TPU:0, one launch (start us, length us, event | category | flops | bytes accessed | tf_op | source)
XLA Modules:
  0.0 84.8 jit_solution(9304914013869707057)
XLA Ops:
  0.0 2.4 %add_rows.1 = (bf16[64,512]{1,0:T(8,128)(2,1)}, bf16[64,640]{1,0:T(8,128)(2,1)}) custom-call(s32[1,64]{1,0:T(1,128)} %ids_ref.1, bf16[64,512]{1,0:T(8,128)(2,1)} %stream_ref.1, bf16[512,512]{1,0:T(8,128)(2,1)} %table_ref.1, f32[1,8192]{1,0:T(1,128)} %bitcast.20), custom_call_target="tpu_custom_call" | custom-call | tf_op jit(solution)/shard_map/add_rows/pallas_call | solution.py:128
  5.0 3.5 %first_up_block.1 = (bf16[64,1792]{1,0:T(8,128)(2,1)S(1)}, bf16[64,1664]{1,0:T(8,128)(2,1)S(1)}, bf16[64,1024]{1,0:T(8,128)(2,1)S(1)}, f32[64,128]{1,0:T(8,128)S(1)}) custom-call(bf16[64,640]{1,0:T(8,128)(2,1)S(1)} %copy-done, bf16[64,640]{1,0:T(8,128)(2,1)S(1)} %collective-permute-done.other_ref, bf16[1024,13312]{1,0:T(8,128)(2,1)} %bitcast.6, ...), custom_call_target="tpu_custom_call" | custom-call | flops 436207616 | bytes 6815744 | tf_op jit(solution)/shard_map/first_up_block/pallas_call | solution.py:204
  8.5 2.9 %collective-permute-start.2 = (bf16[64,1664]{1,0:T(8,128)(2,1)S(1)}, bf16[64,1664]{1,0:T(8,128)(2,1)S(1)}, u32[]{:S(2)}, u32[]{:S(2)}) collective-permute-start(bf16[64,1664]{1,0:T(8,128)(2,1)S(1)} %get-tuple-element.38.rest_1_), channel_id=1, source_target_pairs={{0,2},{1,3},{4,0},{5,1},{8,4},{9,5},{12,8},{13,9},{14,12},{15,13},... | collective-permute-start | bytes 638984 | tf_op jit(solution)/shard_map/ppermute | solution.py:371
  11.5 5.4 %up_blocks.4 = (f32[64,3456]{1,0:T(8,128)S(1)}, f32[64,3456]{1,0:T(8,128)S(1)}) custom-call(bf16[64,1024]{1,0:T(8,128)(2,1)S(1)} %get-tuple-element.35.x_ref, f32[64,128]{1,0:T(8,128)S(1)} %get-tuple-element.36.squares_ref, bf16[1024,13312]{1,0:T(8,128)(2,1)} %bitcast.7, bf16[1024,13312]{1,0:T(8,128)(2,1)} %bitcast.12, ...), custom_call_target="tpu_custom_call" | custom-call | flops 872415232 | bytes 13631488 | tf_op jit(solution)/shard_map/up_blocks/pallas_call | solution.py:240
  17.2 1.9 %collective-permute-start.4 = (bf16[64,3456]{1,0:T(8,128)(2,1)S(1)}, bf16[64,3456]{1,0:T(8,128)(2,1)S(1)}, u32[]{:S(2)}, u32[]{:S(2)}) collective-permute-start(bf16[64,3456]{1,0:T(8,128)(2,1)S(1)} %pad_maximum_fusion.1.rest_1_), channel_id=1, source_target_pairs={{0,2},{1,3},{4,0},{5,1},{8,4},{9,5},{12,8},{13,9},{14,12},{15,13},... | collective-permute-start | bytes 1327112 | tf_op jit(solution)/shard_map/ppermute | solution.py:371
  19.5 5.4 %up_blocks.5 = (f32[64,3456]{1,0:T(8,128)S(1)}, f32[64,3456]{1,0:T(8,128)S(1)}) custom-call(bf16[64,1024]{1,0:T(8,128)(2,1)S(1)} %get-tuple-element.35.x_ref, f32[64,128]{1,0:T(8,128)S(1)} %get-tuple-element.36.squares_ref, bf16[1024,13312]{1,0:T(8,128)(2,1)} %bitcast.8, bf16[1024,13312]{1,0:T(8,128)(2,1)} %bitcast.13, ...), custom_call_target="tpu_custom_call" | custom-call | flops 872415232 | bytes 13631488 | tf_op jit(solution)/shard_map/up_blocks/pallas_call | solution.py:240
  25.0 4.3 %collective-permute-done.4 = bf16[64,3456]{1,0:T(8,128)(2,1)S(1)} collective-permute-done((bf16[64,3456]{1,0:T(8,128)(2,1)S(1)}, bf16[64,3456]{1,0:T(8,128)(2,1)S(1)}, u32[]{:S(2)}, u32[]{:S(2)}) %collective-permute-start.4) | collective-permute-done | bytes 442400 | tf_op jit(solution)/shard_map/ppermute | solution.py:371
  29.4 1.5 %collective-permute-start.6 = (bf16[64,3456]{1,0:T(8,128)(2,1)S(1)}, bf16[64,3456]{1,0:T(8,128)(2,1)S(1)}, u32[]{:S(2)}, u32[]{:S(2)}) collective-permute-start(bf16[64,3456]{1,0:T(8,128)(2,1)S(1)} %add_convert_fusion.2.rest_1_), channel_id=1, source_target_pairs={{0,2},{1,3},{4,0},{5,1},{8,4},{9,5},{12,8},{13,9},{14,12},{15,13},... | collective-permute-start | bytes 1327112 | tf_op jit(solution)/shard_map/ppermute | solution.py:371
  31.6 5.5 %up_blocks.6 = (f32[64,3456]{1,0:T(8,128)S(1)}, f32[64,3456]{1,0:T(8,128)S(1)}) custom-call(bf16[64,1024]{1,0:T(8,128)(2,1)S(1)} %get-tuple-element.35.x_ref, f32[64,128]{1,0:T(8,128)S(1)} %get-tuple-element.36.squares_ref, bf16[1024,13312]{1,0:T(8,128)(2,1)} %bitcast.9, bf16[1024,13312]{1,0:T(8,128)(2,1)} %bitcast.14, ...), custom_call_target="tpu_custom_call" | custom-call | flops 872415232 | bytes 13631488 | tf_op jit(solution)/shard_map/up_blocks/pallas_call | solution.py:240
  37.1 3.4 %collective-permute-done.6 = bf16[64,3456]{1,0:T(8,128)(2,1)S(1)} collective-permute-done((bf16[64,3456]{1,0:T(8,128)(2,1)S(1)}, bf16[64,3456]{1,0:T(8,128)(2,1)S(1)}, u32[]{:S(2)}, u32[]{:S(2)}) %collective-permute-start.6) | collective-permute-done | bytes 442400 | tf_op jit(solution)/shard_map/ppermute | solution.py:371
  40.6 1.2 %collective-permute-start.8 = (bf16[64,3456]{1,0:T(8,128)(2,1)S(1)}, bf16[64,3456]{1,0:T(8,128)(2,1)S(1)}, u32[]{:S(2)}, u32[]{:S(2)}) collective-permute-start(bf16[64,3456]{1,0:T(8,128)(2,1)S(1)} %add_convert_fusion.rest_1_), channel_id=1, source_target_pairs={{0,2},{1,3},{4,0},{5,1},{8,4},{9,5},{12,8},{13,9},{14,12},{15,13},... | collective-permute-start | bytes 1327112 | tf_op jit(solution)/shard_map/ppermute | solution.py:371
  42.8 3.5 %up_blocks.7 = f32[64,3456]{1,0:T(8,128)S(1)} custom-call(bf16[64,1024]{1,0:T(8,128)(2,1)S(1)} %get-tuple-element.35.x_ref, f32[64,128]{1,0:T(8,128)S(1)} %get-tuple-element.36.squares_ref, bf16[1024,13312]{1,0:T(8,128)(2,1)} %bitcast.10, bf16[1024,13312]{1,0:T(8,128)(2,1)} %bitcast.15, bf16[64,3456]{1,0:T(8,128)(2,1)S(1)} %add_convert_fusion.1.rest_0_, ...), custom_call_target="tpu_custom_call" | custom-call | flops 436207616 | bytes 6815744 | tf_op jit(solution)/shard_map/up_blocks/pallas_call | solution.py:240
  46.2 4.5 %collective-permute-done.8 = bf16[64,3456]{1,0:T(8,128)(2,1)S(1)} collective-permute-done((bf16[64,3456]{1,0:T(8,128)(2,1)S(1)}, bf16[64,3456]{1,0:T(8,128)(2,1)S(1)}, u32[]{:S(2)}, u32[]{:S(2)}) %collective-permute-start.8) | collective-permute-done | bytes 442400 | tf_op jit(solution)/shard_map/ppermute | solution.py:371
  52.0 1.6 %collective-permute-start.10 = (bf16[64,1664]{1,0:T(8,128)(2,1)S(1)}, bf16[64,1664]{1,0:T(8,128)(2,1)S(1)}, u32[]{:S(2)}, u32[]{:S(2)}) collective-permute-start(bf16[64,1664]{1,0:T(8,128)(2,1)S(1)} %fusion.rest_0_), channel_id=1, source_target_pairs={{0,2},{1,3},{4,0},{5,1},{8,4},{9,5},{12,8},{13,9},{14,12},{15,13},... | collective-permute-start | bytes 638984 | tf_op jit(solution)/shard_map/ppermute | solution.py:371
  54.1 2.7 %down_blocks.4.rest_0_ = f32[64,1024]{1,0:T(8,128)S(1)} custom-call(bf16[64,1664]{1,0:T(8,128)(2,1)S(1)} %fusion.rest_0_, bf16[13312,1024]{1,0:T(8,128)(2,1)} %bitcast.16), custom_call_target="tpu_custom_call" | custom-call | flops 218103808 | bytes 3407872 | tf_op jit(solution)/shard_map/down_blocks/pallas_call | solution.py:314
  56.8 1.6 %collective-permute-done.10.rest_2_ = bf16[64,1664]{1,0:T(8,128)(2,1)S(1)} collective-permute-done((bf16[64,1664]{1,0:T(8,128)(2,1)S(1)}, bf16[64,1664]{1,0:T(8,128)(2,1)S(1)}, u32[]{:S(2)}, u32[]{:S(2)}) %collective-permute-start.10) | collective-permute-done | bytes 213024 | tf_op jit(solution)/shard_map/ppermute | solution.py:371
  58.3 3.4 %collective-permute-done.9.rest_1_ = bf16[64,1664]{1,0:T(8,128)(2,1)S(1)} collective-permute-done((bf16[64,1664]{1,0:T(8,128)(2,1)S(1)}, bf16[64,1664]{1,0:T(8,128)(2,1)S(1)}, u32[]{:S(2)}, u32[]{:S(2)}) %collective-permute-start.9) | collective-permute-done | bytes 213024 | tf_op jit(solution)/shard_map/ppermute | solution.py:371
  62.2 1.6 %collective-permute-start.12 = (bf16[64,1664]{1,0:T(8,128)(2,1)S(1)}, bf16[64,1664]{1,0:T(8,128)(2,1)S(1)}, u32[]{:S(2)}, u32[]{:S(2)}) collective-permute-start(bf16[64,1664]{1,0:T(8,128)(2,1)S(1)} %collective-permute-done.10.rest_2_), channel_id=1, source_target_pairs={{0,2},{1,3},{4,0},{5,1},{8,4},{9,5},{12,8},{13,9},{14,12},{15,13},... | collective-permute-start | bytes 638984 | tf_op jit(solution)/shard_map/ppermute | solution.py:371
  63.7 3.4 %down_blocks.5.rest_0_ = f32[64,1024]{1,0:T(8,128)S(1)} custom-call(f32[64,1024]{1,0:T(8,128)S(1)} %down_blocks.4.rest_0_, bf16[64,1664]{1,0:T(8,128)(2,1)S(1)} %collective-permute-done.9.rest_1_, bf16[64,1664]{1,0:T(8,128)(2,1)S(1)} %collective-permute-done.10.rest_2_, bf16[13312,1024]{1,0:T(8,128)(2,1)} %bitcast.17), custom_call_target="tpu_custom_call" | custom-call | flops 436207616 | bytes 6815744 | tf_op jit(solution)/shard_map/down_blocks/pallas_call | solution.py:314
  67.2 1.8 %collective-permute-done.11.rest_1_ = bf16[64,1664]{1,0:T(8,128)(2,1)S(1)} collective-permute-done((bf16[64,1664]{1,0:T(8,128)(2,1)S(1)}, bf16[64,1664]{1,0:T(8,128)(2,1)S(1)}, u32[]{:S(2)}, u32[]{:S(2)}) %collective-permute-start.11) | collective-permute-done | bytes 213024 | tf_op jit(solution)/shard_map/ppermute | solution.py:371
  71.2 3.4 %down_blocks.6.rest_0_ = f32[64,1024]{1,0:T(8,128)S(1)} custom-call(f32[64,1024]{1,0:T(8,128)S(1)} %down_blocks.5.rest_0_, bf16[64,1664]{1,0:T(8,128)(2,1)S(1)} %collective-permute-done.11.rest_1_, bf16[64,1664]{1,0:T(8,128)(2,1)S(1)} %collective-permute-done.12.rest_2_, bf16[13312,1024]{1,0:T(8,128)(2,1)} %bitcast.18), custom_call_target="tpu_custom_call" | custom-call | flops 436207616 | bytes 6815744 | tf_op jit(solution)/shard_map/down_blocks/pallas_call | solution.py:314
  75.9 1.4 %collective-permute-start.15 = (bf16[32,1664]{1,0:T(8,128)(2,1)S(1)}, bf16[32,1664]{1,0:T(8,128)(2,1)S(1)}, u32[]{:S(2)}, u32[]{:S(2)}) collective-permute-start(bf16[32,1664]{1,0:T(8,128)(2,1)S(1)} %slice.40), channel_id=1, source_target_pairs={{0,4},{1,5},{4,8},{5,9},{8,12},{9,13},{12,14},{13,15},{14,10},{15,... | collective-permute-start | bytes 319496 | tf_op jit(solution)/shard_map/ppermute | solution.py:371
  78.1 4.0 %down_blocks.7 = (f32[64,1024]{1,0:T(8,128)S(1)}, bf16[1664,1024]{1,0:T(8,128)(2,1)S(1)}) custom-call(f32[64,1024]{1,0:T(8,128)S(1)} %down_blocks.6.rest_0_, bf16[64,1664]{1,0:T(8,128)(2,1)S(1)} %collective-permute-done.13.rest_1_, bf16[64,1664]{1,0:T(8,128)(2,1)S(1)} %collective-permute-done.14.rest_2_, bf16[13312,1024]{1,0:T(8,128)(2,1)} %bitcast.19), custom_call_target="tpu_custom_call" | custom-call | flops 654311424 | bytes 10223616 | tf_op jit(solution)/shard_map/down_blocks/pallas_call | solution.py:314
  82.9 1.2 %collective-permute-done.17 = bf16[64,512]{1,0:T(8,128)(2,1)S(1)} collective-permute-done((bf16[64,512]{1,0:T(8,128)(2,1)S(1)}, bf16[64,512]{1,0:T(8,128)(2,1)S(1)}, u32[]{:S(2)}, u32[]{:S(2)}) %collective-permute-start.17) | collective-permute-done | bytes 65568 | tf_op jit(solution)/shard_map/ppermute | solution.py:22
  (45 shorter events, 12.8 us)
Async XLA Ops:
  2.5 1.7 %collective-permute-start = (bf16[64,640]{1,0:T(8,128)(2,1)}, bf16[64,640]{1,0:T(8,128)(2,1)S(1)}, u32[]{:S(2)}, u32[]{:S(2)}) collective-permute-start(bf16[64,640]{1,0:T(8,128)(2,1)} %get-tuple-element.34.own_ref), channel_id=1, source_target_pairs={{0,1},{1,0},{2,3},{3,2},{4,5},{5,4},{6,7},{7,6},{8,9},{9,8},{10,11... | collective-permute-start | bytes 245768 | tf_op jit(solution)/shard_map/ppermute | solution.py:22
  4.1 0.9 %copy-start = (bf16[64,640]{1,0:T(8,128)(2,1)S(1)}, bf16[64,640]{1,0:T(8,128)(2,1)}, u32[]{:S(2)}) copy-start(bf16[64,640]{1,0:T(8,128)(2,1)} %get-tuple-element.34.own_ref) | copy-start | bytes 245764
  8.5 8.6 %collective-permute-start.2 = (bf16[64,1664]{1,0:T(8,128)(2,1)S(1)}, bf16[64,1664]{1,0:T(8,128)(2,1)S(1)}, u32[]{:S(2)}, u32[]{:S(2)}) collective-permute-start(bf16[64,1664]{1,0:T(8,128)(2,1)S(1)} %get-tuple-element.38.rest_1_), channel_id=1, source_target_pairs={{0,2},{1,3},{4,0},{5,1},{8,4},{9,5},{12,8},{13,9},{14,12},{15,13},... | collective-permute-start | bytes 638984 | tf_op jit(solution)/shard_map/ppermute | solution.py:371
  11.4 7.7 %collective-permute-start.1 = (bf16[64,1792]{1,0:T(8,128)(2,1)S(1)}, bf16[64,1792]{1,0:T(8,128)(2,1)S(1)}, u32[]{:S(2)}, u32[]{:S(2)}) collective-permute-start(bf16[64,1792]{1,0:T(8,128)(2,1)S(1)} %get-tuple-element.37.rest_0_), channel_id=1, source_target_pairs={{0,4},{1,5},{4,8},{5,9},{8,12},{9,13},{12,14},{13,15},{14,10},{15,... | collective-permute-start | bytes 688136 | tf_op jit(solution)/shard_map/ppermute | solution.py:371
  17.2 12.1 %collective-permute-start.4 = (bf16[64,3456]{1,0:T(8,128)(2,1)S(1)}, bf16[64,3456]{1,0:T(8,128)(2,1)S(1)}, u32[]{:S(2)}, u32[]{:S(2)}) collective-permute-start(bf16[64,3456]{1,0:T(8,128)(2,1)S(1)} %pad_maximum_fusion.1.rest_1_), channel_id=1, source_target_pairs={{0,2},{1,3},{4,0},{5,1},{8,4},{9,5},{12,8},{13,9},{14,12},{15,13},... | collective-permute-start | bytes 1327112 | tf_op jit(solution)/shard_map/ppermute | solution.py:371
  19.2 11.7 %collective-permute-start.3 = (bf16[64,3456]{1,0:T(8,128)(2,1)S(1)}, bf16[64,3456]{1,0:T(8,128)(2,1)S(1)}, u32[]{:S(2)}, u32[]{:S(2)}) collective-permute-start(bf16[64,3456]{1,0:T(8,128)(2,1)S(1)} %pad_maximum_fusion.rest_0_), channel_id=1, source_target_pairs={{0,4},{1,5},{4,8},{5,9},{8,12},{9,13},{12,14},{13,15},{14,10},{15,... | collective-permute-start | bytes 1327112 | tf_op jit(solution)/shard_map/ppermute | solution.py:371
  29.4 11.1 %collective-permute-start.6 = (bf16[64,3456]{1,0:T(8,128)(2,1)S(1)}, bf16[64,3456]{1,0:T(8,128)(2,1)S(1)}, u32[]{:S(2)}, u32[]{:S(2)}) collective-permute-start(bf16[64,3456]{1,0:T(8,128)(2,1)S(1)} %add_convert_fusion.2.rest_1_), channel_id=1, source_target_pairs={{0,2},{1,3},{4,0},{5,1},{8,4},{9,5},{12,8},{13,9},{14,12},{15,13},... | collective-permute-start | bytes 1327112 | tf_op jit(solution)/shard_map/ppermute | solution.py:371
  31.0 10.8 %collective-permute-start.5 = (bf16[64,3456]{1,0:T(8,128)(2,1)S(1)}, bf16[64,3456]{1,0:T(8,128)(2,1)S(1)}, u32[]{:S(2)}, u32[]{:S(2)}) collective-permute-start(bf16[64,3456]{1,0:T(8,128)(2,1)S(1)} %add_convert_fusion.3.rest_0_), channel_id=1, source_target_pairs={{0,4},{1,5},{4,8},{5,9},{8,12},{9,13},{12,14},{13,15},{14,10},{15,... | collective-permute-start | bytes 1327112 | tf_op jit(solution)/shard_map/ppermute | solution.py:371
  40.6 10.2 %collective-permute-start.8 = (bf16[64,3456]{1,0:T(8,128)(2,1)S(1)}, bf16[64,3456]{1,0:T(8,128)(2,1)S(1)}, u32[]{:S(2)}, u32[]{:S(2)}) collective-permute-start(bf16[64,3456]{1,0:T(8,128)(2,1)S(1)} %add_convert_fusion.rest_1_), channel_id=1, source_target_pairs={{0,2},{1,3},{4,0},{5,1},{8,4},{9,5},{12,8},{13,9},{14,12},{15,13},... | collective-permute-start | bytes 1327112 | tf_op jit(solution)/shard_map/ppermute | solution.py:371
  41.9 9.6 %collective-permute-start.7 = (bf16[64,3456]{1,0:T(8,128)(2,1)S(1)}, bf16[64,3456]{1,0:T(8,128)(2,1)S(1)}, u32[]{:S(2)}, u32[]{:S(2)}) collective-permute-start(bf16[64,3456]{1,0:T(8,128)(2,1)S(1)} %add_convert_fusion.1.rest_0_), channel_id=1, source_target_pairs={{0,4},{1,5},{4,8},{5,9},{8,12},{9,13},{12,14},{13,15},{14,10},{15,... | collective-permute-start | bytes 1327112 | tf_op jit(solution)/shard_map/ppermute | solution.py:371
  52.0 6.4 %collective-permute-start.10 = (bf16[64,1664]{1,0:T(8,128)(2,1)S(1)}, bf16[64,1664]{1,0:T(8,128)(2,1)S(1)}, u32[]{:S(2)}, u32[]{:S(2)}) collective-permute-start(bf16[64,1664]{1,0:T(8,128)(2,1)S(1)} %fusion.rest_0_), channel_id=1, source_target_pairs={{0,2},{1,3},{4,0},{5,1},{8,4},{9,5},{12,8},{13,9},{14,12},{15,13},... | collective-permute-start | bytes 638984 | tf_op jit(solution)/shard_map/ppermute | solution.py:371
  53.6 8.1 %collective-permute-start.9 = (bf16[64,1664]{1,0:T(8,128)(2,1)S(1)}, bf16[64,1664]{1,0:T(8,128)(2,1)S(1)}, u32[]{:S(2)}, u32[]{:S(2)}) collective-permute-start(bf16[64,1664]{1,0:T(8,128)(2,1)S(1)} %fusion.rest_0_), channel_id=1, source_target_pairs={{0,4},{1,5},{4,8},{5,9},{8,12},{9,13},{12,14},{13,15},{14,10},{15,... | collective-permute-start | bytes 638984 | tf_op jit(solution)/shard_map/ppermute | solution.py:371
  61.7 7.3 %collective-permute-start.11 = (bf16[64,1664]{1,0:T(8,128)(2,1)S(1)}, bf16[64,1664]{1,0:T(8,128)(2,1)S(1)}, u32[]{:S(2)}, u32[]{:S(2)}) collective-permute-start(bf16[64,1664]{1,0:T(8,128)(2,1)S(1)} %collective-permute-done.9.rest_1_), channel_id=1, source_target_pairs={{0,4},{1,5},{4,8},{5,9},{8,12},{9,13},{12,14},{13,15},{14,10},{15,... | collective-permute-start | bytes 638984 | tf_op jit(solution)/shard_map/ppermute | solution.py:371
  62.2 7.0 %collective-permute-start.12 = (bf16[64,1664]{1,0:T(8,128)(2,1)S(1)}, bf16[64,1664]{1,0:T(8,128)(2,1)S(1)}, u32[]{:S(2)}, u32[]{:S(2)}) collective-permute-start(bf16[64,1664]{1,0:T(8,128)(2,1)S(1)} %collective-permute-done.10.rest_2_), channel_id=1, source_target_pairs={{0,2},{1,3},{4,0},{5,1},{8,4},{9,5},{12,8},{13,9},{14,12},{15,13},... | collective-permute-start | bytes 638984 | tf_op jit(solution)/shard_map/ppermute | solution.py:371
  67.2 17.0 %copy-start.1 = (bf16[64,512]{1,0:T(8,128)(2,1)S(1)}, bf16[64,512]{1,0:T(8,128)(2,1)}, u32[]{:S(2)}) copy-start(bf16[64,512]{1,0:T(8,128)(2,1)} %get-tuple-element.33) | copy-start | bytes 196612
  69.2 5.8 %collective-permute-start.13 = (bf16[64,1664]{1,0:T(8,128)(2,1)S(1)}, bf16[64,1664]{1,0:T(8,128)(2,1)S(1)}, u32[]{:S(2)}, u32[]{:S(2)}) collective-permute-start(bf16[64,1664]{1,0:T(8,128)(2,1)S(1)} %collective-permute-done.11.rest_1_), channel_id=1, source_target_pairs={{0,4},{1,5},{4,8},{5,9},{8,12},{9,13},{12,14},{13,15},{14,10},{15,... | collective-permute-start | bytes 638984 | tf_op jit(solution)/shard_map/ppermute | solution.py:371
  70.1 5.8 %collective-permute-start.14 = (bf16[64,1664]{1,0:T(8,128)(2,1)S(1)}, bf16[64,1664]{1,0:T(8,128)(2,1)S(1)}, u32[]{:S(2)}, u32[]{:S(2)}) collective-permute-start(bf16[64,1664]{1,0:T(8,128)(2,1)S(1)} %collective-permute-done.12.rest_2_), channel_id=1, source_target_pairs={{0,2},{1,3},{4,0},{5,1},{8,4},{9,5},{12,8},{13,9},{14,12},{15,13},... | collective-permute-start | bytes 638984 | tf_op jit(solution)/shard_map/ppermute | solution.py:371
  75.9 6.2 %collective-permute-start.15 = (bf16[32,1664]{1,0:T(8,128)(2,1)S(1)}, bf16[32,1664]{1,0:T(8,128)(2,1)S(1)}, u32[]{:S(2)}, u32[]{:S(2)}) collective-permute-start(bf16[32,1664]{1,0:T(8,128)(2,1)S(1)} %slice.40), channel_id=1, source_target_pairs={{0,4},{1,5},{4,8},{5,9},{8,12},{9,13},{12,14},{13,15},{14,10},{15,... | collective-permute-start | bytes 319496 | tf_op jit(solution)/shard_map/ppermute | solution.py:371
  77.4 4.8 %collective-permute-start.16 = (bf16[32,1664]{1,0:T(8,128)(2,1)S(1)}, bf16[32,1664]{1,0:T(8,128)(2,1)S(1)}, u32[]{:S(2)}, u32[]{:S(2)}) collective-permute-start(bf16[32,1664]{1,0:T(8,128)(2,1)S(1)} %slice.41), channel_id=1, source_target_pairs={{0,2},{1,3},{4,0},{5,1},{8,4},{9,5},{12,8},{13,9},{14,12},{15,13},... | collective-permute-start | bytes 319496 | tf_op jit(solution)/shard_map/ppermute | solution.py:371
  82.9 1.3 %collective-permute-start.17 = (bf16[64,512]{1,0:T(8,128)(2,1)S(1)}, bf16[64,512]{1,0:T(8,128)(2,1)S(1)}, u32[]{:S(2)}, u32[]{:S(2)}) collective-permute-start(bf16[64,512]{1,0:T(8,128)(2,1)S(1)} %get-tuple-element.60), channel_id=1, source_target_pairs={{0,1},{1,0},{2,3},{3,2},{4,5},{5,4},{6,7},{7,6},{8,9},{9,8},{10,11... | collective-permute-start | bytes 196616 | tf_op jit(solution)/shard_map/ppermute | solution.py:22

commit v4 on v3

--- a/solution.py
+++ b/solution.py
@@ -8,12 +8,12 @@
 D = 8192
 D_WAYS = 8
 LANES = 128
-DOWN_CHUNK = 896
-VMEM_LIMIT = 32 * 2**20
+MIB = 2**20
 BF16 = jnp.bfloat16
 F32 = jnp.float32
 IN_VMEM = pl.BlockSpec(memory_space=pltpu.VMEM)
 IN_PLACE = pl.BlockSpec(memory_space=pl.ANY)
+IN_HBM = pl.BlockSpec(memory_space=pltpu.HBM)
 
 
 def from_partner(value, axis, distance):
@@ -84,8 +84,8 @@
     return (block_in.astype(F32) + summed).astype(BF16)
 
 
-def params():
-    return pltpu.CompilerParams(vmem_limit_bytes=VMEM_LIMIT)
+def params(mib=26):
+    return pltpu.CompilerParams(vmem_limit_bytes=mib * MIB)
 
 
 def position():
@@ -100,14 +100,32 @@
     return (place + distance + D_WAYS) & (D_WAYS - 1)
 
 
-def add_rows(token_ids, stream, table_rows, gain):
+def fetch_up_block(gate_tile, up_tile, distance):
+    depth, units = gate_tile.shape
+    width = units // D_WAYS
+
+    def kernel(gate_ref, up_ref, out_ref, arrived):
+        _, _, place = position()
+        for _, _, copy in start_up_copies(at(place, distance), gate_ref, up_ref, out_ref, arrived):
+            copy.wait()
+
+    return pl.pallas_call(
+        kernel,
+        out_shape=jax.ShapeDtypeStruct((2, depth, width), BF16),
+        in_specs=[IN_HBM] * 2,
+        out_specs=IN_VMEM,
+        scratch_shapes=[pltpu.SemaphoreType.DMA((2, 1))],
+        compiler_params=params(),
+        name="fetch_up_block",
+    )(gate_tile, up_tile)
+
+
+def add_rows(token_ids, stream, table_rows, gain, after):
     entries = table_rows.shape[0]
     rows, share = stream.shape
 
-    def kernel(ids_ref, stream_ref, table_ref, gain_ref, out_ref, message_ref, gains, arrived):
+    def kernel(ids_ref, stream_ref, table_ref, gain_ref, after_ref, out_ref, message_ref):
         place = pl.multiple_of(lax.axis_index("tp") * share, LANES)
-        copy = pltpu.make_async_copy(gain_ref.at[:, pl.ds(place, share)], gains, arrived)
-        copy.start()
         row = lax.broadcasted_iota(jnp.int32, (rows, rows), 0)
         column = lax.broadcasted_iota(jnp.int32, (rows, rows), 1)
         across = jnp.broadcast_to(ids_ref[...].astype(F32), (rows, rows))
@@ -122,8 +140,7 @@
         for lane in range(0, share, LANES):
             squares += value[:, lane : lane + LANES] * value[:, lane : lane + LANES]
         message_ref[:, share:] = squares.astype(BF16)
-        copy.wait()
-        message_ref[:, :share] = (value * gains[...]).astype(BF16)
+        message_ref[:, :share] = (value * gain_ref[:, pl.ds(place, share)]).astype(BF16)
 
     return pl.pallas_call(
         kernel,
@@ -131,11 +148,11 @@
             jax.ShapeDtypeStruct((rows, share), BF16),
             jax.ShapeDtypeStruct((rows, share + LANES), BF16),
         ],
-        in_specs=[IN_VMEM] * 3 + [IN_PLACE],
+        in_specs=[IN_VMEM] * 4 + [IN_PLACE],
         out_specs=[IN_VMEM] * 2,
-        scratch_shapes=[pltpu.VMEM((1, share), F32), pltpu.SemaphoreType.DMA],
+        compiler_params=params(),
         name="add_rows",
-    )(token_ids, stream, table_rows, gain)
+    )(token_ids, stream, table_rows, gain, after)
 
 
 def start_up_copies(block, gate_ref, up_ref, tiles, arrived):
@@ -181,15 +198,13 @@
     )
 
 
-def first_up_block(own, other, gate_tile, up_tile):
-    depth, units = gate_tile.shape
-    width = units // D_WAYS
+def first_up_block(own, other, tiles):
+    _, depth, width = tiles.shape
     rows = own.shape[0]
     share = own.shape[1] - LANES
 
-    def kernel(own_ref, other_ref, gate_ref, up_ref, gate_out, up_out, x_ref, squares_ref, products, tiles, arrived):
-        _, side, place = position()
-        copies = start_up_copies(at(place, 4), gate_ref, up_ref, tiles.at[0], arrived.at[0])
+    def kernel(own_ref, other_ref, tiles_ref, gate_out, up_out, x_ref, squares_ref):
+        _, side, _ = position()
         high = side == 1
         own_x, other_x = own_ref[:, :share], other_ref[:, :share]
         x_ref[:, :share] = jnp.where(high, other_x, own_x)
@@ -197,9 +212,9 @@
         squares = own_ref[:, share:].astype(F32) + other_ref[:, share:].astype(F32)
         squares_ref[...] = squares
         gate_out[:, :LANES] = squares.astype(BF16)
-        up_products(x_ref, copies, tiles.at[0], [products.at[0], products.at[1]])
-        gate_out[:, LANES:] = products[0].astype(BF16)
-        up_out[...] = products[1].astype(BF16)
+        x = x_ref[...]
+        gate_out[:, LANES:] = jnp.dot(x, tiles_ref[0], preferred_element_type=F32).astype(BF16)
+        up_out[...] = jnp.dot(x, tiles_ref[1], preferred_element_type=F32).astype(BF16)
 
     return pl.pallas_call(
         kernel,
@@ -209,73 +224,65 @@
             jax.ShapeDtypeStruct((rows, depth), BF16),
             jax.ShapeDtypeStruct((rows, LANES), F32),
         ],
-        in_specs=[IN_VMEM] * 2 + [IN_PLACE] * 2,
+        in_specs=[IN_VMEM] * 3,
         out_specs=[IN_VMEM] * 4,
-        scratch_shapes=[pltpu.VMEM((2, rows, width), F32)] + up_scratch(1, depth, width),
         compiler_params=params(),
         cost_estimate=up_cost(1, rows, depth, width),
         name="first_up_block",
-    )(own, other, gate_tile, up_tile)
-
-
-def up_blocks(x, squares, gate_tile, up_tile, distances, after):
+    )(own, other, tiles)
+
+
+def up_blocks(x, squares, gate_tile, up_tile, distances, after, down_tile=None, fetch=()):
     depth, units = gate_tile.shape
     width = units // D_WAYS
     rows = x.shape[0]
     count = len(distances)
+    downs = [down_tile] if fetch else []
 
     def kernel(x_ref, squares_ref, gate_ref, up_ref, *rest):
-        out_refs = rest[len(after) : len(after) + count]
-        tiles, arrived = rest[-2:]
+        rest = rest[len(after) :]
+        down_refs, rest = rest[: len(downs)], rest[len(downs) :]
+        out_refs, fetched = rest[:count], rest[count : count + len(fetch)]
+        tiles, arrived, fetch_arrived = rest[-3:]
         _, _, place = position()
         copies = [
             start_up_copies(at(place, distance), gate_ref, up_ref, tiles.at[j], arrived.at[j])
             for j, distance in enumerate(distances)
         ]
+        ahead = start_down_copies(place, fetch, down_refs, fetched, fetch_arrived)
         for j, out_ref in enumerate(out_refs):
             out_ref[:, :LANES] = squares_ref[...]
             pair = [out_ref.at[:, pl.ds(LANES, width)], out_ref.at[:, pl.ds(LANES + width, width)]]
             up_products(x_ref, copies[j], tiles.at[j], pair)
-
-    return pl.pallas_call(
-        kernel,
-        out_shape=[jax.ShapeDtypeStruct((rows, LANES + 2 * width), F32)] * count,
-        in_specs=[IN_VMEM] * 2 + [IN_PLACE] * (2 + len(after)),
-        out_specs=[IN_VMEM] * count,
-        scratch_shapes=up_scratch(count, depth, width),
-        compiler_params=params(),
+        for copy in ahead:
+            copy.wait()
+
+    return pl.pallas_call(
+        kernel,
+        out_shape=[jax.ShapeDtypeStruct((rows, LANES + 2 * width), F32)] * count
+        + [jax.ShapeDtypeStruct(down_tile_shape(down_tile), BF16) for _ in fetch],
+        in_specs=[IN_VMEM] * 2 + [IN_HBM] * 2 + [IN_PLACE] * len(after) + [IN_HBM] * len(downs),
+        out_specs=[IN_VMEM] * (count + len(fetch)),
+        scratch_shapes=up_scratch(count, depth, width) + [pltpu.SemaphoreType.DMA((max(len(fetch), 1),))],
+        compiler_params=params(26 if count == 2 else 14),
         cost_estimate=up_cost(count, rows, depth, width),
         name="up_blocks",
-    )(x, squares, gate_tile, up_tile, *after)
-
-
-def down_chunks(depth):
-    return [(start, min(DOWN_CHUNK, depth - start)) for start in range(0, depth, DOWN_CHUNK)]
-
-
-def start_down_copies(block, down_ref, tiles, arrived):
-    depth = down_ref.shape[0] // D_WAYS
+    )(x, squares, gate_tile, up_tile, *after, *downs)
+
+
+def down_tile_shape(down_tile):
+    return (down_tile.shape[0] // D_WAYS, down_tile.shape[1])
+
+
+def start_down_copies(place, distances, down_refs, tiles, arrived):
     copies = []
-    for c, (start, size) in enumerate(down_chunks(depth)):
-        copy = pltpu.make_async_copy(
-            down_ref.at[pl.ds(pl.multiple_of(block * depth + start, LANES), size), :],
-            tiles.at[pl.ds(start, size), :],
-            arrived.at[c],
-        )
+    for j, distance in enumerate(distances):
+        depth = tiles[j].shape[0]
+        start = pl.multiple_of(at(place, distance) * depth, LANES)
+        copy = pltpu.make_async_copy(down_refs[0].at[pl.ds(start, depth), :], tiles[j], arrived.at[j])
         copy.start()
-        copies.append((start, size, copy))
+        copies.append(copy)
     return copies
-
-
-def down_products(value, hidden_ref, copies, tiles):
-    for start, size, copy in copies:
-        copy.wait()
-        value = value + jnp.dot(
-            hidden_ref[:, start : start + size],
-            tiles[start : start + size, :],
-            preferred_element_type=F32,
-        )
-    return value
 
 
 def down_cost(count, rows, depth, width):
@@ -286,45 +293,44 @@
     )
 
 
-def down_blocks(total, hidden, down_tile, distances, fetch=None):
-    units, width = down_tile.shape
-    depth = units // D_WAYS
-    rows = hidden[0].shape[0]
-    count = len(distances)
+def down_blocks(total, hidden, tiles, down_tile, fetch, after):
+    depth, width = tiles[0].shape
+    half = hidden[0][0].shape[0]
+    rows = 2 * half
+    count = len(hidden)
     totals = [] if total is None else [total]
-    fetches = 0 if fetch is None else 1
+    downs = [down_tile] if fetch else []
 
     def kernel(*rest):
-        hidden_refs = rest[len(totals) : len(totals) + count]
-        down_ref, out_ref, *fetched, tiles, arrived = rest[len(totals) + count :]
+        total_refs, rest = rest[: len(totals)], rest[len(totals) :]
+        hidden_refs, tile_refs, rest = rest[: 2 * count], rest[2 * count : 3 * count], rest[3 * count :]
+        down_refs, rest = rest[: len(downs)], rest[len(downs) + len(after) :]
+        out_ref, *fetched, whole, arrived = rest
         _, _, place = position()
-        copies = [
-            start_down_copies(at(place, distance), down_ref, tiles.at[j], arrived.at[j])
-            for j, distance in enumerate(distances)
-        ]
-        ahead = [start_down_copies(at(place, fetch), down_ref, ref, arrived.at[count]) for ref in fetched]
-        value = rest[0][...] if totals else jnp.zeros((rows, width), F32)
-        for j in range(count):
-            value = down_products(value, hidden_refs[j], copies[j], tiles.at[j])
+        ahead = start_down_copies(place, fetch, down_refs, fetched, arrived)
+        value = total_refs[0][...] if totals else jnp.zeros((rows, width), F32)
+        for j, tile_ref in enumerate(tile_refs):
+            whole[j, :half] = hidden_refs[2 * j][...]
+            whole[j, half:] = hidden_refs[2 * j + 1][...]
+            value = value + jnp.dot(whole[j], tile_ref[...], preferred_element_type=F32)
         out_ref[...] = value
-        for pieces in ahead:
-            for _, _, copy in pieces:
-                copy.wait()
+        for copy in ahead:
+            copy.wait()
 
     return pl.pallas_call(
         kernel,
         out_shape=[jax.ShapeDtypeStruct((rows, width), F32)]
-        + [jax.ShapeDtypeStruct((depth, width), BF16)] * fetches,
-        in_specs=[IN_VMEM] * (len(totals) + count) + [IN_PLACE],
-        out_specs=[IN_VMEM] * (1 + fetches),
+        + [jax.ShapeDtypeStruct((depth, width), BF16)] * len(fetch),
+        in_specs=[IN_VMEM] * (len(totals) + 3 * count) + [IN_HBM] * len(downs) + [IN_PLACE] * len(after),
+        out_specs=[IN_VMEM] * (1 + len(fetch)),
         scratch_shapes=[
-            pltpu.VMEM((count, depth, width), BF16),
-            pltpu.SemaphoreType.DMA((count + fetches, len(down_chunks(depth)))),
+            pltpu.VMEM((count, rows, depth), BF16),
+            pltpu.SemaphoreType.DMA((max(len(fetch), 1),)),
         ],
-        compiler_params=params(),
-        cost_estimate=down_cost(count + fetches, rows, depth, width),
+        compiler_params=params(8),
+        cost_estimate=down_cost(count + len(fetch), rows, depth, width),
         name="down_blocks",
-    )(*totals, *hidden, down_tile)
+    )(*totals, *[half for pair in hidden for half in pair], *tiles, *downs, *after)
 
 
 def last_down_block(total, upper, lower, tile):
@@ -350,7 +356,7 @@
         in_specs=[IN_VMEM] * 4,
         out_specs=[IN_VMEM] * 2,
         scratch_shapes=[pltpu.VMEM((rows, depth), BF16)],
-        compiler_params=params(),
+        compiler_params=params(8),
         cost_estimate=down_cost(1, rows, depth, width),
         name="last_down_block",
     )(total, upper, lower, tile)
@@ -370,14 +376,18 @@
         ]
         return lax.ppermute(value, "tp", pairs)
 
-    block_in, own = add_rows(token_ids, stream, table_rows, norm_gain[None])
+    far_tiles = fetch_up_block(gate_tile, up_tile, 4)
+    block_in, own = add_rows(token_ids, stream, table_rows, norm_gain[None], far_tiles)
     other = from_partner(own, "tp", 0)
 
-    right, left, scaled, squares = first_up_block(own, other, gate_tile, up_tile)
+    right, left, scaled, squares = first_up_block(own, other, far_tiles)
     split = LANES + width
-    for distance in (3, 2, 1, 0):
+    down_tiles = []
+    for distance, fetch in ((3, ()), (2, (0, -1)), (1, (1, -2)), (0, (2, -3, 3, 4))):
         distances = [distance, -distance] if distance else [0]
-        own = up_blocks(scaled, squares, gate_tile, up_tile, distances, [right, left])
+        found = up_blocks(scaled, squares, gate_tile, up_tile, distances, [right, left], down_tile, fetch)
+        own = found[: len(distances)]
+        down_tiles += found[len(distances) :]
         right, left = shift(right, 1), shift(left, -1)
         if distance == 3:
             right = jnp.concatenate([own[0][:, :split] + right.astype(F32), own[0][:, split:]], 1)
@@ -394,21 +404,26 @@
     mine = (jax.nn.silu(both[:, :width]) * both[:, width:]).astype(BF16)
 
     half = rows // 2
+    upper, lower = mine[:half], mine[half:]
     total = None
-    right, left = mine, mine
-    for distance in (0, 1, 2, 3):
-        if distance == 3:
-            next_right, next_left = shift(right[:half], 1), shift(left[half:], -1)
+    hidden = [(upper, lower)]
+    upper_right, upper_left, lower_right, lower_left = upper, upper, lower, lower
+    for distance, fetch in ((0, ()), (1, ()), (2, ()), (3, ())):
+        tiles, down_tiles = down_tiles[: len(hidden)], down_tiles[len(hidden) :]
+        upper_right = shift(upper_right, 1)
+        lower_left = shift(lower_left, -1)
+        if distance < 3:
+            upper_left = shift(upper_left, -1)
+            lower_right = shift(lower_right, 1)
+            after = [upper_right, upper_left]
         else:
-            next_right, next_left = shift(right, 1), shift(left, -1)
-        if distance == 3:
-            total, far_tile = down_blocks(total, [right, left], down_tile, [-3, 3], fetch=4)
-        elif distance:
-            (total,) = down_blocks(total, [right, left], down_tile, [-distance, distance])
-        else:
-            (total,) = down_blocks(None, [mine], down_tile, [0])
-        right, left, total = lax.optimization_barrier((next_right, next_left, total))
-    kept, sent = last_down_block(total, right, left, far_tile)
+            after = []
+        total, *fetched = down_blocks(total, hidden, tiles, down_tile, fetch, after)
+        down_tiles += fetched
+        lower_right, lower_left, total = lax.optimization_barrier((lower_right, lower_left, total))
+        hidden = [(upper_right, lower_right), (upper_left, lower_left)]
+    (far_tile,) = down_tiles
+    kept, sent = last_down_block(total, upper_right, lower_left, far_tile)
     summed = kept + from_partner(sent, "tp", 0).astype(F32)
     return (block_in.astype(F32) + summed).astype(BF16)
 

time: 85 us -> 79.1 us (0.931)
  waiting for transfers between devices: 23.6 us -> 16 us
  starting transfers between devices: 18.4 us -> 24.5 us
  Pallas kernels: 40.1 us -> 36.6 us
  local copies, waits for them, and re-layouts: 0.96 us -> 0.09 us
    pallas_call x4, Pallas kernels: 13.5 us -> 4.7 us  [down_blocks(): pl.pallas_call(kernel, out_shape=[jax.ShapeDtypeStruct((rows, width), F32...]
    ppermute x16 -> x22, waiting for transfers between devices: 21.2 us -> 13.8 us  [shift(): return lax.ppermute(value, 'tp', pairs)]
    pallas_call x4, Pallas kernels: 19.9 us -> 26.5 us  [up_blocks(): pl.pallas_call(kernel, out_shape=[jax.ShapeDtypeStruct((rows, LANES + 2 *...]
    ppermute x16 -> x22, starting transfers between devices: 17.8 us -> 23.9 us  [shift(): return lax.ppermute(value, 'tp', pairs)]
    pallas_call x0 -> x1, Pallas kernels: none -> 3.08 us  [fetch_up_block(): pl.pallas_call(kernel, out_shape=jax.ShapeDtypeStruct((2, depth, width),...]
    pallas_call x1, Pallas kernels: 3.48 us -> 1.29 us  [first_up_block(): pl.pallas_call(kernel, out_shape=[jax.ShapeDtypeStruct((rows, LANES + wid...]
    pallas_call x1, Pallas kernels: 2.45 us -> 0.27 us  [add_rows(): pl.pallas_call(kernel, out_shape=[jax.ShapeDtypeStruct((rows, share), BF1...]
    unnamed x4 -> x8, local copies, waits for them, and re-layouts: 0.89 us -> 0.01 us
  transfers between devices with their start and end apart: 18 -> 24, of which waited for: 12 -> 14; matrix products, arithmetic and copies ran while one was open for 1% -> 1% of each run, Pallas kernels for 39% -> 39%
where the time goes in v4:
time: 79.1 us; the launch traced here: 79 us
  Pallas kernels  36.6 us (46%)
  starting transfers between devices  24.5 us (31%)
  waiting for transfers between devices  16 us (20%)
  other arithmetic  1.58 us (2%)
    pallas_call x4, Pallas kernels, up_blocks(): pl.pallas_call(kernel, out_shape=[jax.ShapeDtypeStruct((rows, LANES + 2 *...  26.5 us
    ppermute x22, starting transfers between devices, shift(): return lax.ppermute(value, 'tp', pairs)  23.9 us
    ppermute x22, waiting for transfers between devices, shift(): return lax.ppermute(value, 'tp', pairs)  13.8 us
    pallas_call x4, Pallas kernels, down_blocks(): pl.pallas_call(kernel, out_shape=[jax.ShapeDtypeStruct((rows, width), F32...  4.7 us
    pallas_call x1, Pallas kernels, fetch_up_block(): pl.pallas_call(kernel, out_shape=jax.ShapeDtypeStruct((2, depth, width),...  3.08 us
    ppermute x2, waiting for transfers between devices, from_partner(): return lax.ppermute(value, axis, pairs)  2.16 us
  transfers between devices with their start and end apart: 24, of which 14 were waited for; matrix products, arithmetic and copies ran while one was open for 1% of the time, Pallas kernels for 39%

profile of v4, /device:TPU:0, one launch (start us, length us, event | category | flops | bytes accessed | tf_op | source)
XLA Modules:
  0.0 79.0 jit_solution(13358234897133900769)
XLA Ops:
  0.0 3.1 %fetch_up_block.1.after_ref.tiles_ref = bf16[2,1024,1664]{2,1,0:T(8,128)(2,1)S(1)} custom-call(bf16[1024,13312]{1,0:T(8,128)(2,1)} %bitcast.7, bf16[1024,13312]{1,0:T(8,128)(2,1)} %bitcast.12), custom_call_target="tpu_custom_call" | custom-call | tf_op jit(solution)/shard_map/fetch_up_block/pallas_call | solution.py:112
  4.9 1.3 %first_up_block.1 = (bf16[64,1792]{1,0:T(8,128)(2,1)S(1)}, bf16[64,1664]{1,0:T(8,128)(2,1)S(1)}, bf16[64,1024]{1,0:T(8,128)(2,1)S(1)}, f32[64,128]{1,0:T(8,128)S(1)}) custom-call(bf16[64,640]{1,0:T(8,128)(2,1)S(1)} %get-tuple-element.40.own_ref, bf16[64,640]{1,0:T(8,128)(2,1)S(1)} %collective-permute-done.other_ref, ...), custom_call_target="tpu_custom_call" | custom-call | flops 436207616 | bytes 6815744 | tf_op jit(solution)/shard_map/first_up_block/pallas_call | solution.py:219
  6.2 2.9 %collective-permute-start.2 = (bf16[64,1664]{1,0:T(8,128)(2,1)S(1)}, bf16[64,1664]{1,0:T(8,128)(2,1)S(1)}, u32[]{:S(2)}, u32[]{:S(2)}) collective-permute-start(bf16[64,1664]{1,0:T(8,128)(2,1)S(1)} %get-tuple-element.44.rest_1_), channel_id=1, source_target_pairs={{0,2},{1,3},{4,0},{5,1},{8,4},{9,5},{12,8},{13,9},{14,12},{15,13},... | collective-permute-start | bytes 638984 | tf_op jit(solution)/shard_map/ppermute | solution.py:377
  9.2 5.5 %up_blocks.4 = (f32[64,3456]{1,0:T(8,128)S(1)}, f32[64,3456]{1,0:T(8,128)S(1)}) custom-call(bf16[64,1024]{1,0:T(8,128)(2,1)S(1)} %get-tuple-element.41.x_ref, f32[64,128]{1,0:T(8,128)S(1)} %get-tuple-element.42.squares_ref, bf16[1024,13312]{1,0:T(8,128)(2,1)} %bitcast.8, bf16[1024,13312]{1,0:T(8,128)(2,1)} %bitcast.13, ...), custom_call_target="tpu_custom_call" | custom-call | flops 872415232 | bytes 13631488 | tf_op jit(solution)/shard_map/up_blocks/pallas_call | solution.py:260
  14.8 1.9 %collective-permute-start.4 = (bf16[64,3456]{1,0:T(8,128)(2,1)S(1)}, bf16[64,3456]{1,0:T(8,128)(2,1)S(1)}, u32[]{:S(2)}, u32[]{:S(2)}) collective-permute-start(bf16[64,3456]{1,0:T(8,128)(2,1)S(1)} %pad_maximum_fusion.1.rest_1_), channel_id=1, source_target_pairs={{0,2},{1,3},{4,0},{5,1},{8,4},{9,5},{12,8},{13,9},{14,12},{15,13},... | collective-permute-start | bytes 1327112 | tf_op jit(solution)/shard_map/ppermute | solution.py:377
  17.2 7.0 %up_blocks.5 = (f32[64,3456]{1,0:T(8,128)S(1)}, f32[64,3456]{1,0:T(8,128)S(1)}, bf16[1664,1024]{1,0:T(8,128)(2,1)S(1)}, bf16[1664,1024]{1,0:T(8,128)(2,1)S(1)}) custom-call(bf16[64,1024]{1,0:T(8,128)(2,1)S(1)} %get-tuple-element.41.x_ref, f32[64,128]{1,0:T(8,128)S(1)} %get-tuple-element.42.squares_ref, bf16[1024,13312]{1,0:T(8,128)(2,1)} %bitcast.9, ...), custom_call_target="tpu_custom_call" | custom-call | flops 872415232 | bytes 13631488 | tf_op jit(solution)/shard_map/up_blocks/pallas_call | solution.py:260
  24.2 2.7 %collective-permute-done.4 = bf16[64,3456]{1,0:T(8,128)(2,1)S(1)} collective-permute-done((bf16[64,3456]{1,0:T(8,128)(2,1)S(1)}, bf16[64,3456]{1,0:T(8,128)(2,1)S(1)}, u32[]{:S(2)}, u32[]{:S(2)}) %collective-permute-start.4) | collective-permute-done | bytes 442400 | tf_op jit(solution)/shard_map/ppermute | solution.py:377
  27.0 1.5 %collective-permute-start.6 = (bf16[64,3456]{1,0:T(8,128)(2,1)S(1)}, bf16[64,3456]{1,0:T(8,128)(2,1)S(1)}, u32[]{:S(2)}, u32[]{:S(2)}) collective-permute-start(bf16[64,3456]{1,0:T(8,128)(2,1)S(1)} %add_convert_fusion.2.rest_1_), channel_id=1, source_target_pairs={{0,2},{1,3},{4,0},{5,1},{8,4},{9,5},{12,8},{13,9},{14,12},{15,13},... | collective-permute-start | bytes 1327112 | tf_op jit(solution)/shard_map/ppermute | solution.py:377
  29.3 7.0 %up_blocks.6 = (f32[64,3456]{1,0:T(8,128)S(1)}, f32[64,3456]{1,0:T(8,128)S(1)}, bf16[1664,1024]{1,0:T(8,128)(2,1)S(1)}, bf16[1664,1024]{1,0:T(8,128)(2,1)S(1)}) custom-call(bf16[64,1024]{1,0:T(8,128)(2,1)S(1)} %get-tuple-element.41.x_ref, f32[64,128]{1,0:T(8,128)S(1)} %get-tuple-element.42.squares_ref, bf16[1024,13312]{1,0:T(8,128)(2,1)} %bitcast.10, ...), custom_call_target="tpu_custom_call" | custom-call | flops 872415232 | bytes 13631488 | tf_op jit(solution)/shard_map/up_blocks/pallas_call | solution.py:260
  36.3 1.9 %collective-permute-done.6 = bf16[64,3456]{1,0:T(8,128)(2,1)S(1)} collective-permute-done((bf16[64,3456]{1,0:T(8,128)(2,1)S(1)}, bf16[64,3456]{1,0:T(8,128)(2,1)S(1)}, u32[]{:S(2)}, u32[]{:S(2)}) %collective-permute-start.6) | collective-permute-done | bytes 442400 | tf_op jit(solution)/shard_map/ppermute | solution.py:377
  38.3 1.2 %collective-permute-start.8 = (bf16[64,3456]{1,0:T(8,128)(2,1)S(1)}, bf16[64,3456]{1,0:T(8,128)(2,1)S(1)}, u32[]{:S(2)}, u32[]{:S(2)}) collective-permute-start(bf16[64,3456]{1,0:T(8,128)(2,1)S(1)} %add_convert_fusion.rest_1_), channel_id=1, source_target_pairs={{0,2},{1,3},{4,0},{5,1},{8,4},{9,5},{12,8},{13,9},{14,12},{15,13},... | collective-permute-start | bytes 1327112 | tf_op jit(solution)/shard_map/ppermute | solution.py:377
  40.5 7.0 %up_blocks.7 = (f32[64,3456]{1,0:T(8,128)S(1)}, bf16[1664,1024]{1,0:T(8,128)(2,1)S(1)}, bf16[1664,1024]{1,0:T(8,128)(2,1)S(1)}, bf16[1664,1024]{1,0:T(8,128)(2,1)S(1)}, bf16[1664,1024]{1,0:T(8,128)(2,1)S(1)}) custom-call(bf16[64,1024]{1,0:T(8,128)(2,1)S(1)} %get-tuple-element.41.x_ref, f32[64,128]{1,0:T(8,128)S(1)} %get-tuple-element.42.squares_ref, ...), custom_call_target="tpu_custom_call" | custom-call | flops 436207616 | bytes 6815744 | tf_op jit(solution)/shard_map/up_blocks/pallas_call | solution.py:260
  52.0 1.6 %collective-permute-start.10 = (bf16[32,1664]{1,0:T(8,128)(2,1)S(1)}, bf16[32,1664]{1,0:T(8,128)(2,1)S(1)}, u32[]{:S(2)}, u32[]{:S(2)}) collective-permute-start(bf16[32,1664]{1,0:T(8,128)(2,1)S(1)} %get-tuple-element.74.rest_1_), channel_id=1, source_target_pairs={{0,2},{1,3},{4,0},{5,1},{8,4},{9,5},{12,8},{13,9},{14,12},{15,13},... | collective-permute-start | bytes 319496 | tf_op jit(solution)/shard_map/ppermute | solution.py:377
  58.2 1.2 %collective-permute-done.9.rest_2_ = bf16[32,1664]{1,0:T(8,128)(2,1)S(1)} collective-permute-done((bf16[32,1664]{1,0:T(8,128)(2,1)S(1)}, bf16[32,1664]{1,0:T(8,128)(2,1)S(1)}, u32[]{:S(2)}, u32[]{:S(2)}) %collective-permute-start.9) | collective-permute-done | bytes 106528 | tf_op jit(solution)/shard_map/ppermute | solution.py:377
  59.4 2.0 %collective-permute-start.14 = (bf16[32,1664]{1,0:T(8,128)(2,1)S(1)}, bf16[32,1664]{1,0:T(8,128)(2,1)S(1)}, u32[]{:S(2)}, u32[]{:S(2)}) collective-permute-start(bf16[32,1664]{1,0:T(8,128)(2,1)S(1)} %collective-permute-done.10.rest_4_), channel_id=1, source_target_pairs={{0,2},{1,3},{4,0},{5,1},{8,4},{9,5},{12,8},{13,9},{14,12},{15,13},... | collective-permute-start | bytes 319496 | tf_op jit(solution)/shard_map/ppermute | solution.py:377
  61.4 2.0 %collective-permute-start.20 = (bf16[32,1664]{1,0:T(8,128)(2,1)S(1)}, bf16[32,1664]{1,0:T(8,128)(2,1)S(1)}, u32[]{:S(2)}, u32[]{:S(2)}) collective-permute-start(bf16[32,1664]{1,0:T(8,128)(2,1)S(1)} %collective-permute-done.16.rest_8_.rest_3_), channel_id=1, source_target_pairs={{0,2},{1,3},{4,0},{5,1},{8,4},{9,5},{12,8},{13,9},{14,12},{15,13},... | collective-permute-start | bytes 319496 | tf_op jit(solution)/shard_map/ppermute | solution.py:377
  63.4 1.3 %down_blocks.5.rest_0_ = f32[64,1024]{1,0:T(8,128)S(1)} custom-call(f32[64,1024]{1,0:T(8,128)S(1)} %down_blocks.4.rest_0_, bf16[32,1664]{1,0:T(8,128)(2,1)S(1)} %collective-permute-done.11.rest_3_.rest_1_, bf16[32,1664]{1,0:T(8,128)(2,1)S(1)} %collective-permute-done.9.rest_2_, bf16[32,1664]{1,0:T(8,128)(2,1)S(1)} %collective-permute-done.12.rest_4_.rest_3_, ...), custom_call_target="tpu_custom_call" | custom-call | flops 436207616 | bytes 6815744 | tf_op jit(solution)/shard_map/down_blocks/pallas_call | solution.py:320
  65.4 1.5 %collective-permute-start.18 = (bf16[32,1664]{1,0:T(8,128)(2,1)S(1)}, bf16[32,1664]{1,0:T(8,128)(2,1)S(1)}, u32[]{:S(2)}, u32[]{:S(2)}) collective-permute-start(bf16[32,1664]{1,0:T(8,128)(2,1)S(1)} %collective-permute-done.14.rest_4_), channel_id=1, source_target_pairs={{0,2},{1,3},{4,0},{5,1},{8,4},{9,5},{12,8},{13,9},{14,12},{15,13},... | collective-permute-start | bytes 319496 | tf_op jit(solution)/shard_map/ppermute | solution.py:377
  67.0 1.3 %down_blocks.6.rest_0_ = f32[64,1024]{1,0:T(8,128)S(1)} custom-call(f32[64,1024]{1,0:T(8,128)S(1)} %down_blocks.5.rest_0_, bf16[32,1664]{1,0:T(8,128)(2,1)S(1)} %collective-permute-done.15.rest_7_.rest_1_, bf16[32,1664]{1,0:T(8,128)(2,1)S(1)} %collective-permute-done.13.rest_2_, bf16[32,1664]{1,0:T(8,128)(2,1)S(1)} %collective-permute-done.16.rest_8_.rest_3_, ...), custom_call_target="tpu_custom_call" | custom-call | flops 436207616 | bytes 6815744 | tf_op jit(solution)/shard_map/down_blocks/pallas_call | solution.py:320
  70.1 1.5 %collective-permute-start.21 = (bf16[32,1664]{1,0:T(8,128)(2,1)S(1)}, bf16[32,1664]{1,0:T(8,128)(2,1)S(1)}, u32[]{:S(2)}, u32[]{:S(2)}) collective-permute-start(bf16[32,1664]{1,0:T(8,128)(2,1)S(1)} %collective-permute-done.18.rest_4_), channel_id=1, source_target_pairs={{0,2},{1,3},{4,0},{5,1},{8,4},{9,5},{12,8},{13,9},{14,12},{15,13},... | collective-permute-start | bytes 319496 | tf_op jit(solution)/shard_map/ppermute | solution.py:377
  72.1 1.3 %down_blocks.7.total_ref = f32[64,1024]{1,0:T(8,128)S(1)} custom-call(f32[64,1024]{1,0:T(8,128)S(1)} %down_blocks.6.rest_0_, bf16[32,1664]{1,0:T(8,128)(2,1)S(1)} %collective-permute-done.19.rest_7_.rest_1_, bf16[32,1664]{1,0:T(8,128)(2,1)S(1)} %collective-permute-done.17.rest_2_, bf16[32,1664]{1,0:T(8,128)(2,1)S(1)} %collective-permute-done.20.rest_8_.rest_3_, ...), custom_call_target="tpu_custom_call" | custom-call | flops 436207616 | bytes 6815744 | tf_op jit(solution)/shard_map/down_blocks/pallas_call | solution.py:320
  73.5 1.3 %collective-permute-done.21.lower_ref = bf16[32,1664]{1,0:T(8,128)(2,1)S(1)} collective-permute-done((bf16[32,1664]{1,0:T(8,128)(2,1)S(1)}, bf16[32,1664]{1,0:T(8,128)(2,1)S(1)}, u32[]{:S(2)}, u32[]{:S(2)}) %collective-permute-start.21) | collective-permute-done | bytes 106528 | tf_op jit(solution)/shard_map/ppermute | solution.py:377
  74.8 1.5 %collective-permute-done.22.upper_ref = bf16[32,1664]{1,0:T(8,128)(2,1)S(1)} collective-permute-done((bf16[32,1664]{1,0:T(8,128)(2,1)S(1)}, bf16[32,1664]{1,0:T(8,128)(2,1)S(1)}, u32[]{:S(2)}, u32[]{:S(2)}) %collective-permute-start.22) | collective-permute-done | bytes 106528 | tf_op jit(solution)/shard_map/ppermute | solution.py:377
  77.1 1.2 %collective-permute-done.23 = bf16[64,512]{1,0:T(8,128)(2,1)S(1)} collective-permute-done((bf16[64,512]{1,0:T(8,128)(2,1)S(1)}, bf16[64,512]{1,0:T(8,128)(2,1)S(1)}, u32[]{:S(2)}, u32[]{:S(2)}) %collective-permute-start.23) | collective-permute-done | bytes 65568 | tf_op jit(solution)/shard_map/ppermute | solution.py:22
  (61 shorter events, 17.9 us)
Async XLA Ops:
  3.4 1.5 %collective-permute-start = (bf16[64,640]{1,0:T(8,128)(2,1)S(1)}, bf16[64,640]{1,0:T(8,128)(2,1)S(1)}, u32[]{:S(2)}, u32[]{:S(2)}) collective-permute-start(bf16[64,640]{1,0:T(8,128)(2,1)S(1)} %get-tuple-element.40.own_ref), channel_id=1, source_target_pairs={{0,1},{1,0},{2,3},{3,2},{4,5},{5,4},{6,7},{7,6},{8,9},{9,8},{10,11... | collective-permute-start | bytes 245768 | tf_op jit(solution)/shard_map/ppermute | solution.py:22
  6.2 8.6 %collective-permute-start.2 = (bf16[64,1664]{1,0:T(8,128)(2,1)S(1)}, bf16[64,1664]{1,0:T(8,128)(2,1)S(1)}, u32[]{:S(2)}, u32[]{:S(2)}) collective-permute-start(bf16[64,1664]{1,0:T(8,128)(2,1)S(1)} %get-tuple-element.44.rest_1_), channel_id=1, source_target_pairs={{0,2},{1,3},{4,0},{5,1},{8,4},{9,5},{12,8},{13,9},{14,12},{15,13},... | collective-permute-start | bytes 638984 | tf_op jit(solution)/shard_map/ppermute | solution.py:377
  9.1 7.7 %collective-permute-start.1 = (bf16[64,1792]{1,0:T(8,128)(2,1)S(1)}, bf16[64,1792]{1,0:T(8,128)(2,1)S(1)}, u32[]{:S(2)}, u32[]{:S(2)}) collective-permute-start(bf16[64,1792]{1,0:T(8,128)(2,1)S(1)} %get-tuple-element.43.rest_0_), channel_id=1, source_target_pairs={{0,4},{1,5},{4,8},{5,9},{8,12},{9,13},{12,14},{13,15},{14,10},{15,... | collective-permute-start | bytes 688136 | tf_op jit(solution)/shard_map/ppermute | solution.py:377
  14.8 12.1 %collective-permute-start.4 = (bf16[64,3456]{1,0:T(8,128)(2,1)S(1)}, bf16[64,3456]{1,0:T(8,128)(2,1)S(1)}, u32[]{:S(2)}, u32[]{:S(2)}) collective-permute-start(bf16[64,3456]{1,0:T(8,128)(2,1)S(1)} %pad_maximum_fusion.1.rest_1_), channel_id=1, source_target_pairs={{0,2},{1,3},{4,0},{5,1},{8,4},{9,5},{12,8},{13,9},{14,12},{15,13},... | collective-permute-start | bytes 1327112 | tf_op jit(solution)/shard_map/ppermute | solution.py:377
  16.9 11.7 %collective-permute-start.3 = (bf16[64,3456]{1,0:T(8,128)(2,1)S(1)}, bf16[64,3456]{1,0:T(8,128)(2,1)S(1)}, u32[]{:S(2)}, u32[]{:S(2)}) collective-permute-start(bf16[64,3456]{1,0:T(8,128)(2,1)S(1)} %pad_maximum_fusion.rest_0_), channel_id=1, source_target_pairs={{0,4},{1,5},{4,8},{5,9},{8,12},{9,13},{12,14},{13,15},{14,10},{15,... | collective-permute-start | bytes 1327112 | tf_op jit(solution)/shard_map/ppermute | solution.py:377
  27.0 11.1 %collective-permute-start.6 = (bf16[64,3456]{1,0:T(8,128)(2,1)S(1)}, bf16[64,3456]{1,0:T(8,128)(2,1)S(1)}, u32[]{:S(2)}, u32[]{:S(2)}) collective-permute-start(bf16[64,3456]{1,0:T(8,128)(2,1)S(1)} %add_convert_fusion.2.rest_1_), channel_id=1, source_target_pairs={{0,2},{1,3},{4,0},{5,1},{8,4},{9,5},{12,8},{13,9},{14,12},{15,13},... | collective-permute-start | bytes 1327112 | tf_op jit(solution)/shard_map/ppermute | solution.py:377
  28.7 10.8 %collective-permute-start.5 = (bf16[64,3456]{1,0:T(8,128)(2,1)S(1)}, bf16[64,3456]{1,0:T(8,128)(2,1)S(1)}, u32[]{:S(2)}, u32[]{:S(2)}) collective-permute-start(bf16[64,3456]{1,0:T(8,128)(2,1)S(1)} %add_convert_fusion.3.rest_0_), channel_id=1, source_target_pairs={{0,4},{1,5},{4,8},{5,9},{8,12},{9,13},{12,14},{13,15},{14,10},{15,... | collective-permute-start | bytes 1327112 | tf_op jit(solution)/shard_map/ppermute | solution.py:377
  38.3 10.2 %collective-permute-start.8 = (bf16[64,3456]{1,0:T(8,128)(2,1)S(1)}, bf16[64,3456]{1,0:T(8,128)(2,1)S(1)}, u32[]{:S(2)}, u32[]{:S(2)}) collective-permute-start(bf16[64,3456]{1,0:T(8,128)(2,1)S(1)} %add_convert_fusion.rest_1_), channel_id=1, source_target_pairs={{0,2},{1,3},{4,0},{5,1},{8,4},{9,5},{12,8},{13,9},{14,12},{15,13},... | collective-permute-start | bytes 1327112 | tf_op jit(solution)/shard_map/ppermute | solution.py:377
  39.6 9.8 %collective-permute-start.7 = (bf16[64,3456]{1,0:T(8,128)(2,1)S(1)}, bf16[64,3456]{1,0:T(8,128)(2,1)S(1)}, u32[]{:S(2)}, u32[]{:S(2)}) collective-permute-start(bf16[64,3456]{1,0:T(8,128)(2,1)S(1)} %add_convert_fusion.1.rest_0_), channel_id=1, source_target_pairs={{0,4},{1,5},{4,8},{5,9},{8,12},{9,13},{12,14},{13,15},{14,10},{15,... | collective-permute-start | bytes 1327112 | tf_op jit(solution)/shard_map/ppermute | solution.py:377
  49.9 5.2 %collective-permute-start.11 = (bf16[32,1664]{1,0:T(8,128)(2,1)S(1)}, bf16[32,1664]{1,0:T(8,128)(2,1)S(1)}, u32[]{:S(2)}, u32[]{:S(2)}) collective-permute-start(bf16[32,1664]{1,0:T(8,128)(2,1)S(1)} %get-tuple-element.73.rest_0_), channel_id=1, source_target_pairs={{0,4},{1,5},{4,8},{5,9},{8,12},{9,13},{12,14},{13,15},{14,10},{15,... | collective-permute-start | bytes 319496 | tf_op jit(solution)/shard_map/ppermute | solution.py:377
  50.9 5.3 %collective-permute-start.12 = (bf16[32,1664]{1,0:T(8,128)(2,1)S(1)}, bf16[32,1664]{1,0:T(8,128)(2,1)S(1)}, u32[]{:S(2)}, u32[]{:S(2)}) collective-permute-start(bf16[32,1664]{1,0:T(8,128)(2,1)S(1)} %get-tuple-element.73.rest_0_), channel_id=1, source_target_pairs={{0,2},{1,3},{4,0},{5,1},{8,4},{9,5},{12,8},{13,9},{14,12},{15,13},... | collective-permute-start | bytes 319496 | tf_op jit(solution)/shard_map/ppermute | solution.py:377
  52.0 6.2 %collective-permute-start.10 = (bf16[32,1664]{1,0:T(8,128)(2,1)S(1)}, bf16[32,1664]{1,0:T(8,128)(2,1)S(1)}, u32[]{:S(2)}, u32[]{:S(2)}) collective-permute-start(bf16[32,1664]{1,0:T(8,128)(2,1)S(1)} %get-tuple-element.74.rest_1_), channel_id=1, source_target_pairs={{0,2},{1,3},{4,0},{5,1},{8,4},{9,5},{12,8},{13,9},{14,12},{15,13},... | collective-permute-start | bytes 319496 | tf_op jit(solution)/shard_map/ppermute | solution.py:377
  53.5 5.8 %collective-permute-start.9 = (bf16[32,1664]{1,0:T(8,128)(2,1)S(1)}, bf16[32,1664]{1,0:T(8,128)(2,1)S(1)}, u32[]{:S(2)}, u32[]{:S(2)}) collective-permute-start(bf16[32,1664]{1,0:T(8,128)(2,1)S(1)} %get-tuple-element.74.rest_1_), channel_id=1, source_target_pairs={{0,4},{1,5},{4,8},{5,9},{8,12},{9,13},{12,14},{13,15},{14,10},{15,... | collective-permute-start | bytes 319496 | tf_op jit(solution)/shard_map/ppermute | solution.py:377
  55.1 6.3 %collective-permute-start.15 = (bf16[32,1664]{1,0:T(8,128)(2,1)S(1)}, bf16[32,1664]{1,0:T(8,128)(2,1)S(1)}, u32[]{:S(2)}, u32[]{:S(2)}) collective-permute-start(bf16[32,1664]{1,0:T(8,128)(2,1)S(1)} %collective-permute-done.11.rest_3_.rest_1_), channel_id=1, source_target_pairs={{0,4},{1,5},{4,8},{5,9},{8,12},{9,13},{12,14},{13,15},{14,10},{15,... | collective-permute-start | bytes 319496 | tf_op jit(solution)/shard_map/ppermute | solution.py:377
  56.3 5.1 %collective-permute-start.16 = (bf16[32,1664]{1,0:T(8,128)(2,1)S(1)}, bf16[32,1664]{1,0:T(8,128)(2,1)S(1)}, u32[]{:S(2)}, u32[]{:S(2)}) collective-permute-start(bf16[32,1664]{1,0:T(8,128)(2,1)S(1)} %collective-permute-done.12.rest_4_.rest_3_), channel_id=1, source_target_pairs={{0,2},{1,3},{4,0},{5,1},{8,4},{9,5},{12,8},{13,9},{14,12},{15,13},... | collective-permute-start | bytes 319496 | tf_op jit(solution)/shard_map/ppermute | solution.py:377
  59.3 5.4 %collective-permute-start.13 = (bf16[32,1664]{1,0:T(8,128)(2,1)S(1)}, bf16[32,1664]{1,0:T(8,128)(2,1)S(1)}, u32[]{:S(2)}, u32[]{:S(2)}) collective-permute-start(bf16[32,1664]{1,0:T(8,128)(2,1)S(1)} %collective-permute-done.9.rest_2_), channel_id=1, source_target_pairs={{0,4},{1,5},{4,8},{5,9},{8,12},{9,13},{12,14},{13,15},{14,10},{15,... | collective-permute-start | bytes 319496 | tf_op jit(solution)/shard_map/ppermute | solution.py:377
  59.4 5.4 %collective-permute-start.14 = (bf16[32,1664]{1,0:T(8,128)(2,1)S(1)}, bf16[32,1664]{1,0:T(8,128)(2,1)S(1)}, u32[]{:S(2)}, u32[]{:S(2)}) collective-permute-start(bf16[32,1664]{1,0:T(8,128)(2,1)S(1)} %collective-permute-done.10.rest_4_), channel_id=1, source_target_pairs={{0,2},{1,3},{4,0},{5,1},{8,4},{9,5},{12,8},{13,9},{14,12},{15,13},... | collective-permute-start | bytes 319496 | tf_op jit(solution)/shard_map/ppermute | solution.py:377
  61.4 5.5 %collective-permute-start.19 = (bf16[32,1664]{1,0:T(8,128)(2,1)S(1)}, bf16[32,1664]{1,0:T(8,128)(2,1)S(1)}, u32[]{:S(2)}, u32[]{:S(2)}) collective-permute-start(bf16[32,1664]{1,0:T(8,128)(2,1)S(1)} %collective-permute-done.15.rest_7_.rest_1_), channel_id=1, source_target_pairs={{0,4},{1,5},{4,8},{5,9},{8,12},{9,13},{12,14},{13,15},{14,10},{15,... | collective-permute-start | bytes 319496 | tf_op jit(solution)/shard_map/ppermute | solution.py:377
  61.4 5.7 %collective-permute-start.20 = (bf16[32,1664]{1,0:T(8,128)(2,1)S(1)}, bf16[32,1664]{1,0:T(8,128)(2,1)S(1)}, u32[]{:S(2)}, u32[]{:S(2)}) collective-permute-start(bf16[32,1664]{1,0:T(8,128)(2,1)S(1)} %collective-permute-done.16.rest_8_.rest_3_), channel_id=1, source_target_pairs={{0,2},{1,3},{4,0},{5,1},{8,4},{9,5},{12,8},{13,9},{14,12},{15,13},... | collective-permute-start | bytes 319496 | tf_op jit(solution)/shard_map/ppermute | solution.py:377
  64.8 4.8 %collective-permute-start.17 = (bf16[32,1664]{1,0:T(8,128)(2,1)S(1)}, bf16[32,1664]{1,0:T(8,128)(2,1)S(1)}, u32[]{:S(2)}, u32[]{:S(2)}) collective-permute-start(bf16[32,1664]{1,0:T(8,128)(2,1)S(1)} %collective-permute-done.13.rest_2_), channel_id=1, source_target_pairs={{0,4},{1,5},{4,8},{5,9},{8,12},{9,13},{12,14},{13,15},{14,10},{15,... | collective-permute-start | bytes 319496 | tf_op jit(solution)/shard_map/ppermute | solution.py:377
  65.4 4.7 %collective-permute-start.18 = (bf16[32,1664]{1,0:T(8,128)(2,1)S(1)}, bf16[32,1664]{1,0:T(8,128)(2,1)S(1)}, u32[]{:S(2)}, u32[]{:S(2)}) collective-permute-start(bf16[32,1664]{1,0:T(8,128)(2,1)S(1)} %collective-permute-done.14.rest_4_), channel_id=1, source_target_pairs={{0,2},{1,3},{4,0},{5,1},{8,4},{9,5},{12,8},{13,9},{14,12},{15,13},... | collective-permute-start | bytes 319496 | tf_op jit(solution)/shard_map/ppermute | solution.py:377
  70.1 4.7 %collective-permute-start.21 = (bf16[32,1664]{1,0:T(8,128)(2,1)S(1)}, bf16[32,1664]{1,0:T(8,128)(2,1)S(1)}, u32[]{:S(2)}, u32[]{:S(2)}) collective-permute-start(bf16[32,1664]{1,0:T(8,128)(2,1)S(1)} %collective-permute-done.18.rest_4_), channel_id=1, source_target_pairs={{0,2},{1,3},{4,0},{5,1},{8,4},{9,5},{12,8},{13,9},{14,12},{15,13},... | collective-permute-start | bytes 319496 | tf_op jit(solution)/shard_map/ppermute | solution.py:377
  71.5 4.7 %collective-permute-start.22 = (bf16[32,1664]{1,0:T(8,128)(2,1)S(1)}, bf16[32,1664]{1,0:T(8,128)(2,1)S(1)}, u32[]{:S(2)}, u32[]{:S(2)}) collective-permute-start(bf16[32,1664]{1,0:T(8,128)(2,1)S(1)} %collective-permute-done.19.rest_7_.rest_1_), channel_id=1, source_target_pairs={{0,4},{1,5},{4,8},{5,9},{8,12},{9,13},{12,14},{13,15},{14,10},{15,... | collective-permute-start | bytes 319496 | tf_op jit(solution)/shard_map/ppermute | solution.py:377
  77.0 1.3 %collective-permute-start.23 = (bf16[64,512]{1,0:T(8,128)(2,1)S(1)}, bf16[64,512]{1,0:T(8,128)(2,1)S(1)}, u32[]{:S(2)}, u32[]{:S(2)}) collective-permute-start(bf16[64,512]{1,0:T(8,128)(2,1)S(1)} %get-tuple-element.72), channel_id=1, source_target_pairs={{0,1},{1,0},{2,3},{3,2},{4,5},{5,4},{6,7},{7,6},{8,9},{9,8},{10,11... | collective-permute-start | bytes 196616 | tf_op jit(solution)/shard_map/ppermute | solution.py:22
  (4 other events, 12.5 us)

commit v5 on v4

--- a/solution.py
+++ b/solution.py
@@ -155,7 +155,7 @@
     )(token_ids, stream, table_rows, gain, after)
 
 
-def start_up_copies(block, gate_ref, up_ref, tiles, arrived):
+def start_up_copies(block, gate_ref, up_ref, tiles, arrived, gate_here=None):
     cuts = arrived.shape[1]
     cut = gate_ref.shape[0] // cuts
     width = gate_ref.shape[1] // D_WAYS
@@ -167,7 +167,10 @@
             copy = pltpu.make_async_copy(
                 ref.at[pl.ds(c * cut, cut), columns], tiles.at[m, pl.ds(c * cut, cut), :], arrived.at[m, c]
             )
-            copy.start()
+            if m == 0 and gate_here is not None:
+                pl.when(jnp.logical_not(gate_here))(copy.start)
+            else:
+                copy.start()
             copies.append((m, features, copy))
     return copies
 
@@ -182,6 +185,18 @@
             out_refs[m][...] += product
 
 
+def up_products_ahead(x_ref, copies, tiles, out_refs, gate_here, ahead_ref):
+    @pl.when(gate_here)
+    def _():
+        out_refs[0][...] = jnp.dot(x_ref[...], ahead_ref[...], preferred_element_type=F32)
+
+    @pl.when(jnp.logical_not(gate_here))
+    def _():
+        up_products(x_ref, [copy for copy in copies if copy[0] == 0], tiles, out_refs)
+
+    up_products(x_ref, [copy for copy in copies if copy[0] == 1], tiles, out_refs)
+
+
 def up_scratch(count, depth, width):
     cuts = 2
     return [
@@ -198,14 +213,21 @@
     )
 
 
-def first_up_block(own, other, tiles):
+def first_up_block(own, other, tiles, gate_tile):
     _, depth, width = tiles.shape
     rows = own.shape[0]
     share = own.shape[1] - LANES
 
-    def kernel(own_ref, other_ref, tiles_ref, gate_out, up_out, x_ref, squares_ref):
-        _, side, _ = position()
+    def kernel(own_ref, other_ref, tiles_ref, gate_ref, gate_out, up_out, x_ref, squares_ref, ahead_ref, arrived):
+        _, side, place = position()
         high = side == 1
+        columns = pl.ds(pl.multiple_of(at(place, 3) * width, LANES), width)
+        copy = pltpu.make_async_copy(gate_ref.at[:, columns], ahead_ref, arrived)
+
+        @pl.when(side == 0)
+        def _():
+            copy.start()
+
         own_x, other_x = own_ref[:, :share], other_ref[:, :share]
         x_ref[:, :share] = jnp.where(high, other_x, own_x)
         x_ref[:, share:] = jnp.where(high, own_x, other_x)
@@ -216,6 +238,10 @@
         gate_out[:, LANES:] = jnp.dot(x, tiles_ref[0], preferred_element_type=F32).astype(BF16)
         up_out[...] = jnp.dot(x, tiles_ref[1], preferred_element_type=F32).astype(BF16)
 
+        @pl.when(side == 0)
+        def _():
+            copy.wait()
+
     return pl.pallas_call(
         kernel,
         out_shape=[
@@ -223,37 +249,52 @@
             jax.ShapeDtypeStruct((rows, width), BF16),
             jax.ShapeDtypeStruct((rows, depth), BF16),
             jax.ShapeDtypeStruct((rows, LANES), F32),
+            jax.ShapeDtypeStruct((depth, width), BF16),
         ],
-        in_specs=[IN_VMEM] * 3,
-        out_specs=[IN_VMEM] * 4,
+        in_specs=[IN_VMEM] * 3 + [IN_HBM],
+        out_specs=[IN_VMEM] * 5,
+        scratch_shapes=[pltpu.SemaphoreType.DMA],
         compiler_params=params(),
         cost_estimate=up_cost(1, rows, depth, width),
         name="first_up_block",
-    )(own, other, tiles)
-
-
-def up_blocks(x, squares, gate_tile, up_tile, distances, after, down_tile=None, fetch=()):
+    )(own, other, tiles, gate_tile)
+
+
+def up_blocks(x, squares, gate_tile, up_tile, distances, after, down_tile=None, fetch=(), ahead_tile=None):
     depth, units = gate_tile.shape
     width = units // D_WAYS
     rows = x.shape[0]
     count = len(distances)
     downs = [down_tile] if fetch else []
+    aheads = [] if ahead_tile is None else [ahead_tile]
 
     def kernel(x_ref, squares_ref, gate_ref, up_ref, *rest):
         rest = rest[len(after) :]
         down_refs, rest = rest[: len(downs)], rest[len(downs) :]
+        ahead_refs, rest = rest[: len(aheads)], rest[len(aheads) :]
         out_refs, fetched = rest[:count], rest[count : count + len(fetch)]
         tiles, arrived, fetch_arrived = rest[-3:]
-        _, _, place = position()
+        _, side, place = position()
+        here = side == 0
         copies = [
-            start_up_copies(at(place, distance), gate_ref, up_ref, tiles.at[j], arrived.at[j])
+            start_up_copies(
+                at(place, distance),
+                gate_ref,
+                up_ref,
+                tiles.at[j],
+                arrived.at[j],
+                here if j == 0 and aheads else None,
+            )
             for j, distance in enumerate(distances)
         ]
         ahead = start_down_copies(place, fetch, down_refs, fetched, fetch_arrived)
         for j, out_ref in enumerate(out_refs):
             out_ref[:, :LANES] = squares_ref[...]
             pair = [out_ref.at[:, pl.ds(LANES, width)], out_ref.at[:, pl.ds(LANES + width, width)]]
-            up_products(x_ref, copies[j], tiles.at[j], pair)
+            if j == 0 and aheads:
+                up_products_ahead(x_ref, copies[j], tiles.at[j], pair, here, ahead_refs[0])
+            else:
+                up_products(x_ref, copies[j], tiles.at[j], pair)
         for copy in ahead:
             copy.wait()
 
@@ -261,13 +302,17 @@
         kernel,
         out_shape=[jax.ShapeDtypeStruct((rows, LANES + 2 * width), F32)] * count
         + [jax.ShapeDtypeStruct(down_tile_shape(down_tile), BF16) for _ in fetch],
-        in_specs=[IN_VMEM] * 2 + [IN_HBM] * 2 + [IN_PLACE] * len(after) + [IN_HBM] * len(downs),
+        in_specs=[IN_VMEM] * 2
+        + [IN_HBM] * 2
+        + [IN_PLACE] * len(after)
+        + [IN_HBM] * len(downs)
+        + [IN_VMEM] * len(aheads),
         out_specs=[IN_VMEM] * (count + len(fetch)),
         scratch_shapes=up_scratch(count, depth, width) + [pltpu.SemaphoreType.DMA((max(len(fetch), 1),))],
         compiler_params=params(26 if count == 2 else 14),
         cost_estimate=up_cost(count, rows, depth, width),
         name="up_blocks",
-    )(x, squares, gate_tile, up_tile, *after, *downs)
+    )(x, squares, gate_tile, up_tile, *after, *downs, *aheads)
 
 
 def down_tile_shape(down_tile):
@@ -380,12 +425,13 @@
     block_in, own = add_rows(token_ids, stream, table_rows, norm_gain[None], far_tiles)
     other = from_partner(own, "tp", 0)
 
-    right, left, scaled, squares = first_up_block(own, other, far_tiles)
+    right, left, scaled, squares, ahead_tile = first_up_block(own, other, far_tiles, gate_tile)
     split = LANES + width
     down_tiles = []
     for distance, fetch in ((3, ()), (2, (0, -1)), (1, (1, -2)), (0, (2, -3, 3, 4))):
         distances = [distance, -distance] if distance else [0]
-        found = up_blocks(scaled, squares, gate_tile, up_tile, distances, [right, left], down_tile, fetch)
+        ahead = ahead_tile if distance == 3 else None
+        found = up_blocks(scaled, squares, gate_tile, up_tile, distances, [right, left], down_tile, fetch, ahead)
         own = found[: len(distances)]
         down_tiles += found[len(distances) :]
         right, left = shift(right, 1), shift(left, -1)

time: 79.1 us -> 78.2 us (0.989)
  waiting for transfers between devices: 16 us -> 13.8 us
  Pallas kernels: 36.6 us -> 37.4 us
    ppermute x22, waiting for transfers between devices: 13.8 us -> 11.7 us  [shift(): return lax.ppermute(value, 'tp', pairs)]
    pallas_call x1, Pallas kernels: 1.29 us -> 3.13 us  [first_up_block(): pl.pallas_call(kernel, out_shape=[jax.ShapeDtypeStruct((rows, LANES + wid...]
    pallas_call x4, Pallas kernels: 26.5 us -> 25.5 us  [up_blocks(): pl.pallas_call(kernel, out_shape=[jax.ShapeDtypeStruct((rows, LANES + 2 *...]
  transfers between devices with their start and end apart: 24 -> 24, of which waited for: 14 -> 15; matrix products, arithmetic and copies ran while one was open for 1% -> 1% of each run, Pallas kernels for 39% -> 39%
where the time goes in v5:
time: 78.2 us; the launch traced here: 78.1 us
  Pallas kernels  37.4 us (48%)
  starting transfers between devices  24.8 us (32%)
  waiting for transfers between devices  13.8 us (18%)
  other arithmetic  1.58 us (2%)
    pallas_call x4, Pallas kernels, up_blocks(): pl.pallas_call(kernel, out_shape=[jax.ShapeDtypeStruct((rows, LANES + 2 *...  25.5 us
    ppermute x22, starting transfers between devices, shift(): return lax.ppermute(value, 'tp', pairs)  24.2 us
    ppermute x22, waiting for transfers between devices, shift(): return lax.ppermute(value, 'tp', pairs)  11.7 us
    pallas_call x4, Pallas kernels, down_blocks(): pl.pallas_call(kernel, out_shape=[jax.ShapeDtypeStruct((rows, width), F32...  4.71 us
    pallas_call x1, Pallas kernels, first_up_block(): pl.pallas_call(kernel, out_shape=[jax.ShapeDtypeStruct((rows, LANES + wid...  3.13 us
    pallas_call x1, Pallas kernels, fetch_up_block(): pl.pallas_call(kernel, out_shape=jax.ShapeDtypeStruct((2, depth, width),...  3.08 us
    ppermute x2, waiting for transfers between devices, from_partner(): return lax.ppermute(value, axis, pairs)  2.16 us
  transfers between devices with their start and end apart: 24, of which 15 were waited for; matrix products, arithmetic and copies ran while one was open for 1% of the time, Pallas kernels for 39%

profile of v5, /device:TPU:0, one launch (start us, length us, event | category | flops | bytes accessed | tf_op | source)
XLA Modules:
  0.0 78.1 jit_solution(7438681006479046256)
XLA Ops:
  0.0 3.1 %fetch_up_block.1.after_ref.tiles_ref = bf16[2,1024,1664]{2,1,0:T(8,128)(2,1)S(1)} custom-call(bf16[1024,13312]{1,0:T(8,128)(2,1)} %bitcast.7, bf16[1024,13312]{1,0:T(8,128)(2,1)} %bitcast.13), custom_call_target="tpu_custom_call" | custom-call | tf_op jit(solution)/shard_map/fetch_up_block/pallas_call | solution.py:112
  4.9 3.1 %first_up_block.1 = (bf16[64,1792]{1,0:T(8,128)(2,1)S(1)}, bf16[64,1664]{1,0:T(8,128)(2,1)S(1)}, bf16[64,1024]{1,0:T(8,128)(2,1)S(1)}, f32[64,128]{1,0:T(8,128)S(1)}, bf16[1024,1664]{1,0:T(8,128)(2,1)S(1)}) custom-call(bf16[64,640]{1,0:T(8,128)(2,1)S(1)} %get-tuple-element.41.own_ref, bf16[64,640]{1,0:T(8,128)(2,1)S(1)} %collective-permute-done.other_ref, ...), custom_call_target="tpu_custom_call" | custom-call | flops 436207616 | bytes 6815744 | tf_op jit(solution)/shard_map/first_up_block/pallas_call | solution.py:245
  8.0 2.9 %collective-permute-start.2 = (bf16[64,1664]{1,0:T(8,128)(2,1)S(1)}, bf16[64,1664]{1,0:T(8,128)(2,1)S(1)}, u32[]{:S(2)}, u32[]{:S(2)}) collective-permute-start(bf16[64,1664]{1,0:T(8,128)(2,1)S(1)} %get-tuple-element.45.rest_1_), channel_id=1, source_target_pairs={{0,2},{1,3},{4,0},{5,1},{8,4},{9,5},{12,8},{13,9},{14,12},{15,13},... | collective-permute-start | bytes 638984 | tf_op jit(solution)/shard_map/ppermute | solution.py:422
  11.1 4.5 %up_blocks.4 = (f32[64,3456]{1,0:T(8,128)S(1)}, f32[64,3456]{1,0:T(8,128)S(1)}) custom-call(bf16[64,1024]{1,0:T(8,128)(2,1)S(1)} %get-tuple-element.42.x_ref, f32[64,128]{1,0:T(8,128)S(1)} %get-tuple-element.43.squares_ref, bf16[1024,13312]{1,0:T(8,128)(2,1)} %bitcast.9, bf16[1024,13312]{1,0:T(8,128)(2,1)} %bitcast.14, ...), custom_call_target="tpu_custom_call" | custom-call | flops 872415232 | bytes 13631488 | tf_op jit(solution)/shard_map/up_blocks/pallas_call | solution.py:301
  15.7 1.9 %collective-permute-start.4 = (bf16[64,3456]{1,0:T(8,128)(2,1)S(1)}, bf16[64,3456]{1,0:T(8,128)(2,1)S(1)}, u32[]{:S(2)}, u32[]{:S(2)}) collective-permute-start(bf16[64,3456]{1,0:T(8,128)(2,1)S(1)} %pad_maximum_fusion.1.rest_1_), channel_id=1, source_target_pairs={{0,2},{1,3},{4,0},{5,1},{8,4},{9,5},{12,8},{13,9},{14,12},{15,13},... | collective-permute-start | bytes 1327112 | tf_op jit(solution)/shard_map/ppermute | solution.py:422
  18.1 7.0 %up_blocks.5 = (f32[64,3456]{1,0:T(8,128)S(1)}, f32[64,3456]{1,0:T(8,128)S(1)}, bf16[1664,1024]{1,0:T(8,128)(2,1)S(1)}, bf16[1664,1024]{1,0:T(8,128)(2,1)S(1)}) custom-call(bf16[64,1024]{1,0:T(8,128)(2,1)S(1)} %get-tuple-element.42.x_ref, f32[64,128]{1,0:T(8,128)S(1)} %get-tuple-element.43.squares_ref, bf16[1024,13312]{1,0:T(8,128)(2,1)} %bitcast.10, ...), custom_call_target="tpu_custom_call" | custom-call | flops 872415232 | bytes 13631488 | tf_op jit(solution)/shard_map/up_blocks/pallas_call | solution.py:301
  25.1 1.8 %collective-permute-done.4 = bf16[64,3456]{1,0:T(8,128)(2,1)S(1)} collective-permute-done((bf16[64,3456]{1,0:T(8,128)(2,1)S(1)}, bf16[64,3456]{1,0:T(8,128)(2,1)S(1)}, u32[]{:S(2)}, u32[]{:S(2)}) %collective-permute-start.4) | collective-permute-done | bytes 442400 | tf_op jit(solution)/shard_map/ppermute | solution.py:422
  27.1 1.5 %collective-permute-start.6 = (bf16[64,3456]{1,0:T(8,128)(2,1)S(1)}, bf16[64,3456]{1,0:T(8,128)(2,1)S(1)}, u32[]{:S(2)}, u32[]{:S(2)}) collective-permute-start(bf16[64,3456]{1,0:T(8,128)(2,1)S(1)} %add_convert_fusion.2.rest_1_), channel_id=1, source_target_pairs={{0,2},{1,3},{4,0},{5,1},{8,4},{9,5},{12,8},{13,9},{14,12},{15,13},... | collective-permute-start | bytes 1327112 | tf_op jit(solution)/shard_map/ppermute | solution.py:422
  29.3 7.0 %up_blocks.6 = (f32[64,3456]{1,0:T(8,128)S(1)}, f32[64,3456]{1,0:T(8,128)S(1)}, bf16[1664,1024]{1,0:T(8,128)(2,1)S(1)}, bf16[1664,1024]{1,0:T(8,128)(2,1)S(1)}) custom-call(bf16[64,1024]{1,0:T(8,128)(2,1)S(1)} %get-tuple-element.42.x_ref, f32[64,128]{1,0:T(8,128)S(1)} %get-tuple-element.43.squares_ref, bf16[1024,13312]{1,0:T(8,128)(2,1)} %bitcast.11, ...), custom_call_target="tpu_custom_call" | custom-call | flops 872415232 | bytes 13631488 | tf_op jit(solution)/shard_map/up_blocks/pallas_call | solution.py:301
  37.4 1.5 %collective-permute-start.8 = (bf16[64,3456]{1,0:T(8,128)(2,1)S(1)}, bf16[64,3456]{1,0:T(8,128)(2,1)S(1)}, u32[]{:S(2)}, u32[]{:S(2)}) collective-permute-start(bf16[64,3456]{1,0:T(8,128)(2,1)S(1)} %add_convert_fusion.rest_1_), channel_id=1, source_target_pairs={{0,2},{1,3},{4,0},{5,1},{8,4},{9,5},{12,8},{13,9},{14,12},{15,13},... | collective-permute-start | bytes 1327112 | tf_op jit(solution)/shard_map/ppermute | solution.py:422
  39.6 7.0 %up_blocks.7 = (f32[64,3456]{1,0:T(8,128)S(1)}, bf16[1664,1024]{1,0:T(8,128)(2,1)S(1)}, bf16[1664,1024]{1,0:T(8,128)(2,1)S(1)}, bf16[1664,1024]{1,0:T(8,128)(2,1)S(1)}, bf16[1664,1024]{1,0:T(8,128)(2,1)S(1)}) custom-call(bf16[64,1024]{1,0:T(8,128)(2,1)S(1)} %get-tuple-element.42.x_ref, f32[64,128]{1,0:T(8,128)S(1)} %get-tuple-element.43.squares_ref, ...), custom_call_target="tpu_custom_call" | custom-call | flops 436207616 | bytes 6815744 | tf_op jit(solution)/shard_map/up_blocks/pallas_call | solution.py:301
  46.7 2.1 %collective-permute-done.7 = bf16[64,3456]{1,0:T(8,128)(2,1)S(1)} collective-permute-done((bf16[64,3456]{1,0:T(8,128)(2,1)S(1)}, bf16[64,3456]{1,0:T(8,128)(2,1)S(1)}, u32[]{:S(2)}, u32[]{:S(2)}) %collective-permute-start.7) | collective-permute-done | bytes 442400 | tf_op jit(solution)/shard_map/ppermute | solution.py:422
  49.9 1.5 %collective-permute-start.12 = (bf16[32,1664]{1,0:T(8,128)(2,1)S(1)}, bf16[32,1664]{1,0:T(8,128)(2,1)S(1)}, u32[]{:S(2)}, u32[]{:S(2)}) collective-permute-start(bf16[32,1664]{1,0:T(8,128)(2,1)S(1)} %get-tuple-element.75.rest_0_), channel_id=1, source_target_pairs={{0,2},{1,3},{4,0},{5,1},{8,4},{9,5},{12,8},{13,9},{14,12},{15,13},... | collective-permute-start | bytes 319496 | tf_op jit(solution)/shard_map/ppermute | solution.py:422
  51.4 1.6 %collective-permute-start.10 = (bf16[32,1664]{1,0:T(8,128)(2,1)S(1)}, bf16[32,1664]{1,0:T(8,128)(2,1)S(1)}, u32[]{:S(2)}, u32[]{:S(2)}) collective-permute-start(bf16[32,1664]{1,0:T(8,128)(2,1)S(1)} %get-tuple-element.76.rest_1_), channel_id=1, source_target_pairs={{0,2},{1,3},{4,0},{5,1},{8,4},{9,5},{12,8},{13,9},{14,12},{15,13},... | collective-permute-start | bytes 319496 | tf_op jit(solution)/shard_map/ppermute | solution.py:422
  55.2 1.6 %collective-permute-start.16 = (bf16[32,1664]{1,0:T(8,128)(2,1)S(1)}, bf16[32,1664]{1,0:T(8,128)(2,1)S(1)}, u32[]{:S(2)}, u32[]{:S(2)}) collective-permute-start(bf16[32,1664]{1,0:T(8,128)(2,1)S(1)} %collective-permute-done.12.rest_4_.rest_3_), channel_id=1, source_target_pairs={{0,2},{1,3},{4,0},{5,1},{8,4},{9,5},{12,8},{13,9},{14,12},{15,13},... | collective-permute-start | bytes 319496 | tf_op jit(solution)/shard_map/ppermute | solution.py:422
  57.7 1.5 %collective-permute-start.13 = (bf16[32,1664]{1,0:T(8,128)(2,1)S(1)}, bf16[32,1664]{1,0:T(8,128)(2,1)S(1)}, u32[]{:S(2)}, u32[]{:S(2)}) collective-permute-start(bf16[32,1664]{1,0:T(8,128)(2,1)S(1)} %collective-permute-done.9.rest_2_), channel_id=1, source_target_pairs={{0,4},{1,5},{4,8},{5,9},{8,12},{9,13},{12,14},{13,15},{14,10},{15,... | collective-permute-start | bytes 319496 | tf_op jit(solution)/shard_map/ppermute | solution.py:422
  59.7 1.5 %collective-permute-start.19 = (bf16[32,1664]{1,0:T(8,128)(2,1)S(1)}, bf16[32,1664]{1,0:T(8,128)(2,1)S(1)}, u32[]{:S(2)}, u32[]{:S(2)}) collective-permute-start(bf16[32,1664]{1,0:T(8,128)(2,1)S(1)} %collective-permute-done.15.rest_7_.rest_1_), channel_id=1, source_target_pairs={{0,4},{1,5},{4,8},{5,9},{8,12},{9,13},{12,14},{13,15},{14,10},{15,... | collective-permute-start | bytes 319496 | tf_op jit(solution)/shard_map/ppermute | solution.py:422
  62.2 1.3 %down_blocks.5.rest_0_ = f32[64,1024]{1,0:T(8,128)S(1)} custom-call(f32[64,1024]{1,0:T(8,128)S(1)} %down_blocks.4.rest_0_, bf16[32,1664]{1,0:T(8,128)(2,1)S(1)} %collective-permute-done.11.rest_3_.rest_1_, bf16[32,1664]{1,0:T(8,128)(2,1)S(1)} %collective-permute-done.9.rest_2_, bf16[32,1664]{1,0:T(8,128)(2,1)S(1)} %collective-permute-done.12.rest_4_.rest_3_, ...), custom_call_target="tpu_custom_call" | custom-call | flops 436207616 | bytes 6815744 | tf_op jit(solution)/shard_map/down_blocks/pallas_call | solution.py:365
  66.5 1.3 %down_blocks.6.rest_0_ = f32[64,1024]{1,0:T(8,128)S(1)} custom-call(f32[64,1024]{1,0:T(8,128)S(1)} %down_blocks.5.rest_0_, bf16[32,1664]{1,0:T(8,128)(2,1)S(1)} %collective-permute-done.15.rest_7_.rest_1_, bf16[32,1664]{1,0:T(8,128)(2,1)S(1)} %collective-permute-done.13.rest_2_, bf16[32,1664]{1,0:T(8,128)(2,1)S(1)} %collective-permute-done.16.rest_8_.rest_3_, ...), custom_call_target="tpu_custom_call" | custom-call | flops 436207616 | bytes 6815744 | tf_op jit(solution)/shard_map/down_blocks/pallas_call | solution.py:365
  68.6 1.2 %collective-permute-done.18.rest_4_ = bf16[32,1664]{1,0:T(8,128)(2,1)S(1)} collective-permute-done((bf16[32,1664]{1,0:T(8,128)(2,1)S(1)}, bf16[32,1664]{1,0:T(8,128)(2,1)S(1)}, u32[]{:S(2)}, u32[]{:S(2)}) %collective-permute-start.18) | collective-permute-done | bytes 106528 | tf_op jit(solution)/shard_map/ppermute | solution.py:422
  70.6 1.2 %collective-permute-start.22 = (bf16[32,1664]{1,0:T(8,128)(2,1)S(1)}, bf16[32,1664]{1,0:T(8,128)(2,1)S(1)}, u32[]{:S(2)}, u32[]{:S(2)}) collective-permute-start(bf16[32,1664]{1,0:T(8,128)(2,1)S(1)} %collective-permute-done.19.rest_7_.rest_1_), channel_id=1, source_target_pairs={{0,4},{1,5},{4,8},{5,9},{8,12},{9,13},{12,14},{13,15},{14,10},{15,... | collective-permute-start | bytes 319496 | tf_op jit(solution)/shard_map/ppermute | solution.py:422
  71.9 1.3 %down_blocks.7.total_ref = f32[64,1024]{1,0:T(8,128)S(1)} custom-call(f32[64,1024]{1,0:T(8,128)S(1)} %down_blocks.6.rest_0_, bf16[32,1664]{1,0:T(8,128)(2,1)S(1)} %collective-permute-done.19.rest_7_.rest_1_, bf16[32,1664]{1,0:T(8,128)(2,1)S(1)} %collective-permute-done.17.rest_2_, bf16[32,1664]{1,0:T(8,128)(2,1)S(1)} %collective-permute-done.20.rest_8_.rest_3_, ...), custom_call_target="tpu_custom_call" | custom-call | flops 436207616 | bytes 6815744 | tf_op jit(solution)/shard_map/down_blocks/pallas_call | solution.py:365
  73.2 1.3 %collective-permute-done.21.lower_ref = bf16[32,1664]{1,0:T(8,128)(2,1)S(1)} collective-permute-done((bf16[32,1664]{1,0:T(8,128)(2,1)S(1)}, bf16[32,1664]{1,0:T(8,128)(2,1)S(1)}, u32[]{:S(2)}, u32[]{:S(2)}) %collective-permute-start.21) | collective-permute-done | bytes 106528 | tf_op jit(solution)/shard_map/ppermute | solution.py:422
  76.2 1.2 %collective-permute-done.23 = bf16[64,512]{1,0:T(8,128)(2,1)S(1)} collective-permute-done((bf16[64,512]{1,0:T(8,128)(2,1)S(1)}, bf16[64,512]{1,0:T(8,128)(2,1)S(1)}, u32[]{:S(2)}, u32[]{:S(2)}) %collective-permute-start.23) | collective-permute-done | bytes 65568 | tf_op jit(solution)/shard_map/ppermute | solution.py:22
  (61 shorter events, 17.6 us)
Async XLA Ops:
  3.4 1.5 %collective-permute-start = (bf16[64,640]{1,0:T(8,128)(2,1)S(1)}, bf16[64,640]{1,0:T(8,128)(2,1)S(1)}, u32[]{:S(2)}, u32[]{:S(2)}) collective-permute-start(bf16[64,640]{1,0:T(8,128)(2,1)S(1)} %get-tuple-element.41.own_ref), channel_id=1, source_target_pairs={{0,1},{1,0},{2,3},{3,2},{4,5},{5,4},{6,7},{7,6},{8,9},{9,8},{10,11... | collective-permute-start | bytes 245768 | tf_op jit(solution)/shard_map/ppermute | solution.py:22
  8.0 7.6 %collective-permute-start.2 = (bf16[64,1664]{1,0:T(8,128)(2,1)S(1)}, bf16[64,1664]{1,0:T(8,128)(2,1)S(1)}, u32[]{:S(2)}, u32[]{:S(2)}) collective-permute-start(bf16[64,1664]{1,0:T(8,128)(2,1)S(1)} %get-tuple-element.45.rest_1_), channel_id=1, source_target_pairs={{0,2},{1,3},{4,0},{5,1},{8,4},{9,5},{12,8},{13,9},{14,12},{15,13},... | collective-permute-start | bytes 638984 | tf_op jit(solution)/shard_map/ppermute | solution.py:422
  10.9 6.7 %collective-permute-start.1 = (bf16[64,1792]{1,0:T(8,128)(2,1)S(1)}, bf16[64,1792]{1,0:T(8,128)(2,1)S(1)}, u32[]{:S(2)}, u32[]{:S(2)}) collective-permute-start(bf16[64,1792]{1,0:T(8,128)(2,1)S(1)} %get-tuple-element.44.rest_0_), channel_id=1, source_target_pairs={{0,4},{1,5},{4,8},{5,9},{8,12},{9,13},{12,14},{13,15},{14,10},{15,... | collective-permute-start | bytes 688136 | tf_op jit(solution)/shard_map/ppermute | solution.py:422
  15.7 11.3 %collective-permute-start.4 = (bf16[64,3456]{1,0:T(8,128)(2,1)S(1)}, bf16[64,3456]{1,0:T(8,128)(2,1)S(1)}, u32[]{:S(2)}, u32[]{:S(2)}) collective-permute-start(bf16[64,3456]{1,0:T(8,128)(2,1)S(1)} %pad_maximum_fusion.1.rest_1_), channel_id=1, source_target_pairs={{0,2},{1,3},{4,0},{5,1},{8,4},{9,5},{12,8},{13,9},{14,12},{15,13},... | collective-permute-start | bytes 1327112 | tf_op jit(solution)/shard_map/ppermute | solution.py:422
  17.7 10.9 %collective-permute-start.3 = (bf16[64,3456]{1,0:T(8,128)(2,1)S(1)}, bf16[64,3456]{1,0:T(8,128)(2,1)S(1)}, u32[]{:S(2)}, u32[]{:S(2)}) collective-permute-start(bf16[64,3456]{1,0:T(8,128)(2,1)S(1)} %pad_maximum_fusion.rest_0_), channel_id=1, source_target_pairs={{0,4},{1,5},{4,8},{5,9},{8,12},{9,13},{12,14},{13,15},{14,10},{15,... | collective-permute-start | bytes 1327112 | tf_op jit(solution)/shard_map/ppermute | solution.py:422
  27.1 10.3 %collective-permute-start.6 = (bf16[64,3456]{1,0:T(8,128)(2,1)S(1)}, bf16[64,3456]{1,0:T(8,128)(2,1)S(1)}, u32[]{:S(2)}, u32[]{:S(2)}) collective-permute-start(bf16[64,3456]{1,0:T(8,128)(2,1)S(1)} %add_convert_fusion.2.rest_1_), channel_id=1, source_target_pairs={{0,2},{1,3},{4,0},{5,1},{8,4},{9,5},{12,8},{13,9},{14,12},{15,13},... | collective-permute-start | bytes 1327112 | tf_op jit(solution)/shard_map/ppermute | solution.py:422
  28.7 10.3 %collective-permute-start.5 = (bf16[64,3456]{1,0:T(8,128)(2,1)S(1)}, bf16[64,3456]{1,0:T(8,128)(2,1)S(1)}, u32[]{:S(2)}, u32[]{:S(2)}) collective-permute-start(bf16[64,3456]{1,0:T(8,128)(2,1)S(1)} %add_convert_fusion.3.rest_0_), channel_id=1, source_target_pairs={{0,4},{1,5},{4,8},{5,9},{8,12},{9,13},{12,14},{13,15},{14,10},{15,... | collective-permute-start | bytes 1327112 | tf_op jit(solution)/shard_map/ppermute | solution.py:422
  37.4 9.3 %collective-permute-start.8 = (bf16[64,3456]{1,0:T(8,128)(2,1)S(1)}, bf16[64,3456]{1,0:T(8,128)(2,1)S(1)}, u32[]{:S(2)}, u32[]{:S(2)}) collective-permute-start(bf16[64,3456]{1,0:T(8,128)(2,1)S(1)} %add_convert_fusion.rest_1_), channel_id=1, source_target_pairs={{0,2},{1,3},{4,0},{5,1},{8,4},{9,5},{12,8},{13,9},{14,12},{15,13},... | collective-permute-start | bytes 1327112 | tf_op jit(solution)/shard_map/ppermute | solution.py:422
  39.0 9.8 %collective-permute-start.7 = (bf16[64,3456]{1,0:T(8,128)(2,1)S(1)}, bf16[64,3456]{1,0:T(8,128)(2,1)S(1)}, u32[]{:S(2)}, u32[]{:S(2)}) collective-permute-start(bf16[64,3456]{1,0:T(8,128)(2,1)S(1)} %add_convert_fusion.1.rest_0_), channel_id=1, source_target_pairs={{0,4},{1,5},{4,8},{5,9},{8,12},{9,13},{12,14},{13,15},{14,10},{15,... | collective-permute-start | bytes 1327112 | tf_op jit(solution)/shard_map/ppermute | solution.py:422
  49.3 5.1 %collective-permute-start.11 = (bf16[32,1664]{1,0:T(8,128)(2,1)S(1)}, bf16[32,1664]{1,0:T(8,128)(2,1)S(1)}, u32[]{:S(2)}, u32[]{:S(2)}) collective-permute-start(bf16[32,1664]{1,0:T(8,128)(2,1)S(1)} %get-tuple-element.75.rest_0_), channel_id=1, source_target_pairs={{0,4},{1,5},{4,8},{5,9},{8,12},{9,13},{12,14},{13,15},{14,10},{15,... | collective-permute-start | bytes 319496 | tf_op jit(solution)/shard_map/ppermute | solution.py:422
  49.9 5.2 %collective-permute-start.12 = (bf16[32,1664]{1,0:T(8,128)(2,1)S(1)}, bf16[32,1664]{1,0:T(8,128)(2,1)S(1)}, u32[]{:S(2)}, u32[]{:S(2)}) collective-permute-start(bf16[32,1664]{1,0:T(8,128)(2,1)S(1)} %get-tuple-element.75.rest_0_), channel_id=1, source_target_pairs={{0,2},{1,3},{4,0},{5,1},{8,4},{9,5},{12,8},{13,9},{14,12},{15,13},... | collective-permute-start | bytes 319496 | tf_op jit(solution)/shard_map/ppermute | solution.py:422
  51.4 6.1 %collective-permute-start.10 = (bf16[32,1664]{1,0:T(8,128)(2,1)S(1)}, bf16[32,1664]{1,0:T(8,128)(2,1)S(1)}, u32[]{:S(2)}, u32[]{:S(2)}) collective-permute-start(bf16[32,1664]{1,0:T(8,128)(2,1)S(1)} %get-tuple-element.76.rest_1_), channel_id=1, source_target_pairs={{0,2},{1,3},{4,0},{5,1},{8,4},{9,5},{12,8},{13,9},{14,12},{15,13},... | collective-permute-start | bytes 319496 | tf_op jit(solution)/shard_map/ppermute | solution.py:422
  53.0 4.7 %collective-permute-start.9 = (bf16[32,1664]{1,0:T(8,128)(2,1)S(1)}, bf16[32,1664]{1,0:T(8,128)(2,1)S(1)}, u32[]{:S(2)}, u32[]{:S(2)}) collective-permute-start(bf16[32,1664]{1,0:T(8,128)(2,1)S(1)} %get-tuple-element.76.rest_1_), channel_id=1, source_target_pairs={{0,4},{1,5},{4,8},{5,9},{8,12},{9,13},{12,14},{13,15},{14,10},{15,... | collective-permute-start | bytes 319496 | tf_op jit(solution)/shard_map/ppermute | solution.py:422
  54.4 5.3 %collective-permute-start.15 = (bf16[32,1664]{1,0:T(8,128)(2,1)S(1)}, bf16[32,1664]{1,0:T(8,128)(2,1)S(1)}, u32[]{:S(2)}, u32[]{:S(2)}) collective-permute-start(bf16[32,1664]{1,0:T(8,128)(2,1)S(1)} %collective-permute-done.11.rest_3_.rest_1_), channel_id=1, source_target_pairs={{0,4},{1,5},{4,8},{5,9},{8,12},{9,13},{12,14},{13,15},{14,10},{15,... | collective-permute-start | bytes 319496 | tf_op jit(solution)/shard_map/ppermute | solution.py:422
  55.2 6.1 %collective-permute-start.16 = (bf16[32,1664]{1,0:T(8,128)(2,1)S(1)}, bf16[32,1664]{1,0:T(8,128)(2,1)S(1)}, u32[]{:S(2)}, u32[]{:S(2)}) collective-permute-start(bf16[32,1664]{1,0:T(8,128)(2,1)S(1)} %collective-permute-done.12.rest_4_.rest_3_), channel_id=1, source_target_pairs={{0,2},{1,3},{4,0},{5,1},{8,4},{9,5},{12,8},{13,9},{14,12},{15,13},... | collective-permute-start | bytes 319496 | tf_op jit(solution)/shard_map/ppermute | solution.py:422
  57.7 5.8 %collective-permute-start.13 = (bf16[32,1664]{1,0:T(8,128)(2,1)S(1)}, bf16[32,1664]{1,0:T(8,128)(2,1)S(1)}, u32[]{:S(2)}, u32[]{:S(2)}) collective-permute-start(bf16[32,1664]{1,0:T(8,128)(2,1)S(1)} %collective-permute-done.9.rest_2_), channel_id=1, source_target_pairs={{0,4},{1,5},{4,8},{5,9},{8,12},{9,13},{12,14},{13,15},{14,10},{15,... | collective-permute-start | bytes 319496 | tf_op jit(solution)/shard_map/ppermute | solution.py:422
  59.2 4.7 %collective-permute-start.14 = (bf16[32,1664]{1,0:T(8,128)(2,1)S(1)}, bf16[32,1664]{1,0:T(8,128)(2,1)S(1)}, u32[]{:S(2)}, u32[]{:S(2)}) collective-permute-start(bf16[32,1664]{1,0:T(8,128)(2,1)S(1)} %collective-permute-done.10.rest_4_), channel_id=1, source_target_pairs={{0,2},{1,3},{4,0},{5,1},{8,4},{9,5},{12,8},{13,9},{14,12},{15,13},... | collective-permute-start | bytes 319496 | tf_op jit(solution)/shard_map/ppermute | solution.py:422
  59.7 6.2 %collective-permute-start.19 = (bf16[32,1664]{1,0:T(8,128)(2,1)S(1)}, bf16[32,1664]{1,0:T(8,128)(2,1)S(1)}, u32[]{:S(2)}, u32[]{:S(2)}) collective-permute-start(bf16[32,1664]{1,0:T(8,128)(2,1)S(1)} %collective-permute-done.15.rest_7_.rest_1_), channel_id=1, source_target_pairs={{0,4},{1,5},{4,8},{5,9},{8,12},{9,13},{12,14},{13,15},{14,10},{15,... | collective-permute-start | bytes 319496 | tf_op jit(solution)/shard_map/ppermute | solution.py:422
  61.2 5.2 %collective-permute-start.20 = (bf16[32,1664]{1,0:T(8,128)(2,1)S(1)}, bf16[32,1664]{1,0:T(8,128)(2,1)S(1)}, u32[]{:S(2)}, u32[]{:S(2)}) collective-permute-start(bf16[32,1664]{1,0:T(8,128)(2,1)S(1)} %collective-permute-done.16.rest_8_.rest_3_), channel_id=1, source_target_pairs={{0,2},{1,3},{4,0},{5,1},{8,4},{9,5},{12,8},{13,9},{14,12},{15,13},... | collective-permute-start | bytes 319496 | tf_op jit(solution)/shard_map/ppermute | solution.py:422
  63.9 4.7 %collective-permute-start.17 = (bf16[32,1664]{1,0:T(8,128)(2,1)S(1)}, bf16[32,1664]{1,0:T(8,128)(2,1)S(1)}, u32[]{:S(2)}, u32[]{:S(2)}) collective-permute-start(bf16[32,1664]{1,0:T(8,128)(2,1)S(1)} %collective-permute-done.13.rest_2_), channel_id=1, source_target_pairs={{0,4},{1,5},{4,8},{5,9},{8,12},{9,13},{12,14},{13,15},{14,10},{15,... | collective-permute-start | bytes 319496 | tf_op jit(solution)/shard_map/ppermute | solution.py:422
  65.1 4.7 %collective-permute-start.18 = (bf16[32,1664]{1,0:T(8,128)(2,1)S(1)}, bf16[32,1664]{1,0:T(8,128)(2,1)S(1)}, u32[]{:S(2)}, u32[]{:S(2)}) collective-permute-start(bf16[32,1664]{1,0:T(8,128)(2,1)S(1)} %collective-permute-done.14.rest_4_), channel_id=1, source_target_pairs={{0,2},{1,3},{4,0},{5,1},{8,4},{9,5},{12,8},{13,9},{14,12},{15,13},... | collective-permute-start | bytes 319496 | tf_op jit(solution)/shard_map/ppermute | solution.py:422
  69.8 4.7 %collective-permute-start.21 = (bf16[32,1664]{1,0:T(8,128)(2,1)S(1)}, bf16[32,1664]{1,0:T(8,128)(2,1)S(1)}, u32[]{:S(2)}, u32[]{:S(2)}) collective-permute-start(bf16[32,1664]{1,0:T(8,128)(2,1)S(1)} %collective-permute-done.18.rest_4_), channel_id=1, source_target_pairs={{0,2},{1,3},{4,0},{5,1},{8,4},{9,5},{12,8},{13,9},{14,12},{15,13},... | collective-permute-start | bytes 319496 | tf_op jit(solution)/shard_map/ppermute | solution.py:422
  70.6 4.7 %collective-permute-start.22 = (bf16[32,1664]{1,0:T(8,128)(2,1)S(1)}, bf16[32,1664]{1,0:T(8,128)(2,1)S(1)}, u32[]{:S(2)}, u32[]{:S(2)}) collective-permute-start(bf16[32,1664]{1,0:T(8,128)(2,1)S(1)} %collective-permute-done.19.rest_7_.rest_1_), channel_id=1, source_target_pairs={{0,4},{1,5},{4,8},{5,9},{8,12},{9,13},{12,14},{13,15},{14,10},{15,... | collective-permute-start | bytes 319496 | tf_op jit(solution)/shard_map/ppermute | solution.py:422
  76.1 1.3 %collective-permute-start.23 = (bf16[64,512]{1,0:T(8,128)(2,1)S(1)}, bf16[64,512]{1,0:T(8,128)(2,1)S(1)}, u32[]{:S(2)}, u32[]{:S(2)}) collective-permute-start(bf16[64,512]{1,0:T(8,128)(2,1)S(1)} %get-tuple-element.74), channel_id=1, source_target_pairs={{0,1},{1,0},{2,3},{3,2},{4,5},{5,4},{6,7},{7,6},{8,9},{9,8},{10,11... | collective-permute-start | bytes 196616 | tf_op jit(solution)/shard_map/ppermute | solution.py:22
  (4 other events, 12.5 us)

commit v6 on v5

--- a/solution.py
+++ b/solution.py
@@ -155,7 +155,7 @@
     )(token_ids, stream, table_rows, gain, after)
 
 
-def start_up_copies(block, gate_ref, up_ref, tiles, arrived, gate_here=None):
+def start_up_copies(block, gate_ref, up_ref, tiles, arrived, skipped=None, skip=None):
     cuts = arrived.shape[1]
     cut = gate_ref.shape[0] // cuts
     width = gate_ref.shape[1] // D_WAYS
@@ -167,8 +167,8 @@
             copy = pltpu.make_async_copy(
                 ref.at[pl.ds(c * cut, cut), columns], tiles.at[m, pl.ds(c * cut, cut), :], arrived.at[m, c]
             )
-            if m == 0 and gate_here is not None:
-                pl.when(jnp.logical_not(gate_here))(copy.start)
+            if m == skipped:
+                pl.when(jnp.logical_not(skip))(copy.start)
             else:
                 copy.start()
             copies.append((m, features, copy))
@@ -283,7 +283,8 @@
                 up_ref,
                 tiles.at[j],
                 arrived.at[j],
-                here if j == 0 and aheads else None,
+                0 if j == 0 and aheads else None,
+                here,
             )
             for j, distance in enumerate(distances)
         ]
@@ -313,6 +314,86 @@
         cost_estimate=up_cost(count, rows, depth, width),
         name="up_blocks",
     )(x, squares, gate_tile, up_tile, *after, *downs, *aheads)
+
+
+def own_block(x, gate_tile, up_tile, after, down_tile, fetch):
+    depth, units = gate_tile.shape
+    width = units // D_WAYS
+    rows = x.shape[0]
+
+    def kernel(x_ref, gate_ref, up_ref, *rest):
+        down_ref, tiles, gate_out, up_out, *fetched, arrived, fetch_arrived = rest[len(after) :]
+        _, side, place = position()
+        copies = start_up_copies(at(place, 0), gate_ref, up_ref, tiles, arrived)
+        ahead = start_down_copies(place, fetch, [down_ref], fetched, fetch_arrived)
+
+        @pl.when(side == 0)
+        def _():
+            up_products(x_ref, copies, tiles, [gate_out, up_out])
+
+        @pl.when(side == 1)
+        def _():
+            for _, _, copy in copies:
+                copy.wait()
+
+        for copy in ahead:
+            copy.wait()
+
+    return pl.pallas_call(
+        kernel,
+        out_shape=[jax.ShapeDtypeStruct((2, depth, width), BF16)]
+        + [jax.ShapeDtypeStruct((rows, width), F32)] * 2
+        + [jax.ShapeDtypeStruct(down_tile_shape(down_tile), BF16) for _ in fetch],
+        in_specs=[IN_VMEM] + [IN_HBM] * 2 + [IN_PLACE] * len(after) + [IN_HBM],
+        out_specs=[IN_VMEM] * (3 + len(fetch)),
+        scratch_shapes=[
+            pltpu.SemaphoreType.DMA((2, 2)),
+            pltpu.SemaphoreType.DMA((len(fetch),)),
+        ],
+        compiler_params=params(8),
+        cost_estimate=up_cost(1, rows, depth, width),
+        name="own_block",
+    )(x, gate_tile, up_tile, *after, down_tile)
+
+
+def own_hidden(x, squares, tiles, gate_product, up_product, right, left):
+    rows, width = gate_product.shape
+
+    def kernel(x_ref, squares_ref, tiles_ref, gate_ref, up_ref, right_ref, left_ref, upper_ref, lower_ref, gates, ups):
+        _, side, _ = position()
+
+        @pl.when(side == 0)
+        def _():
+            gates[...] = gate_ref[...]
+            ups[...] = up_ref[...]
+
+        @pl.when(side == 1)
+        def _():
+            gates[...] = jnp.dot(x_ref[...], tiles_ref[0], preferred_element_type=F32)
+            ups[...] = jnp.dot(x_ref[...], tiles_ref[1], preferred_element_type=F32)
+
+        def total(own, start, size):
+            place = slice(start, start + size)
+            return own + right_ref[:, place].astype(F32) + left_ref[:, place].astype(F32)
+
+        lanes = total(squares_ref[...], 0, LANES)
+        scale = lax.rsqrt(jnp.sum(lanes, axis=1, keepdims=True) / D + 1e-05)
+        gate = total(gates[...], LANES, width) * scale
+        up = total(ups[...], LANES + width, width) * scale
+        hidden = (gate / (1.0 + jnp.exp(-gate)) * up).astype(BF16)
+        upper_ref[...] = hidden[: rows // 2]
+        lower_ref[...] = hidden[rows // 2 :]
+
+    return pl.pallas_call(
+        kernel,
+        out_shape=[jax.ShapeDtypeStruct((rows // 2, width), BF16)] * 2,
+        in_specs=[IN_VMEM] * 7,
+        out_specs=[IN_VMEM] * 2,
+        scratch_shapes=[pltpu.VMEM((rows, width), F32)] * 2,
+        compiler_params=params(8),
+        cost_estimate=up_cost(1, rows, x.shape[1], width),
+        name="own_hidden",
+    )(x, squares, tiles, gate_product, up_product, right, left)
 
 
 def down_tile_shape(down_tile):
@@ -428,29 +509,25 @@
     right, left, scaled, squares, ahead_tile = first_up_block(own, other, far_tiles, gate_tile)
     split = LANES + width
     down_tiles = []
-    for distance, fetch in ((3, ()), (2, (0, -1)), (1, (1, -2)), (0, (2, -3, 3, 4))):
-        distances = [distance, -distance] if distance else [0]
+    for distance, fetch in ((3, ()), (2, (0, -1)), (1, (1, -2))):
         ahead = ahead_tile if distance == 3 else None
+        distances = [distance, -distance]
         found = up_blocks(scaled, squares, gate_tile, up_tile, distances, [right, left], down_tile, fetch, ahead)
-        own = found[: len(distances)]
-        down_tiles += found[len(distances) :]
+        own = found[:2]
+        down_tiles += found[2:]
         right, left = shift(right, 1), shift(left, -1)
         if distance == 3:
             right = jnp.concatenate([own[0][:, :split] + right.astype(F32), own[0][:, split:]], 1)
             left = jnp.concatenate([own[1][:, :split], own[1][:, split:] + left.astype(F32)], 1)
             right, left = right.astype(BF16), left.astype(BF16)
-        elif distance:
+        else:
             right = (own[0] + right.astype(F32)).astype(BF16)
             left = (own[1] + left.astype(F32)).astype(BF16)
-        else:
-            both = own[0] + right.astype(F32) + left.astype(F32)
-
-    both, total_squares = both[:, LANES:], jnp.sum(both[:, :LANES], axis=1, keepdims=True)
-    both = both * lax.rsqrt(total_squares / D + 1e-05)
-    mine = (jax.nn.silu(both[:, :width]) * both[:, width:]).astype(BF16)
-
-    half = rows // 2
-    upper, lower = mine[:half], mine[half:]
+    own_tiles, gates, ups, *found = own_block(scaled, gate_tile, up_tile, [right, left], down_tile, (2, -3, 3, 4))
+    down_tiles += found
+    right, left = shift(right, 1), shift(left, -1)
+    upper, lower = own_hidden(scaled, squares, own_tiles, gates, ups, right, left)
+
     total = None
     hidden = [(upper, lower)]
     upper_right, upper_left, lower_right, lower_left = upper, upper, lower, lower

time: 78.2 us -> 77 us (0.985)
    pallas_call x0 -> x2, Pallas kernels: none -> 7.39 us  [the longest x1 6.98 us: own_block(): pl.pallas_call(kernel, out_shape=[jax.ShapeDtypeStruct((2, depth, width),...]
    pallas_call x4 -> x3, Pallas kernels: 25.5 us -> 18.5 us  [up_blocks(): pl.pallas_call(kernel, out_shape=[jax.ShapeDtypeStruct((rows, LANES + 2 *...]
  transfers between devices with their start and end apart: 24 -> 24, of which waited for: 15 -> 13; matrix products, arithmetic and copies ran while one was open for 1% -> 1% of each run, Pallas kernels for 39% -> 39%
where the time goes in v6:
time: 77 us; the launch traced here: 76.9 us
  Pallas kernels  37.8 us (49%)
  starting transfers between devices  24.5 us (32%)
  waiting for transfers between devices  13.1 us (17%)
  other arithmetic  1.1 us (1%)
    ppermute x22, starting transfers between devices, shift(): return lax.ppermute(value, 'tp', pairs)  23.9 us
    pallas_call x3, Pallas kernels, up_blocks(): pl.pallas_call(kernel, out_shape=[jax.ShapeDtypeStruct((rows, LANES + 2 *...  18.5 us
    ppermute x22, waiting for transfers between devices, shift(): return lax.ppermute(value, 'tp', pairs)  11 us
    pallas_call x1, Pallas kernels, own_block(): pl.pallas_call(kernel, out_shape=[jax.ShapeDtypeStruct((2, depth, width),...  6.98 us
    pallas_call x4, Pallas kernels, down_blocks(): pl.pallas_call(kernel, out_shape=[jax.ShapeDtypeStruct((rows, width), F32...  4.7 us
    pallas_call x1, Pallas kernels, first_up_block(): pl.pallas_call(kernel, out_shape=[jax.ShapeDtypeStruct((rows, LANES + wid...  3.13 us
    pallas_call x1, Pallas kernels, fetch_up_block(): pl.pallas_call(kernel, out_shape=jax.ShapeDtypeStruct((2, depth, width),...  3.08 us
    ppermute x2, waiting for transfers between devices, from_partner(): return lax.ppermute(value, axis, pairs)  2.16 us
  transfers between devices with their start and end apart: 24, of which 13 were waited for; matrix products, arithmetic and copies ran while one was open for 1% of the time, Pallas kernels for 39%

profile of v6, /device:TPU:0, one launch (start us, length us, event | category | flops | bytes accessed | tf_op | source)
XLA Modules:
  0.0 76.9 jit_solution(15129466028989075304)
XLA Ops:
  0.0 3.1 %fetch_up_block.1.after_ref.tiles_ref = bf16[2,1024,1664]{2,1,0:T(8,128)(2,1)S(1)} custom-call(bf16[1024,13312]{1,0:T(8,128)(2,1)} %bitcast.7, bf16[1024,13312]{1,0:T(8,128)(2,1)} %bitcast.13), custom_call_target="tpu_custom_call" | custom-call | tf_op jit(solution)/shard_map/fetch_up_block/pallas_call | solution.py:112
  4.9 3.1 %first_up_block.1 = (bf16[64,1792]{1,0:T(8,128)(2,1)S(1)}, bf16[64,1664]{1,0:T(8,128)(2,1)S(1)}, bf16[64,1024]{1,0:T(8,128)(2,1)S(1)}, f32[64,128]{1,0:T(8,128)S(1)}, bf16[1024,1664]{1,0:T(8,128)(2,1)S(1)}) custom-call(bf16[64,640]{1,0:T(8,128)(2,1)S(1)} %get-tuple-element.45.own_ref, bf16[64,640]{1,0:T(8,128)(2,1)S(1)} %collective-permute-done.other_ref, ...), custom_call_target="tpu_custom_call" | custom-call | flops 436207616 | bytes 6815744 | tf_op jit(solution)/shard_map/first_up_block/pallas_call | solution.py:245
  8.0 2.9 %collective-permute-start.2 = (bf16[64,1664]{1,0:T(8,128)(2,1)S(1)}, bf16[64,1664]{1,0:T(8,128)(2,1)S(1)}, u32[]{:S(2)}, u32[]{:S(2)}) collective-permute-start(bf16[64,1664]{1,0:T(8,128)(2,1)S(1)} %get-tuple-element.49.rest_1_), channel_id=1, source_target_pairs={{0,2},{1,3},{4,0},{5,1},{8,4},{9,5},{12,8},{13,9},{14,12},{15,13},... | collective-permute-start | bytes 638984 | tf_op jit(solution)/shard_map/ppermute | solution.py:503
  11.1 4.5 %up_blocks.3 = (f32[64,3456]{1,0:T(8,128)S(1)}, f32[64,3456]{1,0:T(8,128)S(1)}) custom-call(bf16[64,1024]{1,0:T(8,128)(2,1)S(1)} %get-tuple-element.46.x_ref, f32[64,128]{1,0:T(8,128)S(1)} %get-tuple-element.47.squares_ref, bf16[1024,13312]{1,0:T(8,128)(2,1)} %bitcast.9, bf16[1024,13312]{1,0:T(8,128)(2,1)} %bitcast.14, ...), custom_call_target="tpu_custom_call" | custom-call | flops 872415232 | bytes 13631488 | tf_op jit(solution)/shard_map/up_blocks/pallas_call | solution.py:302
  15.7 1.9 %collective-permute-start.4 = (bf16[64,3456]{1,0:T(8,128)(2,1)S(1)}, bf16[64,3456]{1,0:T(8,128)(2,1)S(1)}, u32[]{:S(2)}, u32[]{:S(2)}) collective-permute-start(bf16[64,3456]{1,0:T(8,128)(2,1)S(1)} %pad_maximum_fusion.1.rest_1_), channel_id=1, source_target_pairs={{0,2},{1,3},{4,0},{5,1},{8,4},{9,5},{12,8},{13,9},{14,12},{15,13},... | collective-permute-start | bytes 1327112 | tf_op jit(solution)/shard_map/ppermute | solution.py:503
  18.1 7.0 %up_blocks.4 = (f32[64,3456]{1,0:T(8,128)S(1)}, f32[64,3456]{1,0:T(8,128)S(1)}, bf16[1664,1024]{1,0:T(8,128)(2,1)S(1)}, bf16[1664,1024]{1,0:T(8,128)(2,1)S(1)}) custom-call(bf16[64,1024]{1,0:T(8,128)(2,1)S(1)} %get-tuple-element.46.x_ref, f32[64,128]{1,0:T(8,128)S(1)} %get-tuple-element.47.squares_ref, bf16[1024,13312]{1,0:T(8,128)(2,1)} %bitcast.10, ...), custom_call_target="tpu_custom_call" | custom-call | flops 872415232 | bytes 13631488 | tf_op jit(solution)/shard_map/up_blocks/pallas_call | solution.py:302
  25.1 1.8 %collective-permute-done.4 = bf16[64,3456]{1,0:T(8,128)(2,1)S(1)} collective-permute-done((bf16[64,3456]{1,0:T(8,128)(2,1)S(1)}, bf16[64,3456]{1,0:T(8,128)(2,1)S(1)}, u32[]{:S(2)}, u32[]{:S(2)}) %collective-permute-start.4) | collective-permute-done | bytes 442400 | tf_op jit(solution)/shard_map/ppermute | solution.py:503
  27.1 1.5 %collective-permute-start.6 = (bf16[64,3456]{1,0:T(8,128)(2,1)S(1)}, bf16[64,3456]{1,0:T(8,128)(2,1)S(1)}, u32[]{:S(2)}, u32[]{:S(2)}) collective-permute-start(bf16[64,3456]{1,0:T(8,128)(2,1)S(1)} %add_convert_fusion.2.rest_1_), channel_id=1, source_target_pairs={{0,2},{1,3},{4,0},{5,1},{8,4},{9,5},{12,8},{13,9},{14,12},{15,13},... | collective-permute-start | bytes 1327112 | tf_op jit(solution)/shard_map/ppermute | solution.py:503
  29.3 7.0 %up_blocks.5 = (f32[64,3456]{1,0:T(8,128)S(1)}, f32[64,3456]{1,0:T(8,128)S(1)}, bf16[1664,1024]{1,0:T(8,128)(2,1)S(1)}, bf16[1664,1024]{1,0:T(8,128)(2,1)S(1)}) custom-call(bf16[64,1024]{1,0:T(8,128)(2,1)S(1)} %get-tuple-element.46.x_ref, f32[64,128]{1,0:T(8,128)S(1)} %get-tuple-element.47.squares_ref, bf16[1024,13312]{1,0:T(8,128)(2,1)} %bitcast.11, ...), custom_call_target="tpu_custom_call" | custom-call | flops 872415232 | bytes 13631488 | tf_op jit(solution)/shard_map/up_blocks/pallas_call | solution.py:302
  37.4 1.5 %collective-permute-start.8 = (bf16[64,3456]{1,0:T(8,128)(2,1)S(1)}, bf16[64,3456]{1,0:T(8,128)(2,1)S(1)}, u32[]{:S(2)}, u32[]{:S(2)}) collective-permute-start(bf16[64,3456]{1,0:T(8,128)(2,1)S(1)} %add_convert_fusion.rest_1_), channel_id=1, source_target_pairs={{0,2},{1,3},{4,0},{5,1},{8,4},{9,5},{12,8},{13,9},{14,12},{15,13},... | collective-permute-start | bytes 1327112 | tf_op jit(solution)/shard_map/ppermute | solution.py:503
  39.6 7.0 %own_block.1 = (bf16[2,1024,1664]{2,1,0:T(8,128)(2,1)S(1)}, f32[64,1664]{1,0:T(8,128)S(1)}, f32[64,1664]{1,0:T(8,128)S(1)}, bf16[1664,1024]{1,0:T(8,128)(2,1)S(1...) custom-call(bf16[64,1024]{1,0:T(8,128)(2,1)S(1)} %get-tuple-element.46.x_ref, ...), custom_call_target="tpu_custom_call" | custom-call | flops 436207616 | bytes 6815744 | tf_op jit(solution)/shard_map/own_block/pallas_call | solution.py:342
  50.3 1.6 %collective-permute-start.10 = (bf16[32,1664]{1,0:T(8,128)(2,1)S(1)}, bf16[32,1664]{1,0:T(8,128)(2,1)S(1)}, u32[]{:S(2)}, u32[]{:S(2)}) collective-permute-start(bf16[32,1664]{1,0:T(8,128)(2,1)S(1)} %get-tuple-element.60.rest_1_), channel_id=1, source_target_pairs={{0,2},{1,3},{4,0},{5,1},{8,4},{9,5},{12,8},{13,9},{14,12},{15,13},... | collective-permute-start | bytes 319496 | tf_op jit(solution)/shard_map/ppermute | solution.py:503
  52.3 1.7 %collective-permute-done.11.rest_3_.rest_1_ = bf16[32,1664]{1,0:T(8,128)(2,1)S(1)} collective-permute-done((bf16[32,1664]{1,0:T(8,128)(2,1)S(1)}, bf16[32,1664]{1,0:T(8,128)(2,1)S(1)}, u32[]{:S(2)}, u32[]{:S(2)}) %collective-permute-start.11) | collective-permute-done | bytes 106528 | tf_op jit(solution)/shard_map/ppermute | solution.py:503
  54.7 1.3 %collective-permute-start.16 = (bf16[32,1664]{1,0:T(8,128)(2,1)S(1)}, bf16[32,1664]{1,0:T(8,128)(2,1)S(1)}, u32[]{:S(2)}, u32[]{:S(2)}) collective-permute-start(bf16[32,1664]{1,0:T(8,128)(2,1)S(1)} %collective-permute-done.12.rest_4_.rest_3_), channel_id=1, source_target_pairs={{0,2},{1,3},{4,0},{5,1},{8,4},{9,5},{12,8},{13,9},{14,12},{15,13},... | collective-permute-start | bytes 319496 | tf_op jit(solution)/shard_map/ppermute | solution.py:503
  59.7 1.3 %collective-permute-start.20 = (bf16[32,1664]{1,0:T(8,128)(2,1)S(1)}, bf16[32,1664]{1,0:T(8,128)(2,1)S(1)}, u32[]{:S(2)}, u32[]{:S(2)}) collective-permute-start(bf16[32,1664]{1,0:T(8,128)(2,1)S(1)} %collective-permute-done.16.rest_8_.rest_3_), channel_id=1, source_target_pairs={{0,2},{1,3},{4,0},{5,1},{8,4},{9,5},{12,8},{13,9},{14,12},{15,13},... | collective-permute-start | bytes 319496 | tf_op jit(solution)/shard_map/ppermute | solution.py:503
  61.0 1.3 %down_blocks.5.rest_0_ = f32[64,1024]{1,0:T(8,128)S(1)} custom-call(f32[64,1024]{1,0:T(8,128)S(1)} %down_blocks.4.rest_0_, bf16[32,1664]{1,0:T(8,128)(2,1)S(1)} %collective-permute-done.11.rest_3_.rest_1_, bf16[32,1664]{1,0:T(8,128)(2,1)S(1)} %collective-permute-done.9.rest_2_, bf16[32,1664]{1,0:T(8,128)(2,1)S(1)} %collective-permute-done.12.rest_4_.rest_3_, ...), custom_call_target="tpu_custom_call" | custom-call | flops 436207616 | bytes 6815744 | tf_op jit(solution)/shard_map/down_blocks/pallas_call | solution.py:446
  62.7 1.7 %collective-permute-start.17 = (bf16[32,1664]{1,0:T(8,128)(2,1)S(1)}, bf16[32,1664]{1,0:T(8,128)(2,1)S(1)}, u32[]{:S(2)}, u32[]{:S(2)}) collective-permute-start(bf16[32,1664]{1,0:T(8,128)(2,1)S(1)} %collective-permute-done.13.rest_2_), channel_id=1, source_target_pairs={{0,4},{1,5},{4,8},{5,9},{8,12},{9,13},{12,14},{13,15},{14,10},{15,... | collective-permute-start | bytes 319496 | tf_op jit(solution)/shard_map/ppermute | solution.py:503
  64.8 1.3 %down_blocks.6.rest_0_ = f32[64,1024]{1,0:T(8,128)S(1)} custom-call(f32[64,1024]{1,0:T(8,128)S(1)} %down_blocks.5.rest_0_, bf16[32,1664]{1,0:T(8,128)(2,1)S(1)} %collective-permute-done.15.rest_7_.rest_1_, bf16[32,1664]{1,0:T(8,128)(2,1)S(1)} %collective-permute-done.13.rest_2_, bf16[32,1664]{1,0:T(8,128)(2,1)S(1)} %collective-permute-done.16.rest_8_.rest_3_, ...), custom_call_target="tpu_custom_call" | custom-call | flops 436207616 | bytes 6815744 | tf_op jit(solution)/shard_map/down_blocks/pallas_call | solution.py:446
  66.1 1.4 %collective-permute-done.17.rest_2_ = bf16[32,1664]{1,0:T(8,128)(2,1)S(1)} collective-permute-done((bf16[32,1664]{1,0:T(8,128)(2,1)S(1)}, bf16[32,1664]{1,0:T(8,128)(2,1)S(1)}, u32[]{:S(2)}, u32[]{:S(2)}) %collective-permute-start.17) | collective-permute-done | bytes 106528 | tf_op jit(solution)/shard_map/ppermute | solution.py:503
  67.5 1.7 %collective-permute-done.18.rest_4_ = bf16[32,1664]{1,0:T(8,128)(2,1)S(1)} collective-permute-done((bf16[32,1664]{1,0:T(8,128)(2,1)S(1)}, bf16[32,1664]{1,0:T(8,128)(2,1)S(1)}, u32[]{:S(2)}, u32[]{:S(2)}) %collective-permute-start.18) | collective-permute-done | bytes 106528 | tf_op jit(solution)/shard_map/ppermute | solution.py:503
  69.5 1.7 %collective-permute-start.22 = (bf16[32,1664]{1,0:T(8,128)(2,1)S(1)}, bf16[32,1664]{1,0:T(8,128)(2,1)S(1)}, u32[]{:S(2)}, u32[]{:S(2)}) collective-permute-start(bf16[32,1664]{1,0:T(8,128)(2,1)S(1)} %collective-permute-done.19.rest_7_.rest_1_), channel_id=1, source_target_pairs={{0,4},{1,5},{4,8},{5,9},{8,12},{9,13},{12,14},{13,15},{14,10},{15,... | collective-permute-start | bytes 319496 | tf_op jit(solution)/shard_map/ppermute | solution.py:503
  71.2 1.3 %down_blocks.7.total_ref = f32[64,1024]{1,0:T(8,128)S(1)} custom-call(f32[64,1024]{1,0:T(8,128)S(1)} %down_blocks.6.rest_0_, bf16[32,1664]{1,0:T(8,128)(2,1)S(1)} %collective-permute-done.19.rest_7_.rest_1_, bf16[32,1664]{1,0:T(8,128)(2,1)S(1)} %collective-permute-done.17.rest_2_, bf16[32,1664]{1,0:T(8,128)(2,1)S(1)} %collective-permute-done.20.rest_8_.rest_3_, ...), custom_call_target="tpu_custom_call" | custom-call | flops 436207616 | bytes 6815744 | tf_op jit(solution)/shard_map/down_blocks/pallas_call | solution.py:446
  72.5 1.3 %collective-permute-done.21.lower_ref = bf16[32,1664]{1,0:T(8,128)(2,1)S(1)} collective-permute-done((bf16[32,1664]{1,0:T(8,128)(2,1)S(1)}, bf16[32,1664]{1,0:T(8,128)(2,1)S(1)}, u32[]{:S(2)}, u32[]{:S(2)}) %collective-permute-start.21) | collective-permute-done | bytes 106528 | tf_op jit(solution)/shard_map/ppermute | solution.py:503
  75.0 1.2 %collective-permute-done.23 = bf16[64,512]{1,0:T(8,128)(2,1)S(1)} collective-permute-done((bf16[64,512]{1,0:T(8,128)(2,1)S(1)}, bf16[64,512]{1,0:T(8,128)(2,1)S(1)}, u32[]{:S(2)}, u32[]{:S(2)}) %collective-permute-start.23) | collective-permute-done | bytes 65568 | tf_op jit(solution)/shard_map/ppermute | solution.py:22
  (56 shorter events, 16.2 us)
Async XLA Ops:
  3.4 1.5 %collective-permute-start = (bf16[64,640]{1,0:T(8,128)(2,1)S(1)}, bf16[64,640]{1,0:T(8,128)(2,1)S(1)}, u32[]{:S(2)}, u32[]{:S(2)}) collective-permute-start(bf16[64,640]{1,0:T(8,128)(2,1)S(1)} %get-tuple-element.45.own_ref), channel_id=1, source_target_pairs={{0,1},{1,0},{2,3},{3,2},{4,5},{5,4},{6,7},{7,6},{8,9},{9,8},{10,11... | collective-permute-start | bytes 245768 | tf_op jit(solution)/shard_map/ppermute | solution.py:22
  8.0 7.6 %collective-permute-start.2 = (bf16[64,1664]{1,0:T(8,128)(2,1)S(1)}, bf16[64,1664]{1,0:T(8,128)(2,1)S(1)}, u32[]{:S(2)}, u32[]{:S(2)}) collective-permute-start(bf16[64,1664]{1,0:T(8,128)(2,1)S(1)} %get-tuple-element.49.rest_1_), channel_id=1, source_target_pairs={{0,2},{1,3},{4,0},{5,1},{8,4},{9,5},{12,8},{13,9},{14,12},{15,13},... | collective-permute-start | bytes 638984 | tf_op jit(solution)/shard_map/ppermute | solution.py:503
  10.9 6.7 %collective-permute-start.1 = (bf16[64,1792]{1,0:T(8,128)(2,1)S(1)}, bf16[64,1792]{1,0:T(8,128)(2,1)S(1)}, u32[]{:S(2)}, u32[]{:S(2)}) collective-permute-start(bf16[64,1792]{1,0:T(8,128)(2,1)S(1)} %get-tuple-element.48.rest_0_), channel_id=1, source_target_pairs={{0,4},{1,5},{4,8},{5,9},{8,12},{9,13},{12,14},{13,15},{14,10},{15,... | collective-permute-start | bytes 688136 | tf_op jit(solution)/shard_map/ppermute | solution.py:503
  15.7 11.3 %collective-permute-start.4 = (bf16[64,3456]{1,0:T(8,128)(2,1)S(1)}, bf16[64,3456]{1,0:T(8,128)(2,1)S(1)}, u32[]{:S(2)}, u32[]{:S(2)}) collective-permute-start(bf16[64,3456]{1,0:T(8,128)(2,1)S(1)} %pad_maximum_fusion.1.rest_1_), channel_id=1, source_target_pairs={{0,2},{1,3},{4,0},{5,1},{8,4},{9,5},{12,8},{13,9},{14,12},{15,13},... | collective-permute-start | bytes 1327112 | tf_op jit(solution)/shard_map/ppermute | solution.py:503
  17.7 10.9 %collective-permute-start.3 = (bf16[64,3456]{1,0:T(8,128)(2,1)S(1)}, bf16[64,3456]{1,0:T(8,128)(2,1)S(1)}, u32[]{:S(2)}, u32[]{:S(2)}) collective-permute-start(bf16[64,3456]{1,0:T(8,128)(2,1)S(1)} %pad_maximum_fusion.rest_0_), channel_id=1, source_target_pairs={{0,4},{1,5},{4,8},{5,9},{8,12},{9,13},{12,14},{13,15},{14,10},{15,... | collective-permute-start | bytes 1327112 | tf_op jit(solution)/shard_map/ppermute | solution.py:503
  27.1 10.3 %collective-permute-start.6 = (bf16[64,3456]{1,0:T(8,128)(2,1)S(1)}, bf16[64,3456]{1,0:T(8,128)(2,1)S(1)}, u32[]{:S(2)}, u32[]{:S(2)}) collective-permute-start(bf16[64,3456]{1,0:T(8,128)(2,1)S(1)} %add_convert_fusion.2.rest_1_), channel_id=1, source_target_pairs={{0,2},{1,3},{4,0},{5,1},{8,4},{9,5},{12,8},{13,9},{14,12},{15,13},... | collective-permute-start | bytes 1327112 | tf_op jit(solution)/shard_map/ppermute | solution.py:503
  28.7 10.3 %collective-permute-start.5 = (bf16[64,3456]{1,0:T(8,128)(2,1)S(1)}, bf16[64,3456]{1,0:T(8,128)(2,1)S(1)}, u32[]{:S(2)}, u32[]{:S(2)}) collective-permute-start(bf16[64,3456]{1,0:T(8,128)(2,1)S(1)} %add_convert_fusion.3.rest_0_), channel_id=1, source_target_pairs={{0,4},{1,5},{4,8},{5,9},{8,12},{9,13},{12,14},{13,15},{14,10},{15,... | collective-permute-start | bytes 1327112 | tf_op jit(solution)/shard_map/ppermute | solution.py:503
  37.4 9.3 %collective-permute-start.8 = (bf16[64,3456]{1,0:T(8,128)(2,1)S(1)}, bf16[64,3456]{1,0:T(8,128)(2,1)S(1)}, u32[]{:S(2)}, u32[]{:S(2)}) collective-permute-start(bf16[64,3456]{1,0:T(8,128)(2,1)S(1)} %add_convert_fusion.rest_1_), channel_id=1, source_target_pairs={{0,2},{1,3},{4,0},{5,1},{8,4},{9,5},{12,8},{13,9},{14,12},{15,13},... | collective-permute-start | bytes 1327112 | tf_op jit(solution)/shard_map/ppermute | solution.py:503
  39.0 8.8 %collective-permute-start.7 = (bf16[64,3456]{1,0:T(8,128)(2,1)S(1)}, bf16[64,3456]{1,0:T(8,128)(2,1)S(1)}, u32[]{:S(2)}, u32[]{:S(2)}) collective-permute-start(bf16[64,3456]{1,0:T(8,128)(2,1)S(1)} %add_convert_fusion.1.rest_0_), channel_id=1, source_target_pairs={{0,4},{1,5},{4,8},{5,9},{8,12},{9,13},{12,14},{13,15},{14,10},{15,... | collective-permute-start | bytes 1327112 | tf_op jit(solution)/shard_map/ppermute | solution.py:503
  48.2 5.8 %collective-permute-start.11 = (bf16[32,1664]{1,0:T(8,128)(2,1)S(1)}, bf16[32,1664]{1,0:T(8,128)(2,1)S(1)}, u32[]{:S(2)}, u32[]{:S(2)}) collective-permute-start(bf16[32,1664]{1,0:T(8,128)(2,1)S(1)} %get-tuple-element.61.rest_0_), channel_id=1, source_target_pairs={{0,4},{1,5},{4,8},{5,9},{8,12},{9,13},{12,14},{13,15},{14,10},{15,... | collective-permute-start | bytes 319496 | tf_op jit(solution)/shard_map/ppermute | solution.py:503
  49.1 5.7 %collective-permute-start.12 = (bf16[32,1664]{1,0:T(8,128)(2,1)S(1)}, bf16[32,1664]{1,0:T(8,128)(2,1)S(1)}, u32[]{:S(2)}, u32[]{:S(2)}) collective-permute-start(bf16[32,1664]{1,0:T(8,128)(2,1)S(1)} %get-tuple-element.61.rest_0_), channel_id=1, source_target_pairs={{0,2},{1,3},{4,0},{5,1},{8,4},{9,5},{12,8},{13,9},{14,12},{15,13},... | collective-permute-start | bytes 319496 | tf_op jit(solution)/shard_map/ppermute | solution.py:503
  50.3 6.5 %collective-permute-start.10 = (bf16[32,1664]{1,0:T(8,128)(2,1)S(1)}, bf16[32,1664]{1,0:T(8,128)(2,1)S(1)}, u32[]{:S(2)}, u32[]{:S(2)}) collective-permute-start(bf16[32,1664]{1,0:T(8,128)(2,1)S(1)} %get-tuple-element.60.rest_1_), channel_id=1, source_target_pairs={{0,2},{1,3},{4,0},{5,1},{8,4},{9,5},{12,8},{13,9},{14,12},{15,13},... | collective-permute-start | bytes 319496 | tf_op jit(solution)/shard_map/ppermute | solution.py:503
  51.9 4.9 %collective-permute-start.9 = (bf16[32,1664]{1,0:T(8,128)(2,1)S(1)}, bf16[32,1664]{1,0:T(8,128)(2,1)S(1)}, u32[]{:S(2)}, u32[]{:S(2)}) collective-permute-start(bf16[32,1664]{1,0:T(8,128)(2,1)S(1)} %get-tuple-element.60.rest_1_), channel_id=1, source_target_pairs={{0,4},{1,5},{4,8},{5,9},{8,12},{9,13},{12,14},{13,15},{14,10},{15,... | collective-permute-start | bytes 319496 | tf_op jit(solution)/shard_map/ppermute | solution.py:503
  54.0 4.9 %collective-permute-start.15 = (bf16[32,1664]{1,0:T(8,128)(2,1)S(1)}, bf16[32,1664]{1,0:T(8,128)(2,1)S(1)}, u32[]{:S(2)}, u32[]{:S(2)}) collective-permute-start(bf16[32,1664]{1,0:T(8,128)(2,1)S(1)} %collective-permute-done.11.rest_3_.rest_1_), channel_id=1, source_target_pairs={{0,4},{1,5},{4,8},{5,9},{8,12},{9,13},{12,14},{13,15},{14,10},{15,... | collective-permute-start | bytes 319496 | tf_op jit(solution)/shard_map/ppermute | solution.py:503
  54.7 5.0 %collective-permute-start.16 = (bf16[32,1664]{1,0:T(8,128)(2,1)S(1)}, bf16[32,1664]{1,0:T(8,128)(2,1)S(1)}, u32[]{:S(2)}, u32[]{:S(2)}) collective-permute-start(bf16[32,1664]{1,0:T(8,128)(2,1)S(1)} %collective-permute-done.12.rest_4_.rest_3_), channel_id=1, source_target_pairs={{0,2},{1,3},{4,0},{5,1},{8,4},{9,5},{12,8},{13,9},{14,12},{15,13},... | collective-permute-start | bytes 319496 | tf_op jit(solution)/shard_map/ppermute | solution.py:503
  56.8 5.5 %collective-permute-start.13 = (bf16[32,1664]{1,0:T(8,128)(2,1)S(1)}, bf16[32,1664]{1,0:T(8,128)(2,1)S(1)}, u32[]{:S(2)}, u32[]{:S(2)}) collective-permute-start(bf16[32,1664]{1,0:T(8,128)(2,1)S(1)} %collective-permute-done.9.rest_2_), channel_id=1, source_target_pairs={{0,4},{1,5},{4,8},{5,9},{8,12},{9,13},{12,14},{13,15},{14,10},{15,... | collective-permute-start | bytes 319496 | tf_op jit(solution)/shard_map/ppermute | solution.py:503
  57.7 5.1 %collective-permute-start.14 = (bf16[32,1664]{1,0:T(8,128)(2,1)S(1)}, bf16[32,1664]{1,0:T(8,128)(2,1)S(1)}, u32[]{:S(2)}, u32[]{:S(2)}) collective-permute-start(bf16[32,1664]{1,0:T(8,128)(2,1)S(1)} %collective-permute-done.10.rest_4_), channel_id=1, source_target_pairs={{0,2},{1,3},{4,0},{5,1},{8,4},{9,5},{12,8},{13,9},{14,12},{15,13},... | collective-permute-start | bytes 319496 | tf_op jit(solution)/shard_map/ppermute | solution.py:503
  59.0 5.8 %collective-permute-start.19 = (bf16[32,1664]{1,0:T(8,128)(2,1)S(1)}, bf16[32,1664]{1,0:T(8,128)(2,1)S(1)}, u32[]{:S(2)}, u32[]{:S(2)}) collective-permute-start(bf16[32,1664]{1,0:T(8,128)(2,1)S(1)} %collective-permute-done.15.rest_7_.rest_1_), channel_id=1, source_target_pairs={{0,4},{1,5},{4,8},{5,9},{8,12},{9,13},{12,14},{13,15},{14,10},{15,... | collective-permute-start | bytes 319496 | tf_op jit(solution)/shard_map/ppermute | solution.py:503
  59.7 5.1 %collective-permute-start.20 = (bf16[32,1664]{1,0:T(8,128)(2,1)S(1)}, bf16[32,1664]{1,0:T(8,128)(2,1)S(1)}, u32[]{:S(2)}, u32[]{:S(2)}) collective-permute-start(bf16[32,1664]{1,0:T(8,128)(2,1)S(1)} %collective-permute-done.16.rest_8_.rest_3_), channel_id=1, source_target_pairs={{0,2},{1,3},{4,0},{5,1},{8,4},{9,5},{12,8},{13,9},{14,12},{15,13},... | collective-permute-start | bytes 319496 | tf_op jit(solution)/shard_map/ppermute | solution.py:503
  62.7 4.8 %collective-permute-start.17 = (bf16[32,1664]{1,0:T(8,128)(2,1)S(1)}, bf16[32,1664]{1,0:T(8,128)(2,1)S(1)}, u32[]{:S(2)}, u32[]{:S(2)}) collective-permute-start(bf16[32,1664]{1,0:T(8,128)(2,1)S(1)} %collective-permute-done.13.rest_2_), channel_id=1, source_target_pairs={{0,4},{1,5},{4,8},{5,9},{8,12},{9,13},{12,14},{13,15},{14,10},{15,... | collective-permute-start | bytes 319496 | tf_op jit(solution)/shard_map/ppermute | solution.py:503
  64.5 4.7 %collective-permute-start.18 = (bf16[32,1664]{1,0:T(8,128)(2,1)S(1)}, bf16[32,1664]{1,0:T(8,128)(2,1)S(1)}, u32[]{:S(2)}, u32[]{:S(2)}) collective-permute-start(bf16[32,1664]{1,0:T(8,128)(2,1)S(1)} %collective-permute-done.14.rest_4_), channel_id=1, source_target_pairs={{0,2},{1,3},{4,0},{5,1},{8,4},{9,5},{12,8},{13,9},{14,12},{15,13},... | collective-permute-start | bytes 319496 | tf_op jit(solution)/shard_map/ppermute | solution.py:503
  69.2 4.7 %collective-permute-start.21 = (bf16[32,1664]{1,0:T(8,128)(2,1)S(1)}, bf16[32,1664]{1,0:T(8,128)(2,1)S(1)}, u32[]{:S(2)}, u32[]{:S(2)}) collective-permute-start(bf16[32,1664]{1,0:T(8,128)(2,1)S(1)} %collective-permute-done.18.rest_4_), channel_id=1, source_target_pairs={{0,2},{1,3},{4,0},{5,1},{8,4},{9,5},{12,8},{13,9},{14,12},{15,13},... | collective-permute-start | bytes 319496 | tf_op jit(solution)/shard_map/ppermute | solution.py:503
  69.5 4.7 %collective-permute-start.22 = (bf16[32,1664]{1,0:T(8,128)(2,1)S(1)}, bf16[32,1664]{1,0:T(8,128)(2,1)S(1)}, u32[]{:S(2)}, u32[]{:S(2)}) collective-permute-start(bf16[32,1664]{1,0:T(8,128)(2,1)S(1)} %collective-permute-done.19.rest_7_.rest_1_), channel_id=1, source_target_pairs={{0,4},{1,5},{4,8},{5,9},{8,12},{9,13},{12,14},{13,15},{14,10},{15,... | collective-permute-start | bytes 319496 | tf_op jit(solution)/shard_map/ppermute | solution.py:503
  74.9 1.3 %collective-permute-start.23 = (bf16[64,512]{1,0:T(8,128)(2,1)S(1)}, bf16[64,512]{1,0:T(8,128)(2,1)S(1)}, u32[]{:S(2)}, u32[]{:S(2)}) collective-permute-start(bf16[64,512]{1,0:T(8,128)(2,1)S(1)} %get-tuple-element.82), channel_id=1, source_target_pairs={{0,1},{1,0},{2,3},{3,2},{4,5},{5,4},{6,7},{7,6},{8,9},{9,8},{10,11... | collective-permute-start | bytes 196616 | tf_op jit(solution)/shard_map/ppermute | solution.py:22
  (4 other events, 12.5 us)

commit v7 on v6

--- a/solution.py
+++ b/solution.py
@@ -538,12 +538,12 @@
         if distance < 3:
             upper_left = shift(upper_left, -1)
             lower_right = shift(lower_right, 1)
-            after = [upper_right, upper_left]
+            after = [upper_right, lower_left]
         else:
             after = []
         total, *fetched = down_blocks(total, hidden, tiles, down_tile, fetch, after)
         down_tiles += fetched
-        lower_right, lower_left, total = lax.optimization_barrier((lower_right, lower_left, total))
+        upper_left, lower_right, total = lax.optimization_barrier((upper_left, lower_right, total))
         hidden = [(upper_right, lower_right), (upper_left, lower_left)]
     (far_tile,) = down_tiles
     kept, sent = last_down_block(total, upper_right, lower_left, far_tile)

time: 77 us -> 74.2 us (0.964)
  waiting for transfers between devices: 13.1 us -> 10.5 us
    ppermute x22, waiting for transfers between devices: 11 us -> 8.34 us  [shift(): return lax.ppermute(value, 'tp', pairs)]
  transfers between devices with their start and end apart: 24 -> 24, of which waited for: 13 -> 11; matrix products, arithmetic and copies ran while one was open for 1% -> 1% of each run, Pallas kernels for 39% -> 41%
where the time goes in v7:
time: 74.2 us; the launch traced here: 74.1 us
  Pallas kernels  37.8 us (51%)
  starting transfers between devices  24.4 us (33%)
  waiting for transfers between devices  10.5 us (14%)
  other arithmetic  1.1 us (1%)
    ppermute x22, starting transfers between devices, shift(): return lax.ppermute(value, 'tp', pairs)  23.7 us
    pallas_call x3, Pallas kernels, up_blocks(): pl.pallas_call(kernel, out_shape=[jax.ShapeDtypeStruct((rows, LANES + 2 *...  18.5 us
    ppermute x22, waiting for transfers between devices, shift(): return lax.ppermute(value, 'tp', pairs)  8.34 us
    pallas_call x1, Pallas kernels, own_block(): pl.pallas_call(kernel, out_shape=[jax.ShapeDtypeStruct((2, depth, width),...  6.98 us
    pallas_call x4, Pallas kernels, down_blocks(): pl.pallas_call(kernel, out_shape=[jax.ShapeDtypeStruct((rows, width), F32...  4.68 us
    pallas_call x1, Pallas kernels, first_up_block(): pl.pallas_call(kernel, out_shape=[jax.ShapeDtypeStruct((rows, LANES + wid...  3.13 us
    pallas_call x1, Pallas kernels, fetch_up_block(): pl.pallas_call(kernel, out_shape=jax.ShapeDtypeStruct((2, depth, width),...  3.08 us
    ppermute x2, waiting for transfers between devices, from_partner(): return lax.ppermute(value, axis, pairs)  2.16 us
  transfers between devices with their start and end apart: 24, of which 11 were waited for; matrix products, arithmetic and copies ran while one was open for 1% of the time, Pallas kernels for 41%

profile of v7, /device:TPU:0, one launch (start us, length us, event | category | flops | bytes accessed | tf_op | source)
XLA Modules:
  0.0 74.1 jit_solution(13047454801418591074)
XLA Ops:
  0.0 3.1 %fetch_up_block.1.after_ref.tiles_ref = bf16[2,1024,1664]{2,1,0:T(8,128)(2,1)S(1)} custom-call(bf16[1024,13312]{1,0:T(8,128)(2,1)} %bitcast.7, bf16[1024,13312]{1,0:T(8,128)(2,1)} %bitcast.13), custom_call_target="tpu_custom_call" | custom-call | tf_op jit(solution)/shard_map/fetch_up_block/pallas_call | solution.py:112
  4.9 3.1 %first_up_block.1 = (bf16[64,1792]{1,0:T(8,128)(2,1)S(1)}, bf16[64,1664]{1,0:T(8,128)(2,1)S(1)}, bf16[64,1024]{1,0:T(8,128)(2,1)S(1)}, f32[64,128]{1,0:T(8,128)S(1)}, bf16[1024,1664]{1,0:T(8,128)(2,1)S(1)}) custom-call(bf16[64,640]{1,0:T(8,128)(2,1)S(1)} %get-tuple-element.44.own_ref, bf16[64,640]{1,0:T(8,128)(2,1)S(1)} %collective-permute-done.other_ref, ...), custom_call_target="tpu_custom_call" | custom-call | flops 436207616 | bytes 6815744 | tf_op jit(solution)/shard_map/first_up_block/pallas_call | solution.py:245
  8.0 2.9 %collective-permute-start.2 = (bf16[64,1664]{1,0:T(8,128)(2,1)S(1)}, bf16[64,1664]{1,0:T(8,128)(2,1)S(1)}, u32[]{:S(2)}, u32[]{:S(2)}) collective-permute-start(bf16[64,1664]{1,0:T(8,128)(2,1)S(1)} %get-tuple-element.48.rest_1_), channel_id=1, source_target_pairs={{0,2},{1,3},{4,0},{5,1},{8,4},{9,5},{12,8},{13,9},{14,12},{15,13},... | collective-permute-start | bytes 638984 | tf_op jit(solution)/shard_map/ppermute | solution.py:503
  11.1 4.5 %up_blocks.3 = (f32[64,3456]{1,0:T(8,128)S(1)}, f32[64,3456]{1,0:T(8,128)S(1)}) custom-call(bf16[64,1024]{1,0:T(8,128)(2,1)S(1)} %get-tuple-element.45.x_ref, f32[64,128]{1,0:T(8,128)S(1)} %get-tuple-element.46.squares_ref, bf16[1024,13312]{1,0:T(8,128)(2,1)} %bitcast.9, bf16[1024,13312]{1,0:T(8,128)(2,1)} %bitcast.14, ...), custom_call_target="tpu_custom_call" | custom-call | flops 872415232 | bytes 13631488 | tf_op jit(solution)/shard_map/up_blocks/pallas_call | solution.py:302
  15.7 1.9 %collective-permute-start.4 = (bf16[64,3456]{1,0:T(8,128)(2,1)S(1)}, bf16[64,3456]{1,0:T(8,128)(2,1)S(1)}, u32[]{:S(2)}, u32[]{:S(2)}) collective-permute-start(bf16[64,3456]{1,0:T(8,128)(2,1)S(1)} %pad_maximum_fusion.1.rest_1_), channel_id=1, source_target_pairs={{0,2},{1,3},{4,0},{5,1},{8,4},{9,5},{12,8},{13,9},{14,12},{15,13},... | collective-permute-start | bytes 1327112 | tf_op jit(solution)/shard_map/ppermute | solution.py:503
  18.1 7.0 %up_blocks.4 = (f32[64,3456]{1,0:T(8,128)S(1)}, f32[64,3456]{1,0:T(8,128)S(1)}, bf16[1664,1024]{1,0:T(8,128)(2,1)S(1)}, bf16[1664,1024]{1,0:T(8,128)(2,1)S(1)}) custom-call(bf16[64,1024]{1,0:T(8,128)(2,1)S(1)} %get-tuple-element.45.x_ref, f32[64,128]{1,0:T(8,128)S(1)} %get-tuple-element.46.squares_ref, bf16[1024,13312]{1,0:T(8,128)(2,1)} %bitcast.10, ...), custom_call_target="tpu_custom_call" | custom-call | flops 872415232 | bytes 13631488 | tf_op jit(solution)/shard_map/up_blocks/pallas_call | solution.py:302
  25.1 1.8 %collective-permute-done.4 = bf16[64,3456]{1,0:T(8,128)(2,1)S(1)} collective-permute-done((bf16[64,3456]{1,0:T(8,128)(2,1)S(1)}, bf16[64,3456]{1,0:T(8,128)(2,1)S(1)}, u32[]{:S(2)}, u32[]{:S(2)}) %collective-permute-start.4) | collective-permute-done | bytes 442400 | tf_op jit(solution)/shard_map/ppermute | solution.py:503
  27.1 1.5 %collective-permute-start.6 = (bf16[64,3456]{1,0:T(8,128)(2,1)S(1)}, bf16[64,3456]{1,0:T(8,128)(2,1)S(1)}, u32[]{:S(2)}, u32[]{:S(2)}) collective-permute-start(bf16[64,3456]{1,0:T(8,128)(2,1)S(1)} %add_convert_fusion.2.rest_1_), channel_id=1, source_target_pairs={{0,2},{1,3},{4,0},{5,1},{8,4},{9,5},{12,8},{13,9},{14,12},{15,13},... | collective-permute-start | bytes 1327112 | tf_op jit(solution)/shard_map/ppermute | solution.py:503
  29.3 7.0 %up_blocks.5 = (f32[64,3456]{1,0:T(8,128)S(1)}, f32[64,3456]{1,0:T(8,128)S(1)}, bf16[1664,1024]{1,0:T(8,128)(2,1)S(1)}, bf16[1664,1024]{1,0:T(8,128)(2,1)S(1)}) custom-call(bf16[64,1024]{1,0:T(8,128)(2,1)S(1)} %get-tuple-element.45.x_ref, f32[64,128]{1,0:T(8,128)S(1)} %get-tuple-element.46.squares_ref, bf16[1024,13312]{1,0:T(8,128)(2,1)} %bitcast.11, ...), custom_call_target="tpu_custom_call" | custom-call | flops 872415232 | bytes 13631488 | tf_op jit(solution)/shard_map/up_blocks/pallas_call | solution.py:302
  37.4 1.5 %collective-permute-start.8 = (bf16[64,3456]{1,0:T(8,128)(2,1)S(1)}, bf16[64,3456]{1,0:T(8,128)(2,1)S(1)}, u32[]{:S(2)}, u32[]{:S(2)}) collective-permute-start(bf16[64,3456]{1,0:T(8,128)(2,1)S(1)} %add_convert_fusion.rest_1_), channel_id=1, source_target_pairs={{0,2},{1,3},{4,0},{5,1},{8,4},{9,5},{12,8},{13,9},{14,12},{15,13},... | collective-permute-start | bytes 1327112 | tf_op jit(solution)/shard_map/ppermute | solution.py:503
  39.6 7.0 %own_block.1 = (bf16[2,1024,1664]{2,1,0:T(8,128)(2,1)S(1)}, f32[64,1664]{1,0:T(8,128)S(1)}, f32[64,1664]{1,0:T(8,128)S(1)}, bf16[1664,1024]{1,0:T(8,128)(2,1)S(1...) custom-call(bf16[64,1024]{1,0:T(8,128)(2,1)S(1)} %get-tuple-element.45.x_ref, ...), custom_call_target="tpu_custom_call" | custom-call | flops 436207616 | bytes 6815744 | tf_op jit(solution)/shard_map/own_block/pallas_call | solution.py:342
  46.7 1.1 %collective-permute-done.7.right_ref = bf16[64,3456]{1,0:T(8,128)(2,1)S(1)} collective-permute-done((bf16[64,3456]{1,0:T(8,128)(2,1)S(1)}, bf16[64,3456]{1,0:T(8,128)(2,1)S(1)}, u32[]{:S(2)}, u32[]{:S(2)}) %collective-permute-start.7) | collective-permute-done | bytes 442400 | tf_op jit(solution)/shard_map/ppermute | solution.py:503
  49.1 1.2 %collective-permute-start.12 = (bf16[32,1664]{1,0:T(8,128)(2,1)S(1)}, bf16[32,1664]{1,0:T(8,128)(2,1)S(1)}, u32[]{:S(2)}, u32[]{:S(2)}) collective-permute-start(bf16[32,1664]{1,0:T(8,128)(2,1)S(1)} %get-tuple-element.60.rest_1_), channel_id=1, source_target_pairs={{0,2},{1,3},{4,0},{5,1},{8,4},{9,5},{12,8},{13,9},{14,12},{15,13},... | collective-permute-start | bytes 319496 | tf_op jit(solution)/shard_map/ppermute | solution.py:503
  51.1 1.2 %collective-permute-start.9 = (bf16[32,1664]{1,0:T(8,128)(2,1)S(1)}, bf16[32,1664]{1,0:T(8,128)(2,1)S(1)}, u32[]{:S(2)}, u32[]{:S(2)}) collective-permute-start(bf16[32,1664]{1,0:T(8,128)(2,1)S(1)} %get-tuple-element.59.rest_0_), channel_id=1, source_target_pairs={{0,2},{1,3},{4,0},{5,1},{8,4},{9,5},{12,8},{13,9},{14,12},{15,13},... | collective-permute-start | bytes 319496 | tf_op jit(solution)/shard_map/ppermute | solution.py:503
  52.3 1.4 %collective-permute-done.11.rest_3_.rest_1_ = bf16[32,1664]{1,0:T(8,128)(2,1)S(1)} collective-permute-done((bf16[32,1664]{1,0:T(8,128)(2,1)S(1)}, bf16[32,1664]{1,0:T(8,128)(2,1)S(1)}, u32[]{:S(2)}, u32[]{:S(2)}) %collective-permute-start.11) | collective-permute-done | bytes 106528 | tf_op jit(solution)/shard_map/ppermute | solution.py:503
  56.7 1.4 %collective-permute-start.13 = (bf16[32,1664]{1,0:T(8,128)(2,1)S(1)}, bf16[32,1664]{1,0:T(8,128)(2,1)S(1)}, u32[]{:S(2)}, u32[]{:S(2)}) collective-permute-start(bf16[32,1664]{1,0:T(8,128)(2,1)S(1)} %collective-permute-done.9.rest_3_), channel_id=1, source_target_pairs={{0,2},{1,3},{4,0},{5,1},{8,4},{9,5},{12,8},{13,9},{14,12},{15,13},... | collective-permute-start | bytes 319496 | tf_op jit(solution)/shard_map/ppermute | solution.py:503
  58.8 1.3 %collective-permute-start.19 = (bf16[32,1664]{1,0:T(8,128)(2,1)S(1)}, bf16[32,1664]{1,0:T(8,128)(2,1)S(1)}, u32[]{:S(2)}, u32[]{:S(2)}) collective-permute-start(bf16[32,1664]{1,0:T(8,128)(2,1)S(1)} %collective-permute-done.15.rest_7_.rest_1_), channel_id=1, source_target_pairs={{0,4},{1,5},{4,8},{5,9},{8,12},{9,13},{12,14},{13,15},{14,10},{15,... | collective-permute-start | bytes 319496 | tf_op jit(solution)/shard_map/ppermute | solution.py:503
  60.8 1.3 %down_blocks.5.rest_0_ = f32[64,1024]{1,0:T(8,128)S(1)} custom-call(f32[64,1024]{1,0:T(8,128)S(1)} %down_blocks.4.rest_0_, bf16[32,1664]{1,0:T(8,128)(2,1)S(1)} %collective-permute-done.11.rest_3_.rest_1_, bf16[32,1664]{1,0:T(8,128)(2,1)S(1)} %collective-permute-done.10.rest_2_, bf16[32,1664]{1,0:T(8,128)(2,1)S(1)} %collective-permute-done.9.rest_3_, ...), custom_call_target="tpu_custom_call" | custom-call | flops 436207616 | bytes 6815744 | tf_op jit(solution)/shard_map/down_blocks/pallas_call | solution.py:446
  62.1 1.5 %collective-permute-done.14.rest_2_ = bf16[32,1664]{1,0:T(8,128)(2,1)S(1)} collective-permute-done((bf16[32,1664]{1,0:T(8,128)(2,1)S(1)}, bf16[32,1664]{1,0:T(8,128)(2,1)S(1)}, u32[]{:S(2)}, u32[]{:S(2)}) %collective-permute-start.14) | collective-permute-done | bytes 106528 | tf_op jit(solution)/shard_map/ppermute | solution.py:503
  63.6 1.7 %collective-permute-start.17 = (bf16[32,1664]{1,0:T(8,128)(2,1)S(1)}, bf16[32,1664]{1,0:T(8,128)(2,1)S(1)}, u32[]{:S(2)}, u32[]{:S(2)}) collective-permute-start(bf16[32,1664]{1,0:T(8,128)(2,1)S(1)} %collective-permute-done.13.rest_3_), channel_id=1, source_target_pairs={{0,2},{1,3},{4,0},{5,1},{8,4},{9,5},{12,8},{13,9},{14,12},{15,13},... | collective-permute-start | bytes 319496 | tf_op jit(solution)/shard_map/ppermute | solution.py:503
  66.3 1.4 %collective-permute-start.22 = (bf16[32,1664]{1,0:T(8,128)(2,1)S(1)}, bf16[32,1664]{1,0:T(8,128)(2,1)S(1)}, u32[]{:S(2)}, u32[]{:S(2)}) collective-permute-start(bf16[32,1664]{1,0:T(8,128)(2,1)S(1)} %collective-permute-done.20.rest_8_.rest_4_), channel_id=1, source_target_pairs={{0,2},{1,3},{4,0},{5,1},{8,4},{9,5},{12,8},{13,9},{14,12},{15,13},... | collective-permute-start | bytes 319496 | tf_op jit(solution)/shard_map/ppermute | solution.py:503
  67.7 1.3 %down_blocks.6.rest_0_ = f32[64,1024]{1,0:T(8,128)S(1)} custom-call(f32[64,1024]{1,0:T(8,128)S(1)} %down_blocks.5.rest_0_, bf16[32,1664]{1,0:T(8,128)(2,1)S(1)} %collective-permute-done.15.rest_7_.rest_1_, bf16[32,1664]{1,0:T(8,128)(2,1)S(1)} %collective-permute-done.14.rest_2_, bf16[32,1664]{1,0:T(8,128)(2,1)S(1)} %collective-permute-done.13.rest_3_, ...), custom_call_target="tpu_custom_call" | custom-call | flops 436207616 | bytes 6815744 | tf_op jit(solution)/shard_map/down_blocks/pallas_call | solution.py:446
  70.1 1.3 %down_blocks.7.total_ref = f32[64,1024]{1,0:T(8,128)S(1)} custom-call(f32[64,1024]{1,0:T(8,128)S(1)} %down_blocks.6.rest_0_, bf16[32,1664]{1,0:T(8,128)(2,1)S(1)} %collective-permute-done.19.rest_7_.rest_1_, bf16[32,1664]{1,0:T(8,128)(2,1)S(1)} %collective-permute-done.18.rest_2_, bf16[32,1664]{1,0:T(8,128)(2,1)S(1)} %collective-permute-done.17.rest_3_, ...), custom_call_target="tpu_custom_call" | custom-call | flops 436207616 | bytes 6815744 | tf_op jit(solution)/shard_map/down_blocks/pallas_call | solution.py:446
  72.2 1.2 %collective-permute-done.23 = bf16[64,512]{1,0:T(8,128)(2,1)S(1)} collective-permute-done((bf16[64,512]{1,0:T(8,128)(2,1)S(1)}, bf16[64,512]{1,0:T(8,128)(2,1)S(1)}, u32[]{:S(2)}, u32[]{:S(2)}) %collective-permute-start.23) | collective-permute-done | bytes 65568 | tf_op jit(solution)/shard_map/ppermute | solution.py:22
  (56 shorter events, 15.0 us)
Async XLA Ops:
  3.4 1.5 %collective-permute-start = (bf16[64,640]{1,0:T(8,128)(2,1)S(1)}, bf16[64,640]{1,0:T(8,128)(2,1)S(1)}, u32[]{:S(2)}, u32[]{:S(2)}) collective-permute-start(bf16[64,640]{1,0:T(8,128)(2,1)S(1)} %get-tuple-element.44.own_ref), channel_id=1, source_target_pairs={{0,1},{1,0},{2,3},{3,2},{4,5},{5,4},{6,7},{7,6},{8,9},{9,8},{10,11... | collective-permute-start | bytes 245768 | tf_op jit(solution)/shard_map/ppermute | solution.py:22
  8.0 7.6 %collective-permute-start.2 = (bf16[64,1664]{1,0:T(8,128)(2,1)S(1)}, bf16[64,1664]{1,0:T(8,128)(2,1)S(1)}, u32[]{:S(2)}, u32[]{:S(2)}) collective-permute-start(bf16[64,1664]{1,0:T(8,128)(2,1)S(1)} %get-tuple-element.48.rest_1_), channel_id=1, source_target_pairs={{0,2},{1,3},{4,0},{5,1},{8,4},{9,5},{12,8},{13,9},{14,12},{15,13},... | collective-permute-start | bytes 638984 | tf_op jit(solution)/shard_map/ppermute | solution.py:503
  10.9 6.7 %collective-permute-start.1 = (bf16[64,1792]{1,0:T(8,128)(2,1)S(1)}, bf16[64,1792]{1,0:T(8,128)(2,1)S(1)}, u32[]{:S(2)}, u32[]{:S(2)}) collective-permute-start(bf16[64,1792]{1,0:T(8,128)(2,1)S(1)} %get-tuple-element.47.rest_0_), channel_id=1, source_target_pairs={{0,4},{1,5},{4,8},{5,9},{8,12},{9,13},{12,14},{13,15},{14,10},{15,... | collective-permute-start | bytes 688136 | tf_op jit(solution)/shard_map/ppermute | solution.py:503
  15.7 11.3 %collective-permute-start.4 = (bf16[64,3456]{1,0:T(8,128)(2,1)S(1)}, bf16[64,3456]{1,0:T(8,128)(2,1)S(1)}, u32[]{:S(2)}, u32[]{:S(2)}) collective-permute-start(bf16[64,3456]{1,0:T(8,128)(2,1)S(1)} %pad_maximum_fusion.1.rest_1_), channel_id=1, source_target_pairs={{0,2},{1,3},{4,0},{5,1},{8,4},{9,5},{12,8},{13,9},{14,12},{15,13},... | collective-permute-start | bytes 1327112 | tf_op jit(solution)/shard_map/ppermute | solution.py:503
  17.7 10.9 %collective-permute-start.3 = (bf16[64,3456]{1,0:T(8,128)(2,1)S(1)}, bf16[64,3456]{1,0:T(8,128)(2,1)S(1)}, u32[]{:S(2)}, u32[]{:S(2)}) collective-permute-start(bf16[64,3456]{1,0:T(8,128)(2,1)S(1)} %pad_maximum_fusion.rest_0_), channel_id=1, source_target_pairs={{0,4},{1,5},{4,8},{5,9},{8,12},{9,13},{12,14},{13,15},{14,10},{15,... | collective-permute-start | bytes 1327112 | tf_op jit(solution)/shard_map/ppermute | solution.py:503
  27.1 10.3 %collective-permute-start.6 = (bf16[64,3456]{1,0:T(8,128)(2,1)S(1)}, bf16[64,3456]{1,0:T(8,128)(2,1)S(1)}, u32[]{:S(2)}, u32[]{:S(2)}) collective-permute-start(bf16[64,3456]{1,0:T(8,128)(2,1)S(1)} %add_convert_fusion.2.rest_1_), channel_id=1, source_target_pairs={{0,2},{1,3},{4,0},{5,1},{8,4},{9,5},{12,8},{13,9},{14,12},{15,13},... | collective-permute-start | bytes 1327112 | tf_op jit(solution)/shard_map/ppermute | solution.py:503
  28.7 10.3 %collective-permute-start.5 = (bf16[64,3456]{1,0:T(8,128)(2,1)S(1)}, bf16[64,3456]{1,0:T(8,128)(2,1)S(1)}, u32[]{:S(2)}, u32[]{:S(2)}) collective-permute-start(bf16[64,3456]{1,0:T(8,128)(2,1)S(1)} %add_convert_fusion.3.rest_0_), channel_id=1, source_target_pairs={{0,4},{1,5},{4,8},{5,9},{8,12},{9,13},{12,14},{13,15},{14,10},{15,... | collective-permute-start | bytes 1327112 | tf_op jit(solution)/shard_map/ppermute | solution.py:503
  37.4 9.3 %collective-permute-start.8 = (bf16[64,3456]{1,0:T(8,128)(2,1)S(1)}, bf16[64,3456]{1,0:T(8,128)(2,1)S(1)}, u32[]{:S(2)}, u32[]{:S(2)}) collective-permute-start(bf16[64,3456]{1,0:T(8,128)(2,1)S(1)} %add_convert_fusion.rest_1_), channel_id=1, source_target_pairs={{0,2},{1,3},{4,0},{5,1},{8,4},{9,5},{12,8},{13,9},{14,12},{15,13},... | collective-permute-start | bytes 1327112 | tf_op jit(solution)/shard_map/ppermute | solution.py:503
  39.0 8.8 %collective-permute-start.7 = (bf16[64,3456]{1,0:T(8,128)(2,1)S(1)}, bf16[64,3456]{1,0:T(8,128)(2,1)S(1)}, u32[]{:S(2)}, u32[]{:S(2)}) collective-permute-start(bf16[64,3456]{1,0:T(8,128)(2,1)S(1)} %add_convert_fusion.1.rest_0_), channel_id=1, source_target_pairs={{0,4},{1,5},{4,8},{5,9},{8,12},{9,13},{12,14},{13,15},{14,10},{15,... | collective-permute-start | bytes 1327112 | tf_op jit(solution)/shard_map/ppermute | solution.py:503
  48.2 5.5 %collective-permute-start.11 = (bf16[32,1664]{1,0:T(8,128)(2,1)S(1)}, bf16[32,1664]{1,0:T(8,128)(2,1)S(1)}, u32[]{:S(2)}, u32[]{:S(2)}) collective-permute-start(bf16[32,1664]{1,0:T(8,128)(2,1)S(1)} %get-tuple-element.59.rest_0_), channel_id=1, source_target_pairs={{0,4},{1,5},{4,8},{5,9},{8,12},{9,13},{12,14},{13,15},{14,10},{15,... | collective-permute-start | bytes 319496 | tf_op jit(solution)/shard_map/ppermute | solution.py:503
  49.1 5.8 %collective-permute-start.12 = (bf16[32,1664]{1,0:T(8,128)(2,1)S(1)}, bf16[32,1664]{1,0:T(8,128)(2,1)S(1)}, u32[]{:S(2)}, u32[]{:S(2)}) collective-permute-start(bf16[32,1664]{1,0:T(8,128)(2,1)S(1)} %get-tuple-element.60.rest_1_), channel_id=1, source_target_pairs={{0,2},{1,3},{4,0},{5,1},{8,4},{9,5},{12,8},{13,9},{14,12},{15,13},... | collective-permute-start | bytes 319496 | tf_op jit(solution)/shard_map/ppermute | solution.py:503
  50.3 6.2 %collective-permute-start.10 = (bf16[32,1664]{1,0:T(8,128)(2,1)S(1)}, bf16[32,1664]{1,0:T(8,128)(2,1)S(1)}, u32[]{:S(2)}, u32[]{:S(2)}) collective-permute-start(bf16[32,1664]{1,0:T(8,128)(2,1)S(1)} %get-tuple-element.60.rest_1_), channel_id=1, source_target_pairs={{0,4},{1,5},{4,8},{5,9},{8,12},{9,13},{12,14},{13,15},{14,10},{15,... | collective-permute-start | bytes 319496 | tf_op jit(solution)/shard_map/ppermute | solution.py:503
  51.1 5.7 %collective-permute-start.9 = (bf16[32,1664]{1,0:T(8,128)(2,1)S(1)}, bf16[32,1664]{1,0:T(8,128)(2,1)S(1)}, u32[]{:S(2)}, u32[]{:S(2)}) collective-permute-start(bf16[32,1664]{1,0:T(8,128)(2,1)S(1)} %get-tuple-element.59.rest_0_), channel_id=1, source_target_pairs={{0,2},{1,3},{4,0},{5,1},{8,4},{9,5},{12,8},{13,9},{14,12},{15,13},... | collective-permute-start | bytes 319496 | tf_op jit(solution)/shard_map/ppermute | solution.py:503
  53.7 5.1 %collective-permute-start.15 = (bf16[32,1664]{1,0:T(8,128)(2,1)S(1)}, bf16[32,1664]{1,0:T(8,128)(2,1)S(1)}, u32[]{:S(2)}, u32[]{:S(2)}) collective-permute-start(bf16[32,1664]{1,0:T(8,128)(2,1)S(1)} %collective-permute-done.11.rest_3_.rest_1_), channel_id=1, source_target_pairs={{0,4},{1,5},{4,8},{5,9},{8,12},{9,13},{12,14},{13,15},{14,10},{15,... | collective-permute-start | bytes 319496 | tf_op jit(solution)/shard_map/ppermute | solution.py:503
  54.8 5.3 %collective-permute-start.16 = (bf16[32,1664]{1,0:T(8,128)(2,1)S(1)}, bf16[32,1664]{1,0:T(8,128)(2,1)S(1)}, u32[]{:S(2)}, u32[]{:S(2)}) collective-permute-start(bf16[32,1664]{1,0:T(8,128)(2,1)S(1)} %collective-permute-done.12.rest_4_), channel_id=1, source_target_pairs={{0,2},{1,3},{4,0},{5,1},{8,4},{9,5},{12,8},{13,9},{14,12},{15,13},... | collective-permute-start | bytes 319496 | tf_op jit(solution)/shard_map/ppermute | solution.py:503
  56.7 5.4 %collective-permute-start.13 = (bf16[32,1664]{1,0:T(8,128)(2,1)S(1)}, bf16[32,1664]{1,0:T(8,128)(2,1)S(1)}, u32[]{:S(2)}, u32[]{:S(2)}) collective-permute-start(bf16[32,1664]{1,0:T(8,128)(2,1)S(1)} %collective-permute-done.9.rest_3_), channel_id=1, source_target_pairs={{0,2},{1,3},{4,0},{5,1},{8,4},{9,5},{12,8},{13,9},{14,12},{15,13},... | collective-permute-start | bytes 319496 | tf_op jit(solution)/shard_map/ppermute | solution.py:503
  58.1 5.5 %collective-permute-start.14 = (bf16[32,1664]{1,0:T(8,128)(2,1)S(1)}, bf16[32,1664]{1,0:T(8,128)(2,1)S(1)}, u32[]{:S(2)}, u32[]{:S(2)}) collective-permute-start(bf16[32,1664]{1,0:T(8,128)(2,1)S(1)} %collective-permute-done.10.rest_2_), channel_id=1, source_target_pairs={{0,4},{1,5},{4,8},{5,9},{8,12},{9,13},{12,14},{13,15},{14,10},{15,... | collective-permute-start | bytes 319496 | tf_op jit(solution)/shard_map/ppermute | solution.py:503
  58.8 6.9 %collective-permute-start.19 = (bf16[32,1664]{1,0:T(8,128)(2,1)S(1)}, bf16[32,1664]{1,0:T(8,128)(2,1)S(1)}, u32[]{:S(2)}, u32[]{:S(2)}) collective-permute-start(bf16[32,1664]{1,0:T(8,128)(2,1)S(1)} %collective-permute-done.15.rest_7_.rest_1_), channel_id=1, source_target_pairs={{0,4},{1,5},{4,8},{5,9},{8,12},{9,13},{12,14},{13,15},{14,10},{15,... | collective-permute-start | bytes 319496 | tf_op jit(solution)/shard_map/ppermute | solution.py:503
  60.1 6.2 %collective-permute-start.20 = (bf16[32,1664]{1,0:T(8,128)(2,1)S(1)}, bf16[32,1664]{1,0:T(8,128)(2,1)S(1)}, u32[]{:S(2)}, u32[]{:S(2)}) collective-permute-start(bf16[32,1664]{1,0:T(8,128)(2,1)S(1)} %collective-permute-done.16.rest_8_.rest_4_), channel_id=1, source_target_pairs={{0,2},{1,3},{4,0},{5,1},{8,4},{9,5},{12,8},{13,9},{14,12},{15,13},... | collective-permute-start | bytes 319496 | tf_op jit(solution)/shard_map/ppermute | solution.py:503
  63.6 5.4 %collective-permute-start.17 = (bf16[32,1664]{1,0:T(8,128)(2,1)S(1)}, bf16[32,1664]{1,0:T(8,128)(2,1)S(1)}, u32[]{:S(2)}, u32[]{:S(2)}) collective-permute-start(bf16[32,1664]{1,0:T(8,128)(2,1)S(1)} %collective-permute-done.13.rest_3_), channel_id=1, source_target_pairs={{0,2},{1,3},{4,0},{5,1},{8,4},{9,5},{12,8},{13,9},{14,12},{15,13},... | collective-permute-start | bytes 319496 | tf_op jit(solution)/shard_map/ppermute | solution.py:503
  65.3 4.7 %collective-permute-start.18 = (bf16[32,1664]{1,0:T(8,128)(2,1)S(1)}, bf16[32,1664]{1,0:T(8,128)(2,1)S(1)}, u32[]{:S(2)}, u32[]{:S(2)}) collective-permute-start(bf16[32,1664]{1,0:T(8,128)(2,1)S(1)} %collective-permute-done.14.rest_2_), channel_id=1, source_target_pairs={{0,4},{1,5},{4,8},{5,9},{8,12},{9,13},{12,14},{13,15},{14,10},{15,... | collective-permute-start | bytes 319496 | tf_op jit(solution)/shard_map/ppermute | solution.py:503
  65.7 5.7 %collective-permute-start.21 = (bf16[32,1664]{1,0:T(8,128)(2,1)S(1)}, bf16[32,1664]{1,0:T(8,128)(2,1)S(1)}, u32[]{:S(2)}, u32[]{:S(2)}) collective-permute-start(bf16[32,1664]{1,0:T(8,128)(2,1)S(1)} %collective-permute-done.19.rest_7_.rest_1_), channel_id=1, source_target_pairs={{0,4},{1,5},{4,8},{5,9},{8,12},{9,13},{12,14},{13,15},{14,10},{15,... | collective-permute-start | bytes 319496 | tf_op jit(solution)/shard_map/ppermute | solution.py:503
  66.3 5.1 %collective-permute-start.22 = (bf16[32,1664]{1,0:T(8,128)(2,1)S(1)}, bf16[32,1664]{1,0:T(8,128)(2,1)S(1)}, u32[]{:S(2)}, u32[]{:S(2)}) collective-permute-start(bf16[32,1664]{1,0:T(8,128)(2,1)S(1)} %collective-permute-done.20.rest_8_.rest_4_), channel_id=1, source_target_pairs={{0,2},{1,3},{4,0},{5,1},{8,4},{9,5},{12,8},{13,9},{14,12},{15,13},... | collective-permute-start | bytes 319496 | tf_op jit(solution)/shard_map/ppermute | solution.py:503
  72.1 1.3 %collective-permute-start.23 = (bf16[64,512]{1,0:T(8,128)(2,1)S(1)}, bf16[64,512]{1,0:T(8,128)(2,1)S(1)}, u32[]{:S(2)}, u32[]{:S(2)}) collective-permute-start(bf16[64,512]{1,0:T(8,128)(2,1)S(1)} %get-tuple-element.80), channel_id=1, source_target_pairs={{0,1},{1,0},{2,3},{3,2},{4,5},{5,4},{6,7},{7,6},{8,9},{9,8},{10,11... | collective-permute-start | bytes 196616 | tf_op jit(solution)/shard_map/ppermute | solution.py:22
  (4 other events, 12.5 us)
